TPU v7x, 32 devices: a whole 2x2x4 slice. The times are simulated.
32 devices in a mesh: dp: 8 (over y, x, core), segment: 4 (over z).
Axes of the slice: x: 2, y: 2, z: 4, core: 2. Of those that a mesh axis runs over, the one named last changes fastest.
Arguments:
- inputs: bfloat16 [4, 8, 256, 1024], P('segment', 'dp'), may hold values from -6 to 6
- values: bfloat16 [4, 8, 256, 1024], P('segment', 'dp'), may hold values from -6 to 6
- gate_values: bfloat16 [4, 8, 256, 1024], P('segment', 'dp'), may hold values from -6 to 6
- out_grad: bfloat16 [4, 8, 256, 1024], P('segment', 'dp'), may hold values from -6 to 6
- lengths: int32 [4, 8], P('segment', 'dp'), may hold values from 32 to 256, as said below
- qk_weight: bfloat16 [4, 1024, 2048], P('segment', 'dp'), may hold values from -0.1875 to 0.1875
Outputs:
- grad_inputs: bfloat16 [4, 8, 256, 1024], P('segment', 'dp')
- grad_values: bfloat16 [4, 8, 256, 1024], P('segment', 'dp')
- grad_gates: bfloat16 [4, 8, 256, 1024], P('segment', 'dp')
- grad_weight: float32 [4, 1024, 2048], P('segment', 'dp')
Inputs may be any that keep to these rules, and one draw needn't show every extreme that they name: `lengths`: in every layer some sequence has the full length 256.
All inputs are finite; a program needn't handle non-finite values.
Results may differ from a plain program's by a relative error of at most 0.025.
Values may be sent and summed in bfloat16 or wider, within the bound.
No kernel may reach another device: no remote copies, remote signals or barrier semaphores. Data moves between devices by JAX's collectives and lax.ppermute only.
A program may use at most 64 MiB of HBM per device.

v0:
```python
import jax
import jax.numpy as jnp
from jax import lax
from jax.sharding import PartitionSpec as P

H = 8
DH = 128


def from_behind(x, axis, by):
    count = lax.axis_size(axis)
    return lax.ppermute(x, axis, [(i, (i + by) % count) for i in range(count)])


def window(qk_pre, values, gate_values, length):
    seq_len = qk_pre.shape[0]
    qk_act = jax.nn.silu(qk_pre).astype(jnp.bfloat16)
    queries = qk_act[:, : H * DH].reshape(seq_len, H, DH)
    keys = qk_act[:, H * DH :].reshape(seq_len, H, DH)
    scores = jnp.einsum("ihd,jhd->hij", queries, keys, preferred_element_type=jnp.float32) * DH ** (
        -0.5
    )
    row_ids = lax.broadcasted_iota(jnp.int32, (seq_len, seq_len), 0)
    col_ids = lax.broadcasted_iota(jnp.int32, (seq_len, seq_len), 1)
    valid = (col_ids <= row_ids) & (row_ids < length)
    attention = jnp.where(valid[None], jax.nn.silu(scores), 0.0).astype(jnp.bfloat16)
    heads_values = values.reshape(seq_len, H, DH)
    mixed_heads = jnp.einsum(
        "hij,jhd->ihd", attention, heads_values, preferred_element_type=jnp.float32
    ).reshape(seq_len, H * DH)
    row_mean = jnp.mean(mixed_heads, axis=-1, keepdims=True)
    centered = mixed_heads - row_mean
    variance = jnp.mean(centered * centered, axis=-1, keepdims=True)
    normed = centered * lax.rsqrt(variance + 1e-05)
    live = (lax.broadcasted_iota(jnp.int32, (seq_len, 1), 0) < length).astype(jnp.float32)
    return normed * gate_values.astype(jnp.float32) * live


def on_device(inputs, values, gate_values, out_grad, lengths, qk_weight):
    tokens_in = inputs[0, 0]
    seq_values = values[0, 0]
    seq_gates = gate_values[0, 0]
    length = lengths[0, 0]
    shard_weight = qk_weight[0]
    full_weight = lax.all_gather(shard_weight, "dp", axis=0, tiled=True)
    pre = jnp.dot(tokens_in, full_weight, preferred_element_type=jnp.float32)
    incoming = from_behind(out_grad[0, 0], "segment", -1)
    outcome, pullback = jax.vjp(lambda a, b, c: window(a, b, c, length), pre, seq_values, seq_gates)
    grad_pre, grad_val, grad_gate = pullback(incoming.astype(jnp.float32))
    grad_pre_b = grad_pre.astype(jnp.bfloat16)
    grad_in = lax.dot_general(
        grad_pre_b, full_weight, (((1,), (1,)), ((), ())), preferred_element_type=jnp.float32
    ).astype(jnp.bfloat16)
    term = lax.dot_general(
        tokens_in, grad_pre_b, (((0,), (0,)), ((), ())), preferred_element_type=jnp.float32
    )
    grad_shard = lax.psum_scatter(
        term.astype(jnp.bfloat16), "dp", scatter_dimension=0, tiled=True
    ).astype(jnp.float32)
    return (grad_in[None, None], grad_val[None, None], grad_gate[None, None], grad_shard[None])


def solution(mesh):
    return jax.shard_map(
        on_device,
        mesh=mesh,
        in_specs=(
            P("segment", "dp", None, None),
            P("segment", "dp", None, None),
            P("segment", "dp", None, None),
            P("segment", "dp", None, None),
            P("segment", "dp"),
            P("segment", "dp", None),
        ),
        out_specs=(
            P("segment", "dp", None, None),
            P("segment", "dp", None, None),
            P("segment", "dp", None, None),
            P("segment", "dp", None),
        ),
        check_vma=False,
    )
```

profile of v0, /device:TPU:0, one launch (start us, length us, event | category | flops | bytes accessed | tf_op | source)
XLA Modules:
  0.0 141.3 jit_solution(18202141778787650643)
XLA Ops:
  7.2 0.0 copy-start
  7.2 0.0 all-gather.3.cloned.1.call-start
  7.2 0.7 all-gather.3.cloned.1.call-update
  7.9 0.0 reduce-scatter.4.cloned.1.call-start
  8.0 5.1 %collective-permute-start = (bf16[256,1024]{1,0:T(8,128)(2,1)}, bf16[256,1024]{1,0:T(8,128)(2,1)}, u32[]{:S(2)}, u32[]{:S(2)}) collective-permute-start(bf16[256,1024]{1,0:T(8,128)(2,1)} %bitcast.86), channel_id=1, source_target_pairs={{0,3},{1,0},{2,1},{3,2},{4,7},{5,4},{6,5},{7,6},{8,11},{9,8},{10,9... | collective-permute-start | bytes 1572872 | tf_op jit(solution)/shard_map/ppermute | solution.py:12
  13.7 1.1 copy.44
  14.9 0.0 copy-start.4
  14.9 0.1 fusion.24
  15.0 34.4 %all-gather.3.cloned.1.call-done = bf16[1,1024,2048]{2,1,0:T(8,128)(2,1)} async-done(((bf16[1,128,2048]{2,1,0:T(8,128)(2,1)}), bf16[1,1024,2048]{2,1,0:T(8,128)(2,1)}) %all-gather.3.cloned.1.call-update) | async-done | bytes 4194320 | tf_op jit(solution)/shard_map/all_gather | solution.py:45
  49.4 4.8 %multiply_convert_fusion = (bf16[256,2048]{1,0:T(8,128)(2,1)S(1)}, f32[256,2048]{1,0:T(8,128)}) fusion(bf16[1,1024,2048]{2,1,0:T(8,128)(2,1)} %all-gather.3.cloned.1.call-done, bf16[1,1,256,1024]{3,2,1,0:T(8,128)(2,1)S(1)} %copy-done), kind=kOutput, calls=%fused_computation.17 | convolution fusion | flops 1076363264 | bytes 7864320 | tf_op jit(solution)/shard_map/dot_general | solution.py:46
  54.2 0.1 fusion.30
  54.2 0.2 copy.42
  54.5 0.2 copy.43
  54.7 0.0 copy-start.8
  54.7 2.1 %select_convert_fusion = (bf16[8,256,256]{2,1,0:T(8,128)(2,1)S(1)}, f32[8,256,256]{2,1,0:T(8,128)}) fusion(pred[256,256]{1,0:T(8,128)(4,1)S(1)} %fusion.24, bf16[256,8,128]{0,2,1:T(8,128)(2,1)S(1)} %bitcast.76, bf16[256,8,128]{0,2,1:T(8,128)(2,1)S(1)} %bitcast.78), kind=kOutput, calls=%fused_computation.15 | convolution fusion | flops 137887744 | bytes 4259840 | tf_op jit(solution)/shard_map/jvp(ihd,jhd->hij)/dot_general | solution.py:20
  56.8 0.0 copy-done.6
  56.8 0.5 fusion.31
  57.3 0.0 copy-start.3
  57.3 0.4 copy-done.1
  57.8 0.3 copy.26
  58.1 0.2 fusion.17
  58.3 0.0 collective-permute-done
  58.3 0.1 copy-done.3
  58.4 1.5 %multiply_reduce_fusion = f32[256]{0:T(256)S(1)} fusion(bf16[256,1024]{1,0:T(8,128)(2,1)} %collective-permute-done, f32[256,1024]{1,0:T(8,128)S(1)} %copy.26, bf16[1,1,256,1024]{3,2,1,0:T(8,128)(2,1)S(1)} %copy-done.3, f32[256]{0:T(256)S(1)} %broadcast_multiply_fusion, f32[256]{0:T(256)S(1)} %fusion.26), kind=kLoop, calls=%fused_computation.31 | loop fusion | flops 1834752 | bytes 2100224 | tf_op jit(solution)/shard_map/transpose(jvp())/reduce_sum | solution.py:34
  59.9 2.4 %fusion.29 = (f32[256]{0:T(256)S(1)}, f32[256,1024]{1,0:T(8,128)S(1)}, bf16[1,1,256,1024]{3,2,1,0:T(8,128)(2,1)}) fusion(f32[256]{0:T(256)S(1)} %get-tuple-element.18, f32[256,1024]{1,0:T(8,128)S(1)} %copy.26, f32[256]{0:T(256)S(1)} %broadcast_multiply_fusion, f32[256]{0:T(256)S(1)} %get-tuple-element.17, bf16[1,1,256,1024]{3,2,1,0:T(8,128)(2,1)S(1)} %copy-done.3, ...), kind=kLoop, calls=%fused_computation.50 | loop fusion | flops 3407616 | bytes 3675136 | tf_op jit(solution)/shard_map/transpose(jvp())/reduce_sum | solution.py:32
  62.3 0.1 broadcast_add_fusion
  62.4 0.2 copy.37
  62.6 0.7 copy-done.5
  63.3 2.9 %fusion.9 = bf16[8,256,256]{2,1,0:T(8,128)(2,1)S(1)} fusion(f32[8,256,256]{2,1,0:T(8,128)} %get-tuple-element.22, bf16[8,128,256]{2,1,0:T(8,128)(2,1)S(1)} %bitcast.80, pred[256,256]{1,0:T(8,128)(4,1)S(1)} %fusion.24, bf16[256,8,128]{2,1,0:T(8,128)(2,1)S(1)} %bitcast.75), kind=kOutput, calls=%fused_computation.14 | convolution fusion | flops 141557760 | bytes 4259840 | tf_op jit(solution)/shard_map/transpose(jvp(hij,jhd->ihd))/dot_general | solution.py:28
  66.2 0.0 copy-done.9
  66.2 0.0 copy-start.7
  66.2 0.5 fusion.32
  66.7 0.5 copy-done.7
  67.3 0.3 fusion.33
  67.6 0.2 copy.39
  67.8 0.2 copy.38
  68.0 0.0 copy-start.10
  68.0 5.7 %convert_bitcast_fusion = bf16[1024,2048]{0,1:T(8,128)(2,1)} fusion(bf16[1,1,256,1024]{3,2,1,0:T(8,128)(2,1)S(1)} %copy-done, f32[256,2048]{1,0:T(8,128)} %get-tuple-element.20, bf16[256,1024]{1,0:T(8,128)(2,1)S(1)} %copy.39, bf16[256,1024]{1,0:T(8,128)(2,1)S(1)} %copy.38), kind=kOutput, calls=%fused_computation.4 | convolution fusion | flops 1083179008 | bytes 7864320 | tf_op jit(solution)/shard_map/dot_general | solution.py:54
  73.7 6.5 %copy.40 = bf16[1024,2048]{1,0:T(8,128)(2,1)} copy(bf16[1024,2048]{0,1:T(8,128)(2,1)} %convert_bitcast_fusion) | data formatting | bytes 8388608
  80.3 0.0 reduce-scatter.4.cloned.1.call-update
  80.3 1.2 copy-done.2
  81.5 0.3 fusion.34
  81.8 1.0 copy.34
  82.8 5.4 %fusion.13 = bf16[1,1,256,1024]{3,2,1,0:T(8,128)(2,1)} fusion(bf16[1,1024,2048]{2,1,0:T(8,128)(2,1)} %all-gather.3.cloned.1.call-done, f32[256,2048]{1,0:T(8,128)} %get-tuple-element.20, bf16[256,1024]{1,0:T(8,128)(2,1)S(1)} %copy.39, bf16[256,1024]{1,0:T(8,128)(2,1)} %copy-done.10), kind=kOutput, calls=%fused_computation.25 | convolution fusion | flops 1081344000 | bytes 7864320 | tf_op jit(solution)/shard_map/dot_general | solution.py:51
  88.2 43.5 %reduce-scatter.4.cloned.1.call-done = bf16[128,2048]{1,0:T(8,128)(2,1)} async-done(((bf16[1024,2048]{1,0:T(8,128)(2,1)}), bf16[128,2048]{1,0:T(8,128)(2,1)}) %reduce-scatter.4.cloned.1.call-update) | async-done | bytes 524304
  131.8 1.3 copy.41
  133.1 0.1 bitcast_convert_fusion
  133.2 1.3 copy.35
  (14 shorter events, 0.0 us)
Async XLA Ops:
  7.2 42.2 %copy-start = (bf16[1,1,256,1024]{3,2,1,0:T(8,128)(2,1)S(1)}, bf16[1,1,256,1024]{3,2,1,0:T(8,128)(2,1)}, u32[]{:S(2)}) copy-start(bf16[1,1,256,1024]{3,2,1,0:T(8,128)(2,1)} %param.6) | copy-start | bytes 1572868
  7.2 42.2 %all-gather.3.cloned.1.call-start = ((), (), s32[]{:S(2)}) async-start(), calls=%async_computation.1 | async-start | bytes 4718592 | tf_op jit(solution)/shard_map/all_gather | solution.py:45
  7.9 123.9 %reduce-scatter.4.cloned.1.call-start = ((), (), s32[]{:S(2)}) async-start(), calls=%async_computation.2 | async-start | bytes 4718592
  8.0 50.3 %collective-permute-start = (bf16[256,1024]{1,0:T(8,128)(2,1)}, bf16[256,1024]{1,0:T(8,128)(2,1)}, u32[]{:S(2)}, u32[]{:S(2)}) collective-permute-start(bf16[256,1024]{1,0:T(8,128)(2,1)} %bitcast.86), channel_id=1, source_target_pairs={{0,3},{1,0},{2,1},{3,2},{4,7},{5,4},{6,5},{7,6},{8,11},{9,8},{10,9... | collective-permute-start | bytes 1572872 | tf_op jit(solution)/shard_map/ppermute | solution.py:12
  14.9 42.0 %copy-start.4 = (bf16[32,8,8,128]{3,2,1,0:T(8,128)(2,1)}, bf16[32,8,8,128]{3,2,1,0:T(8,128)(2,1)S(1)}, u32[]{:S(2)}) copy-start(bf16[32,8,8,128]{3,2,1,0:T(8,128)(2,1)S(1)} %copy.44) | copy-start | bytes 1572868
  54.5 2.4 %copy-start.6 = (bf16[256,1024]{0,1:T(8,128)(2,1)}, bf16[256,1024]{0,1:T(8,128)(2,1)S(1)}, u32[]{:S(2)}) copy-start(bf16[256,1024]{0,1:T(8,128)(2,1)S(1)} %copy.42) | copy-start | bytes 1572868
  54.7 2.1 %copy-start.8 = (bf16[256,1024]{0,1:T(8,128)(2,1)}, bf16[256,1024]{0,1:T(8,128)(2,1)S(1)}, u32[]{:S(2)}) copy-start(bf16[256,1024]{0,1:T(8,128)(2,1)S(1)} %copy.43) | copy-start | bytes 1572868
  56.8 1.0 copy-start.1
  57.3 1.0 copy-start.3
  62.2 1.0 copy-start.5
  63.3 2.9 %copy-start.9 = (bf16[256,1024]{0,1:T(8,128)(2,1)S(1)}, bf16[256,1024]{0,1:T(8,128)(2,1)}, u32[]{:S(2)}) copy-start(bf16[256,1024]{0,1:T(8,128)(2,1)} %copy-done.8) | copy-start | bytes 1572868
  66.2 1.0 copy-start.7
  68.0 5.7 %copy-start.10 = (bf16[256,1024]{1,0:T(8,128)(2,1)}, bf16[256,1024]{1,0:T(8,128)(2,1)S(1)}, u32[]{:S(2)}) copy-start(bf16[256,1024]{1,0:T(8,128)(2,1)S(1)} %copy.38) | copy-start | bytes 1572868
  80.3 1.2 copy-start.2
Sparse Core Ops, SparseCore 0:
  9.9 39.4 all-gather.2
  80.4 51.3 reduce-scatter.3
where the time goes:
time: 142 us; the launch traced here: 141 us
  waiting for transfers between devices  78.6 us (55%)
  matrix products  22.6 us (16%)
  local copies, waits for them, and re-layouts  15.7 us (11%)
  between operations  14.9 us (10%)
  starting transfers between devices  5.18 us (4%)
  other arithmetic  4.35 us (3%)
    unnamed x3, waiting for transfers between devices  44.2 us
    all_gather x1, waiting for transfers between devices, on_device(): full_weight = lax.all_gather(shard_weight, 'dp', axis=0, tiled=True)  34.4 us
    unnamed x27, local copies, waits for them, and re-layouts  14.3 us
    dot_general x1, matrix products, on_device(): lax.dot_general(tokens_in, grad_pre_b, (((0,), (0,)), ((), ())), preferre...  5.72 us
    dot_general x1, matrix products, on_device(): lax.dot_general(grad_pre_b, full_weight, (((1,), (1,)), ((), ())), prefer...  5.44 us
    ppermute x1, starting transfers between devices, from_behind(): return lax.ppermute(x, axis, [(i, (i + by) % count) for i in range(count)])  5.1 us
    dot_general x1, matrix products, on_device(): pre = jnp.dot(tokens_in, full_weight, preferred_element_type=jnp.float32)  4.81 us
    dot_general x3, matrix products, window(): jnp.einsum('hij,jhd->ihd', attention, heads_values, preferred_element_typ...  3.73 us
  transfers between devices with their start and end apart: 3, of which 2 were waited for; matrix products, arithmetic and copies ran while one was open for 12% of the time, Pallas kernels for 0%

commit v1 on v0

v1 whole, which is shorter than its diff:
```python
import functools

import jax
import jax.numpy as jnp
from jax import lax
from jax.experimental import pallas as pl
from jax.experimental.pallas import tpu as pltpu
from jax.sharding import PartitionSpec as P

H = 8
DH = 128
F = H * DH
HALF = F // 2
HL = H // 2
SCALE = DH**-0.5
EPS = 1e-05
BF = jnp.bfloat16
F32 = jnp.float32
GROUPS = ((0, 1), (2, 3))

VMEM = pl.BlockSpec(memory_space=pltpu.VMEM)
SMEM = pl.BlockSpec(memory_space=pltpu.SMEM)


def pair(x, mask):
    count = lax.axis_size("dp")
    return lax.ppermute(x, "dp", [(i, i ^ mask) for i in range(count)])


def from_next(x, mask):
    dp, seg = lax.axis_size("dp"), lax.axis_size("segment")
    return lax.ppermute(
        x,
        ("dp", "segment"),
        [(i * seg + s, (i ^ mask) * seg + (s - 1) % seg) for i in range(dp) for s in range(seg)],
    )


def call(body, out_shape, *args, scratch=()):
    return pl.pallas_call(
        body,
        out_shape=out_shape,
        in_specs=[SMEM] + [VMEM] * (len(args) - 1),
        out_specs=jax.tree.map(lambda _: VMEM, out_shape),
        scratch_shapes=list(scratch),
        compiler_params=pltpu.CompilerParams(vmem_limit_bytes=48 << 20),
    )(*args)


def dot(a, b, ca, cb):
    return lax.dot_general(a, b, (((ca,), (cb,)), ((), ())), preferred_element_type=F32)


def ds(start, size, align):
    return pl.ds(pl.multiple_of(start, align), size)


def block_start(me, masks, rows):
    return lax.div(lax.bitwise_xor(me, masks[0]), len(masks)) * (len(masks) * rows)


def fill_block(me, masks, piece_refs, block):
    rows = piece_refs[0].shape[0]
    for m, ref in zip(masks, piece_refs):
        at = lax.rem(lax.bitwise_xor(me, m), len(masks)) * rows
        block[ds(at, rows, rows), :] = ref[...]


def turn_kernel(sc, xo, xp, xt):
    seq_len = xo.shape[0]
    xt[:, :seq_len] = xo[...].T
    xt[:, seq_len:] = xp[...].T


def pre_part(me, blocks, xo, xp, piece_refs, block, pre, add):
    rows = piece_refs[0].shape[0]
    seq_len = xo.shape[0]
    done = 0
    for masks in blocks:
        fill_block(me, masks, piece_refs[done : done + len(masks)], block)
        done += len(masks)
        cols = ds(block_start(me, masks, rows), len(masks) * rows, len(masks) * rows)
        for s, x in ((0, xo), (1, xp)):
            own = pl.ds(s * seq_len, seq_len)
            part = dot(x[:, cols], block[...], 1, 0)
            pre[own, :] = (pre[own, :] + part) if add else part
        add = True


def pre_kernel(blocks, has_prev, sc, xo, xp, *refs):
    me = sc[0]
    if has_prev:
        prev, refs = refs[0], refs[1:]
    *pieces, pre, block = refs
    if has_prev:
        pre[...] = prev[...]
    pre_part(me, blocks, xo, xp, pieces, block, pre, has_prev)


def forward_kernel(blocks, sc, xo, xp, prev, vo, vp, go, gp, co, cp, *refs):
    *pieces, act, slope, prob, dprob, mixed, stats, pre, block = refs
    me = sc[0]
    core = lax.rem(me, 2)
    seq_len = xo.shape[0]
    pre[...] = prev[...]
    pre_part(me, blocks, xo, xp, pieces, block, pre, True)
    row_ids = lax.broadcasted_iota(jnp.int32, (seq_len, seq_len), 0)
    col_ids = lax.broadcasted_iota(jnp.int32, (seq_len, seq_len), 1)
    for s in range(2):
        length = sc[1 + s]
        own = pl.ds(s * seq_len, seq_len)
        valid = (col_ids <= row_ids) & (row_ids < length)
        for h in range(HL):
            qk = []
            for side in range(2):
                at = pl.ds(side * HALF + h * DH, DH)
                v = pre[own, at]
                sig = 1.0 / (1.0 + jnp.exp(-v))
                a = (v * sig).astype(BF)
                act[own, at] = a
                slope[own, at] = sig * (1.0 + v * (1.0 - sig))
                qk.append(a)
            score = dot(qk[0], qk[1], 1, 1) * SCALE
            sig = 1.0 / (1.0 + jnp.exp(-score))
            p = jnp.where(valid, score * sig, 0.0).astype(BF)
            prob[s * HL + h] = p
            dprob[s * HL + h] = jnp.where(valid, sig * (1.0 + score * (1.0 - sig)) * SCALE, 0.0).astype(BF)
            if s == 0:
                val = vo[:, ds(core * HALF + h * DH, DH, DH)]
            else:
                val = vp[:, pl.ds(h * DH, DH)]
            mixed[own, pl.ds(h * DH, DH)] = dot(p, val, 1, 0)
        live = lax.broadcasted_iota(jnp.int32, (seq_len, 1), 0) < length
        if s == 0:
            gate = go[:, ds(core * HALF, HALF, HALF)]
            cot = co[...]
        else:
            gate = gp[...]
            cot = cp[...]
        grad = jnp.where(live, gate.astype(F32) * cot.astype(F32), 0.0)
        m = mixed[own, :]
        total = jnp.sum(m, axis=1, keepdims=True)
        off = m - total * (1.0 / HALF)
        cols = [
            total,
            jnp.sum(off * off, axis=1, keepdims=True),
            jnp.sum(grad, axis=1, keepdims=True),
            jnp.sum(grad * off, axis=1, keepdims=True),
        ]
        lane = lax.broadcasted_iota(jnp.int32, (seq_len, 128), 1)
        packed = jnp.zeros((seq_len, 128), F32)
        for i, col in enumerate(cols):
            packed = jnp.where(lane == i, col, packed)
        stats[:, own] = packed.T[:8, :]


def backward_kernel(heads, nmask, sc, xt, act, slope, prob, dprob, mixed, mine, theirs, vo, vp, go, gp, co, cp, *refs):
    *terms, gpre, gval, ggate, whole = refs
    me = sc[0]
    core = lax.rem(me, 2)
    seq_len = vo.shape[0]
    width = len(heads) * DH
    for s in range(2):
        length = sc[1 + s]
        own = pl.ds(s * seq_len, seq_len)
        other = pl.ds((1 - s) * seq_len, seq_len)
        mt = mine[:, own].T
        tt = theirs[:, other].T
        mean = (mt[:, 0:1] + tt[:, 0:1]) * (1.0 / F)
        mean_m = mt[:, 0:1] * (1.0 / HALF)
        mean_t = tt[:, 0:1] * (1.0 / HALF)
        gap = mean_m - mean_t
        variance = (mt[:, 1:2] + tt[:, 1:2] + gap * gap * (HALF * 0.5)) * (1.0 / F)
        rstd = lax.rsqrt(variance + EPS)
        c1 = (mt[:, 2:3] + tt[:, 2:3]) * (1.0 / F)
        cross = mt[:, 3:4] + tt[:, 3:4] + (mean_m - mean) * mt[:, 2:3] + (mean_t - mean) * tt[:, 2:3]
        c2 = cross * rstd * (1.0 / F)
        live = lax.broadcasted_iota(jnp.int32, (seq_len, 1), 0) < length
        for i, h in enumerate(heads):
            local = pl.ds(h * DH, DH)
            at = pl.ds(i * DH, DH)
            if s == 0:
                far = ds(core * HALF + h * DH, DH, DH)
                val, gate, cot = vo[:, far], go[:, far], co[:, local]
            else:
                val, gate, cot = vp[:, local], gp[:, local], cp[:, local]
            cot = cot.astype(F32)
            grad = jnp.where(live, gate.astype(F32) * cot, 0.0)
            normed = (mixed[own, local] - mean) * rstd
            ggate[own, at] = jnp.where(live, normed * cot, 0.0).astype(BF)
            dmix = (rstd * (grad - c1 - normed * c2)).astype(BF)
            q, k = act[own, local], act[own, pl.ds(HALF + h * DH, DH)]
            gval[own, at] = dot(prob[s * HL + h], dmix, 0, 0).astype(BF)
            datt = dot(dmix, val, 1, 1)
            dscore = (datt * dprob[s * HL + h].astype(F32)).astype(BF)
            dq = dot(dscore, k, 1, 0)
            dk = dot(dscore, q, 0, 0)
            gpre[own, at] = (dq * slope[own, local]).astype(BF)
            gpre[own, pl.ds(width + i * DH, DH)] = (dk * slope[own, pl.ds(HALF + h * DH, DH)]).astype(BF)
    whole[...] = dot(xt[...], gpre[...], 1, 0).astype(BF)
    rows = terms[0].shape[0]
    for m in range(nmask):
        terms[m][...] = whole[ds(lax.bitwise_xor(me, m) * rows, rows, rows), :]


def input_kernel(blocks, sc, *refs):
    *pieces, g0, g1, own_out, other_out, block = refs
    me = sc[0]
    rows = pieces[0].shape[0]
    seq_len = own_out.shape[0]
    width = g0.shape[1] // 2
    done = 0
    for masks in blocks:
        fill_block(me, masks, pieces[done : done + len(masks)], block)
        done += len(masks)
        cols = ds(block_start(me, masks, rows), len(masks) * rows, len(masks) * rows)
        for s, out in ((0, own_out), (1, other_out)):
            own = pl.ds(s * seq_len, seq_len)
            total = None
            for g, ref in enumerate((g0, g1)):
                for side in range(2):
                    part = dot(
                        ref[own, pl.ds(side * width, width)],
                        block[:, pl.ds(side * HALF + g * width, width)],
                        1,
                        1,
                    )
                    total = part if total is None else total + part
            out[:, cols] = total.astype(out.dtype)


def collect_kernel(sc, gi_o, gi_r, v0, v1, v0r, v1r, g0, g1, g0r, g1r, gi, gv, gg):
    core = lax.rem(sc[0], 2)
    seq_len = gi_o.shape[0]
    gi[...] = (gi_o[...] + gi_r[...].astype(F32)).astype(BF)
    for out, own, far in ((gv, (v0, v1), (v0r, v1r)), (gg, (g0, g1), (g0r, g1r))):
        for g in range(2):
            width = own[g].shape[1]
            out[:, ds(core * HALF + g * width, width, width)] = own[g][pl.ds(0, seq_len), :]
            out[:, ds((1 - core) * HALF + g * width, width, width)] = far[g][...]


def weight_kernel(sc, *refs):
    *parts, out = refs
    core = lax.rem(sc[0], 2)
    for g in range(2):
        own, far = parts[6 * g : 6 * g + 3], parts[6 * g + 3 : 6 * g + 6]
        width = own[0].shape[1] // 2
        for side in range(2):
            at = pl.ds(side * width, width)
            for c, three in ((core, own), (1 - core, far)):
                total = three[0][:, at].astype(F32) + three[1][:, at].astype(F32) + three[2][:, at].astype(F32)
                out[:, ds(side * F + c * HALF + g * width, width, width)] = total


def like(shape, kind):
    return jax.ShapeDtypeStruct(shape, kind)


def on_device(inputs, values, gate_values, out_grad, lengths, qk_weight):
    count = lax.axis_size("dp")
    me = lax.axis_index("dp")
    core = lax.rem(me, 2)
    xo, vo, go, grads = inputs[0, 0], values[0, 0], gate_values[0, 0], out_grad[0, 0]
    shard = qk_weight[0]
    rows, depth = shard.shape[0], xo.shape[1]
    seq_len = xo.shape[0]
    two = 2 * seq_len

    def half(x, c):
        return lax.dynamic_slice_in_dim(x, c * HALF, HALF, 1)

    low = jnp.concatenate([shard[:, :HALF], shard[:, F : F + HALF]], 1)
    high = jnp.concatenate([shard[:, HALF:F], shard[:, F + HALF :]], 1)
    mine = jnp.where(core == 0, low, high)
    other = jnp.where(core == 0, high, low)

    pieces = {0: mine}
    pieces[2] = pair(mine, 2)
    pieces[5] = pair(other, 5)
    pieces[1] = pair(other, 1)
    pieces[3] = pair(other, 3)
    pieces[4] = pair(mine, 4)
    pieces[6] = pair(pieces[2], 4)
    pieces[7] = pair(pieces[5], 2)
    bit = 8
    while bit < count:
        for m in range(bit):
            pieces[m + bit] = pair(pieces[m], bit)
        bit *= 2

    xp = pair(xo, 1)
    vp = pair(half(vo, 1 - core), 1)
    gp = pair(half(go, 1 - core), 1)
    co = from_next(half(grads, core), 0)
    cp = from_next(half(grads, 1 - core), 1)
    sc = jnp.concatenate([me.astype(jnp.int32)[None], lengths[0], pair(lengths[0], 1)])

    per = 256 // rows
    blocks = [tuple(range(b, b + per)) for b in range(0, count, per)]
    block = pltpu.VMEM((per * rows, F), BF)
    pre_shape = like((two, F), F32)

    def held(some):
        return [pieces[m] for masks in some for m in masks]

    xt = call(turn_kernel, like((depth, two), BF), sc, xo, xp)
    pre = call(
        functools.partial(pre_kernel, blocks[:1], False), pre_shape, sc, xo, xp, *held(blocks[:1]), scratch=[block]
    )
    pre = call(
        functools.partial(pre_kernel, blocks[1:-1], True),
        pre_shape,
        sc,
        xo,
        xp,
        pre,
        *held(blocks[1:-1]),
        scratch=[block],
    )
    act, slope, prob, dprob, mixed, stats = call(
        functools.partial(forward_kernel, blocks[-1:]),
        [
            like((two, F), BF),
            like((two, F), F32),
            like((2 * HL, seq_len, seq_len), BF),
            like((2 * HL, seq_len, seq_len), BF),
            like((two, HALF), F32),
            like((8, two), F32),
        ],
        sc,
        xo,
        xp,
        pre,
        vo,
        vp,
        go,
        gp,
        co,
        cp,
        *held(blocks[-1:]),
        scratch=[pltpu.VMEM((two, F), F32), block],
    )
    theirs = pair(stats, 1)

    gpre, gval, ggate, sums = [], [], [], []
    for heads in GROUPS:
        width = 2 * len(heads) * DH
        *terms, gpre_g, gval_g, ggate_g = call(
            functools.partial(backward_kernel, heads, count),
            [like((rows, width), BF)] * count
            + [like((two, width), BF), like((two, width // 2), BF), like((two, width // 2), BF)],
            sc,
            xt,
            act,
            slope,
            prob,
            dprob,
            mixed,
            stats,
            theirs,
            vo,
            vp,
            go,
            gp,
            co,
            cp,
            scratch=[pltpu.VMEM((depth, width), BF)],
        )
        gpre.append(gpre_g)
        gval.append(gval_g)
        ggate.append(ggate_g)
        bit = count // 2
        while bit >= 8:
            for m in range(bit):
                terms[m] = (terms[m].astype(F32) + pair(terms[m + bit], bit).astype(F32)).astype(BF)
            bit //= 2
        t4 = (terms[4].astype(F32) + pair(terms[6], 2).astype(F32)).astype(BF)
        t3 = (terms[3].astype(F32) + pair(terms[7], 4).astype(F32)).astype(BF)
        sums += [terms[0], pair(terms[2], 2), pair(t4, 4)]
        sums += [pair(terms[1], 1), pair(t3, 3), pair(terms[5], 5)]

    gi_o, gi_other = call(
        functools.partial(input_kernel, blocks),
        [like((seq_len, depth), F32), like((seq_len, depth), BF)],
        sc,
        *held(blocks),
        *gpre,
        scratch=[block],
    )
    grad_in, grad_val, grad_gate = call(
        collect_kernel,
        [like((seq_len, F), BF)] * 3,
        sc,
        gi_o,
        pair(gi_other, 1),
        *gval,
        *[pair(x[seq_len:], 1) for x in gval],
        *ggate,
        *[pair(x[seq_len:], 1) for x in ggate],
    )
    grad_shard = call(weight_kernel, like((rows, 2 * F), F32), sc, *sums)
    return (grad_in[None, None], grad_val[None, None], grad_gate[None, None], grad_shard[None])


def solution(mesh):
    return jax.shard_map(
        on_device,
        mesh=mesh,
        in_specs=(
            P("segment", "dp", None, None),
            P("segment", "dp", None, None),
            P("segment", "dp", None, None),
            P("segment", "dp", None, None),
            P("segment", "dp"),
            P("segment", "dp", None),
        ),
        out_specs=(
            P("segment", "dp", None, None),
            P("segment", "dp", None, None),
            P("segment", "dp", None, None),
            P("segment", "dp", None),
        ),
        check_vma=False,
    )
```

time: 142 us -> 79 us (0.56)
  waiting for transfers between devices: 78.6 us -> 16.5 us
  Pallas kernels: 0 us -> 27.1 us
  matrix products: 22.6 us -> 0 us
  starting transfers between devices: 5.18 us -> 26.4 us
  between operations: 14.9 us -> 1.56 us
  local copies, waits for them, and re-layouts: 15.7 us -> 6.15 us
  other arithmetic: 4.35 us -> 0.95 us
    unnamed x3 -> x0, waiting for transfers between devices: 44.2 us -> none
    all_gather x1 -> x0, waiting for transfers between devices: 34.4 us -> none  [on_device(): full_weight = lax.all_gather(shard_weight, 'dp', axis=0, tiled=True)]
    pallas_call x0 -> x9, Pallas kernels: none -> 27.1 us  [call(): pl.pallas_call(body, out_shape=out_shape, in_specs=[SMEM] + [VMEM] * (len...]
    dot_general x9 -> x0, matrix products: 22.6 us -> none  [the longest x1 5.72 us: on_device(): lax.dot_general(tokens_in, grad_pre_b, (((0,), (0,)), ((), ())), preferre...]
    ppermute x1 -> x33, starting transfers between devices: 5.1 us -> 26.4 us  [the longest x31 22.2 us: pair(): return lax.ppermute(x, 'dp', [(i, i ^ mask) for i in range(count)])]
    ppermute x1 -> x33, waiting for transfers between devices: 0.01 us -> 16.5 us  [the longest x31 13 us: pair(): return lax.ppermute(x, 'dp', [(i, i ^ mask) for i in range(count)])]
    unnamed x27 -> x14, local copies, waits for them, and re-layouts: 14.3 us -> 3.76 us
    reduce_sum x3 -> x0, other arithmetic: 4.02 us -> none  [the longest x1 2.39 us: window(): centered = mixed_heads - row_mean]
  transfers between devices with their start and end apart: 3 -> 33, of which waited for: 2 -> 12; matrix products, arithmetic and copies ran while one was open for 12% -> 3% of each run, Pallas kernels for 0% -> 17%
where the time goes in v1:
time: 79 us; the launch traced here: 78.7 us
  Pallas kernels  27.1 us (34%)
  starting transfers between devices  26.4 us (33%)
  waiting for transfers between devices  16.5 us (21%)
  local copies, waits for them, and re-layouts  6.15 us (8%)
  between operations  1.56 us (2%)
  other arithmetic  0.95 us (1%)
    pallas_call x9, Pallas kernels, call(): pl.pallas_call(body, out_shape=out_shape, in_specs=[SMEM] + [VMEM] * (len...  27.1 us
    ppermute x31, starting transfers between devices, pair(): return lax.ppermute(x, 'dp', [(i, i ^ mask) for i in range(count)])  22.2 us
    ppermute x31, waiting for transfers between devices, pair(): return lax.ppermute(x, 'dp', [(i, i ^ mask) for i in range(count)])  13 us
    ppermute x2, starting transfers between devices, from_next(): lax.ppermute(x, ('dp', 'segment'), [(i * seg + s, (i ^ mask) * seg + (s -...  4.23 us
    unnamed x14, local copies, waits for them, and re-layouts  3.76 us
    ppermute x2, waiting for transfers between devices, from_next(): lax.ppermute(x, ('dp', 'segment'), [(i * seg + s, (i ^ mask) * seg + (s -...  3.52 us
  transfers between devices with their start and end apart: 33, of which 12 were waited for; matrix products, arithmetic and copies ran while one was open for 3% of the time, Pallas kernels for 17%

profile of v1, /device:TPU:0, one launch (start us, length us, event | category | flops | bytes accessed | tf_op | source)
XLA Modules:
  0.0 78.7 jit_solution(11803040876942926098)
XLA Ops:
  0.7 1.2 %fusion = (bf16[128,512]{1,0:T(8,128)(2,1)S(1)}, bf16[128,512]{1,0:T(8,128)(2,1)S(1)}, bf16[128,512]{1,0:T(8,128)(2,1)S(1)}, bf16[128,512]{1,0:T(8,128)(2,1)S(1)}) fusion(bf16[128,2048]{1,0:T(8,128)(2,1)} %bitcast.31), kind=kLoop, calls=%fused_computation.13 | loop fusion | bytes 1048576 | tf_op jit(solution)/shard_map/slice | solution.py:273
  2.0 0.5 collective-permute-start.1
  2.6 2.6 %collective-permute-start.2 = (bf16[128,1024]{1,0:T(8,128)(2,1)S(1)}, bf16[128,1024]{1,0:T(8,128)(2,1)S(1)}, u32[]{:S(2)}, u32[]{:S(2)}) collective-permute-start(bf16[128,1024]{1,0:T(8,128)(2,1)S(1)} %get-tuple-element.73.refs_0_), channel_id=1, source_target_pairs={{0,8},{4,12},{8,0},{12,4},{16,24},{20,28},{24,16},{28,20},{1,9},{5... | collective-permute-start | bytes 786440 | tf_op jit(solution)/shard_map/ppermute | solution.py:27
  5.3 1.5 %collective-permute-start.4 = (bf16[128,1024]{1,0:T(8,128)(2,1)S(1)}, bf16[128,1024]{1,0:T(8,128)(2,1)S(1)}, u32[]{:S(2)}, u32[]{:S(2)}) collective-permute-start(bf16[128,1024]{1,0:T(8,128)(2,1)S(1)} %get-tuple-element.73.refs_0_), channel_id=1, source_target_pairs={{0,16},{4,20},{8,24},{12,28},{16,0},{20,4},{24,8},{28,12},{1,17},{... | collective-permute-start | bytes 786440 | tf_op jit(solution)/shard_map/ppermute | solution.py:27
  6.9 1.1 %dynamic-slice_bitcast_fusion = (bf16[256,512]{1,0:T(8,128)(2,1)S(1)}, bf16[256,512]{1,0:T(8,128)(2,1)S(1)}) fusion(bf16[1,1,256,1024]{3,2,1,0:T(8,128)(2,1)} %param.9, s32[]{:T(128)S(6)} %select_n.23, s32[]{:T(128)S(6)} %select_n.24), kind=kLoop, calls=%fused_computation.6 | loop fusion | bytes 1048584 | tf_op jit(solution)/shard_map/dynamic_slice | solution.py:271
  8.0 0.5 collective-permute-start.5
  8.6 0.3 collective-permute-start.3
  8.9 3.4 %collective-permute-done.2.refs_1_.refs_2_ = bf16[128,1024]{1,0:T(8,128)(2,1)S(1)} collective-permute-done((bf16[128,1024]{1,0:T(8,128)(2,1)S(1)}, bf16[128,1024]{1,0:T(8,128)(2,1)S(1)}, u32[]{:S(2)}, u32[]{:S(2)}) %collective-permute-start.2) | collective-permute-done | bytes 262176 | tf_op jit(solution)/shard_map/ppermute | solution.py:27
  12.3 4.1 %collective-permute-start.11 = (bf16[256,512]{1,0:T(8,128)(2,1)S(1)}, bf16[256,512]{1,0:T(8,128)(2,1)S(1)}, u32[]{:S(2)}, u32[]{:S(2)}) collective-permute-start(bf16[256,512]{1,0:T(8,128)(2,1)S(1)} %get-tuple-element.71), channel_id=1, source_target_pairs={{0,3},{1,0},{2,1},{3,2},{4,7},{5,4},{6,5},{7,6},{8,11},{9,8},{10,9... | collective-permute-start | bytes 786440 | tf_op jit(solution)/shard_map/ppermute | solution.py:32
  16.4 0.2 collective-permute-start.12
  16.6 2.3 %collective-permute-done.5.refs_4_.refs_5_ = bf16[128,1024]{1,0:T(8,128)(2,1)S(1)} collective-permute-done((bf16[128,1024]{1,0:T(8,128)(2,1)S(1)}, bf16[128,1024]{1,0:T(8,128)(2,1)S(1)}, u32[]{:S(2)}, u32[]{:S(2)}) %collective-permute-start.5) | collective-permute-done | bytes 262176 | tf_op jit(solution)/shard_map/ppermute | solution.py:27
  18.9 0.7 collective-permute-start.10
  19.6 3.5 %collective-permute-done.11.co = bf16[256,512]{1,0:T(8,128)(2,1)S(1)} collective-permute-done((bf16[256,512]{1,0:T(8,128)(2,1)S(1)}, bf16[256,512]{1,0:T(8,128)(2,1)S(1)}, u32[]{:S(2)}, u32[]{:S(2)}) %collective-permute-start.11) | collective-permute-done | bytes 262176 | tf_op jit(solution)/shard_map/ppermute | solution.py:32
  23.1 1.5 %collective-permute-start.6 = (bf16[128,1024]{1,0:T(8,128)(2,1)S(1)}, bf16[128,1024]{1,0:T(8,128)(2,1)S(1)}, u32[]{:S(2)}, u32[]{:S(2)}) collective-permute-start(bf16[128,1024]{1,0:T(8,128)(2,1)S(1)} %collective-permute-done.2.refs_1_.refs_2_), channel_id=1, source_target_pairs={{0,16},{4,20},{8,24},{12,28},{16,0},{20,4},{24,8},{28,12},{1,17},{... | collective-permute-start | bytes 786440 | tf_op jit(solution)/shard_map/ppermute | solution.py:27
  24.6 1.5 %collective-permute-start.7 = (bf16[128,1024]{1,0:T(8,128)(2,1)S(1)}, bf16[128,1024]{1,0:T(8,128)(2,1)S(1)}, u32[]{:S(2)}, u32[]{:S(2)}) collective-permute-start(bf16[128,1024]{1,0:T(8,128)(2,1)S(1)} %collective-permute-done.5.refs_4_.refs_5_), channel_id=1, source_target_pairs={{0,8},{4,12},{8,0},{12,4},{16,24},{20,28},{24,16},{28,20},{1,9},{5... | collective-permute-start | bytes 786440 | tf_op jit(solution)/shard_map/ppermute | solution.py:27
  26.8 0.7 pad_add_fusion.sc
  27.5 1.0 %shard_map.94.refs_0_ = f32[512,1024]{1,0:T(8,128)S(1)} custom-call(s32[3]{0:T(128)S(1)} %pad_add_fusion.sc, bf16[256,1024]{1,0:T(8,128)(2,1)S(1)} %bitcast.20, bf16[256,1024]{1,0:T(8,128)(2,1)S(1)} %collective-permute-done.8.xp, bf16[128,1024]{1,0:T(8,128)(2,1)S(1)} %get-tuple-element.73.refs_0_, bf16[128,1024]{1,0:T(8,128)(2,1)S(1)} %collective-permute-done.1.refs_1_), custom_call_target="tpu_custom_call" | custom-call | tf_op jit(solution)/shard_map/pallas_call | solution.py:40
  28.5 1.3 %copy-done.1 = f32[512,1024]{1,0:T(8,128)} copy-done((f32[512,1024]{1,0:T(8,128)}, f32[512,1024]{1,0:T(8,128)S(1)}, u32[]{:S(2)}) %copy-start.1) | copy-done | bytes 2097176
  29.8 2.5 %shard_map.95.prev = f32[512,1024]{1,0:T(8,128)S(1)} custom-call(s32[3]{0:T(128)S(1)} %pad_add_fusion.sc, bf16[256,1024]{1,0:T(8,128)(2,1)S(1)} %bitcast.21, bf16[256,1024]{1,0:T(8,128)(2,1)S(1)} %collective-permute-done.8.xp, f32[512,1024]{1,0:T(8,128)} %copy-done.1, bf16[128,1024]{1,0:T(8,128)(2,1)S(1)} %collective-permute-done.2.refs_1_.refs_2_, ...), custom_call_target="tpu_custom_call" | custom-call | tf_op jit(solution)/shard_map/pallas_call | solution.py:40
  32.3 1.3 %copy-done = f32[512,1024]{1,0:T(8,128)} copy-done((f32[512,1024]{1,0:T(8,128)}, f32[512,1024]{1,0:T(8,128)S(1)}, u32[]{:S(2)}) %copy-start) | copy-done | bytes 2097176
  33.7 5.9 %shard_map.96 = (bf16[512,1024]{1,0:T(8,128)(2,1)S(1)}, f32[512,1024]{1,0:T(8,128)}, bf16[8,256,256]{2,1,0:T(8,128)(2,1)S(1)}, bf16[8,256,256]{2,1,0:T(8,128)(2,...) custom-call(s32[3]{0:T(128)S(1)} %pad_add_fusion.sc, bf16[256,1024]{1,0:T(8,128)(2,1)S(1)} %bitcast.22, ...), custom_call_target="tpu_custom_call" | custom-call | tf_op jit(solution)/shard_map/pallas_call | solution.py:40
  39.6 1.0 %copy-done.6 = bf16[8,256,256]{2,1,0:T(8,128)(2,1)} copy-done((bf16[8,256,256]{2,1,0:T(8,128)(2,1)}, bf16[8,256,256]{2,1,0:T(8,128)(2,1)S(1)}, u32[]{:S(2)}) %copy-start.6) | copy-done | bytes 1048600
  40.5 0.9 %shard_map.93.xt = bf16[1024,512]{1,0:T(8,128)(2,1)S(1)} custom-call(s32[3]{0:T(128)S(1)} %pad_add_fusion.sc, bf16[256,1024]{1,0:T(8,128)(2,1)S(1)} %bitcast.23, bf16[256,1024]{1,0:T(8,128)(2,1)S(1)} %collective-permute-done.8.xp), custom_call_target="tpu_custom_call" | custom-call | tf_op jit(solution)/shard_map/pallas_call | solution.py:40
  41.5 0.2 collective-permute-done.13.theirs
  41.7 5.7 %shard_map.98 = (bf16[128,512]{1,0:T(8,128)(2,1)S(1)}, bf16[128,512]{1,0:T(8,128)(2,1)S(1)}, bf16[128,512]{1,0:T(8,128)(2,1)S(1)}, bf16[128,512]{1,0:T(8,128)(2,...) custom-call(s32[3]{0:T(128)S(1)} %pad_add_fusion.sc, ...), custom_call_target="tpu_custom_call" | custom-call | tf_op jit(solution)/shard_map/pallas_call | solution.py:40
  47.4 0.6 collective-permute-start.30
  48.0 0.5 collective-permute-start.27
  48.6 5.7 %shard_map.97 = (bf16[128,512]{1,0:T(8,128)(2,1)S(1)}, bf16[128,512]{1,0:T(8,128)(2,1)S(1)}, bf16[128,512]{1,0:T(8,128)(2,1)S(1)}, bf16[128,512]{1,0:T(8,128)(2,...) custom-call(s32[3]{0:T(128)S(1)} %pad_add_fusion.sc, ...), custom_call_target="tpu_custom_call" | custom-call | tf_op jit(solution)/shard_map/pallas_call | solution.py:40
  54.3 1.6 %collective-permute-start.23 = (bf16[128,512]{1,0:T(8,128)(2,1)S(1)}, bf16[128,512]{1,0:T(8,128)(2,1)S(1)}, u32[]{:S(2)}, u32[]{:S(2)}) collective-permute-start(bf16[128,512]{1,0:T(8,128)(2,1)S(1)} %get-tuple-element.60), channel_id=1, source_target_pairs={{0,16},{4,20},{8,24},{12,28},{16,0},{20,4},{24,8},{28,12},{1,17},{... | collective-permute-start | bytes 393224 | tf_op jit(solution)/shard_map/ppermute | solution.py:27
  55.9 1.5 %collective-permute-start.20 = (bf16[128,512]{1,0:T(8,128)(2,1)S(1)}, bf16[128,512]{1,0:T(8,128)(2,1)S(1)}, u32[]{:S(2)}, u32[]{:S(2)}) collective-permute-start(bf16[128,512]{1,0:T(8,128)(2,1)S(1)} %get-tuple-element.57), channel_id=1, source_target_pairs={{0,8},{4,12},{8,0},{12,4},{16,24},{20,28},{24,16},{28,20},{1,9},{5... | collective-permute-start | bytes 393224 | tf_op jit(solution)/shard_map/ppermute | solution.py:27
  57.3 0.5 collective-permute-start.26
  57.9 2.0 %shard_map.99 = (f32[256,1024]{1,0:T(8,128)S(1)}, bf16[256,1024]{1,0:T(8,128)(2,1)S(1)}) custom-call(s32[3]{0:T(128)S(1)} %pad_add_fusion.sc, bf16[128,1024]{1,0:T(8,128)(2,1)S(1)} %get-tuple-element.73.refs_0_, bf16[128,1024]{1,0:T(8,128)(2,1)S(1)} %collective-permute-done.1.refs_1_, bf16[128,1024]{1,0:T(8,128)(2,1)S(1)} %collective-permute-done.2.refs_1_.refs_2_, ...), custom_call_target="tpu_custom_call" | custom-call | tf_op jit(solution)/shard_map/pallas_call | solution.py:40
  60.0 0.7 collective-permute-start.32
  60.8 1.2 %collective-permute-done.20 = bf16[128,512]{1,0:T(8,128)(2,1)S(1)} collective-permute-done((bf16[128,512]{1,0:T(8,128)(2,1)S(1)}, bf16[128,512]{1,0:T(8,128)(2,1)S(1)}, u32[]{:S(2)}, u32[]{:S(2)}) %collective-permute-start.20) | collective-permute-done | bytes 131104 | tf_op jit(solution)/shard_map/ppermute | solution.py:27
  62.1 1.5 %collective-permute-start.19 = (bf16[128,512]{1,0:T(8,128)(2,1)S(1)}, bf16[128,512]{1,0:T(8,128)(2,1)S(1)}, u32[]{:S(2)}, u32[]{:S(2)}) collective-permute-start(bf16[128,512]{1,0:T(8,128)(2,1)S(1)} %get-tuple-element.55), channel_id=1, source_target_pairs={{0,8},{4,12},{8,0},{12,4},{16,24},{20,28},{24,16},{28,20},{1,9},{5... | collective-permute-start | bytes 393224 | tf_op jit(solution)/shard_map/ppermute | solution.py:27
  63.5 0.6 collective-permute-start.25
  64.2 1.0 %collective-permute-done.32.refs_11_ = bf16[128,512]{1,0:T(8,128)(2,1)S(1)} collective-permute-done((bf16[128,512]{1,0:T(8,128)(2,1)S(1)}, bf16[128,512]{1,0:T(8,128)(2,1)S(1)}, u32[]{:S(2)}, u32[]{:S(2)}) %collective-permute-start.32) | collective-permute-done | bytes 131104 | tf_op jit(solution)/shard_map/ppermute | solution.py:27
  65.3 1.8 %collective-permute-start.31 = (bf16[128,512]{1,0:T(8,128)(2,1)S(1)}, bf16[128,512]{1,0:T(8,128)(2,1)S(1)}, u32[]{:S(2)}, u32[]{:S(2)}) collective-permute-start(bf16[128,512]{1,0:T(8,128)(2,1)S(1)} %add_convert_fusion), channel_id=1, source_target_pairs={{0,12},{4,8},{8,4},{12,0},{16,28},{20,24},{24,20},{28,16},{1,13},{... | collective-permute-start | bytes 393224 | tf_op jit(solution)/shard_map/ppermute | solution.py:27
  67.1 1.3 %collective-permute-start.28 = (bf16[128,512]{1,0:T(8,128)(2,1)S(1)}, bf16[128,512]{1,0:T(8,128)(2,1)S(1)}, u32[]{:S(2)}, u32[]{:S(2)}) collective-permute-start(bf16[128,512]{1,0:T(8,128)(2,1)S(1)} %add_convert_fusion.1), channel_id=1, source_target_pairs={{0,16},{4,20},{8,24},{12,28},{16,0},{20,4},{24,8},{28,12},{1,17},{... | collective-permute-start | bytes 393224 | tf_op jit(solution)/shard_map/ppermute | solution.py:27
  68.3 0.4 collective-permute-start.24
  68.8 0.5 collective-permute-start.21
  69.5 0.9 %collective-permute-done.31.refs_10_ = bf16[128,512]{1,0:T(8,128)(2,1)S(1)} collective-permute-done((bf16[128,512]{1,0:T(8,128)(2,1)S(1)}, bf16[128,512]{1,0:T(8,128)(2,1)S(1)}, u32[]{:S(2)}, u32[]{:S(2)}) %collective-permute-start.31) | collective-permute-done | bytes 131104 | tf_op jit(solution)/shard_map/ppermute | solution.py:27
  70.3 0.9 %collective-permute-start.16 = (bf16[256,256]{1,0:T(8,128)(2,1)S(1)}, bf16[256,256]{1,0:T(8,128)(2,1)S(1)}, u32[]{:S(2)}, u32[]{:S(2)}) collective-permute-start(bf16[256,256]{1,0:T(8,128)(2,1)S(1)} %slice.29), channel_id=1, source_target_pairs={{0,4},{4,0},{8,12},{12,8},{16,20},{20,16},{24,28},{28,24},{1,5},{5... | collective-permute-start | bytes 393224 | tf_op jit(solution)/shard_map/ppermute | solution.py:27
  71.3 1.0 %collective-permute-done.28.refs_8_ = bf16[128,512]{1,0:T(8,128)(2,1)S(1)} collective-permute-done((bf16[128,512]{1,0:T(8,128)(2,1)S(1)}, bf16[128,512]{1,0:T(8,128)(2,1)S(1)}, u32[]{:S(2)}, u32[]{:S(2)}) %collective-permute-start.28) | collective-permute-done | bytes 131104 | tf_op jit(solution)/shard_map/ppermute | solution.py:27
  72.3 1.9 %collective-permute-done.24.refs_4_ = bf16[128,512]{1,0:T(8,128)(2,1)S(1)} collective-permute-done((bf16[128,512]{1,0:T(8,128)(2,1)S(1)}, bf16[128,512]{1,0:T(8,128)(2,1)S(1)}, u32[]{:S(2)}, u32[]{:S(2)}) %collective-permute-start.24) | collective-permute-done | bytes 131104 | tf_op jit(solution)/shard_map/ppermute | solution.py:27
  74.3 0.8 %collective-permute-done.21.refs_2_ = bf16[128,512]{1,0:T(8,128)(2,1)S(1)} collective-permute-done((bf16[128,512]{1,0:T(8,128)(2,1)S(1)}, bf16[128,512]{1,0:T(8,128)(2,1)S(1)}, u32[]{:S(2)}, u32[]{:S(2)}) %collective-permute-start.21) | collective-permute-done | bytes 131104 | tf_op jit(solution)/shard_map/ppermute | solution.py:27
  75.2 1.7 %shard_map.101 = f32[128,2048]{1,0:T(8,128)} custom-call(s32[3]{0:T(128)S(1)} %pad_add_fusion.sc, bf16[128,512]{1,0:T(8,128)(2,1)S(1)} %get-tuple-element.54.refs_0_, bf16[128,512]{1,0:T(8,128)(2,1)S(1)} %collective-permute-done.19.refs_1_, bf16[128,512]{1,0:T(8,128)(2,1)S(1)} %collective-permute-done.21.refs_2_, ...), custom_call_target="tpu_custom_call" | custom-call | tf_op jit(solution)/shard_map/pallas_call | solution.py:40
  76.9 1.8 %shard_map.100 = (bf16[256,1024]{1,0:T(8,128)(2,1)}, bf16[256,1024]{1,0:T(8,128)(2,1)}, bf16[256,1024]{1,0:T(8,128)(2,1)}) custom-call(s32[3]{0:T(128)S(1)} %pad_add_fusion.sc, f32[256,1024]{1,0:T(8,128)S(1)} %get-tuple-element.45.gi_o, bf16[256,1024]{1,0:T(8,128)(2,1)S(1)} %collective-permute-done.14.gi_r, bf16[512,256]{1,0:T(8,128)(2,1)S(1)} %get-tuple-element.47.v0, ...), custom_call_target="tpu_custom_call" | custom-call | tf_op jit(solution)/shard_map/pallas_call | solution.py:40
  (55 shorter events, 1.4 us)
Async XLA Ops:
  0.6 4.5 %copy-start.2 = (bf16[1,1,256,1024]{3,2,1,0:T(8,128)(2,1)S(1)}, bf16[1,1,256,1024]{3,2,1,0:T(8,128)(2,1)}, u32[]{:S(2)}) copy-start(bf16[1,1,256,1024]{3,2,1,0:T(8,128)(2,1)} %param.6) | copy-start | bytes 1572868
  0.6 15.7 %copy-start.4 = (bf16[1,1,256,1024]{3,2,1,0:T(8,128)(2,1)S(1)}, bf16[1,1,256,1024]{3,2,1,0:T(8,128)(2,1)}, u32[]{:S(2)}) copy-start(bf16[1,1,256,1024]{3,2,1,0:T(8,128)(2,1)} %param.8) | copy-start | bytes 1572868
  0.7 15.7 %copy-start.3 = (bf16[1,1,256,1024]{3,2,1,0:T(8,128)(2,1)S(1)}, bf16[1,1,256,1024]{3,2,1,0:T(8,128)(2,1)}, u32[]{:S(2)}) copy-start(bf16[1,1,256,1024]{3,2,1,0:T(8,128)(2,1)} %param.7) | copy-start | bytes 1572868
  2.0 6.5 %collective-permute-start.1 = (bf16[128,1024]{1,0:T(8,128)(2,1)S(1)}, bf16[128,1024]{1,0:T(8,128)(2,1)S(1)}, u32[]{:S(2)}, u32[]{:S(2)}) collective-permute-start(bf16[128,1024]{1,0:T(8,128)(2,1)S(1)} %get-tuple-element.72), channel_id=1, source_target_pairs={{0,4},{4,0},{8,12},{12,8},{16,20},{20,16},{24,28},{28,24},{1,5},{5... | collective-permute-start | bytes 786440 | tf_op jit(solution)/shard_map/ppermute | solution.py:27
  2.6 9.7 %collective-permute-start.2 = (bf16[128,1024]{1,0:T(8,128)(2,1)S(1)}, bf16[128,1024]{1,0:T(8,128)(2,1)S(1)}, u32[]{:S(2)}, u32[]{:S(2)}) collective-permute-start(bf16[128,1024]{1,0:T(8,128)(2,1)S(1)} %get-tuple-element.73.refs_0_), channel_id=1, source_target_pairs={{0,8},{4,12},{8,0},{12,4},{16,24},{20,28},{24,16},{28,20},{1,9},{5... | collective-permute-start | bytes 786440 | tf_op jit(solution)/shard_map/ppermute | solution.py:27
  5.1 19.5 %collective-permute-start.8 = (bf16[256,1024]{1,0:T(8,128)(2,1)S(1)}, bf16[256,1024]{1,0:T(8,128)(2,1)S(1)}, u32[]{:S(2)}, u32[]{:S(2)}) collective-permute-start(bf16[256,1024]{1,0:T(8,128)(2,1)S(1)} %bitcast.19), channel_id=1, source_target_pairs={{0,4},{4,0},{8,12},{12,8},{16,20},{20,16},{24,28},{28,24},{1,5},{5... | collective-permute-start | bytes 1572872 | tf_op jit(solution)/shard_map/ppermute | solution.py:27
  5.3 11.1 %collective-permute-start.4 = (bf16[128,1024]{1,0:T(8,128)(2,1)S(1)}, bf16[128,1024]{1,0:T(8,128)(2,1)S(1)}, u32[]{:S(2)}, u32[]{:S(2)}) collective-permute-start(bf16[128,1024]{1,0:T(8,128)(2,1)S(1)} %get-tuple-element.73.refs_0_), channel_id=1, source_target_pairs={{0,16},{4,20},{8,24},{12,28},{16,0},{20,4},{24,8},{28,12},{1,17},{... | collective-permute-start | bytes 786440 | tf_op jit(solution)/shard_map/ppermute | solution.py:27
  6.8 1.2 %collective-permute-start = (s32[1]{0:T(128)}, s32[1]{0:T(128)}, u32[]{:S(2)}, u32[]{:S(2)}) collective-permute-start(s32[1]{0:T(128)} %bitcast.1), channel_id=1, source_target_pairs={{0,4},{4,0},{8,12},{12,8},{16,20},{20,16},{24,28},{28,24},{1,5},{5... | collective-permute-start | bytes 20 | tf_op jit(solution)/shard_map/ppermute | solution.py:27
  8.0 10.8 %collective-permute-start.5 = (bf16[128,1024]{1,0:T(8,128)(2,1)S(1)}, bf16[128,1024]{1,0:T(8,128)(2,1)S(1)}, u32[]{:S(2)}, u32[]{:S(2)}) collective-permute-start(bf16[128,1024]{1,0:T(8,128)(2,1)S(1)} %get-tuple-element.72), channel_id=1, source_target_pairs={{0,20},{4,16},{8,28},{12,24},{16,4},{20,0},{24,12},{28,8},{1,21},{... | collective-permute-start | bytes 786440 | tf_op jit(solution)/shard_map/ppermute | solution.py:27
  8.6 11.0 %collective-permute-start.3 = (bf16[128,1024]{1,0:T(8,128)(2,1)S(1)}, bf16[128,1024]{1,0:T(8,128)(2,1)S(1)}, u32[]{:S(2)}, u32[]{:S(2)}) collective-permute-start(bf16[128,1024]{1,0:T(8,128)(2,1)S(1)} %get-tuple-element.72), channel_id=1, source_target_pairs={{0,12},{4,8},{8,4},{12,0},{16,28},{20,24},{24,20},{28,16},{1,13},{... | collective-permute-start | bytes 786440 | tf_op jit(solution)/shard_map/ppermute | solution.py:27
  12.3 10.8 %collective-permute-start.11 = (bf16[256,512]{1,0:T(8,128)(2,1)S(1)}, bf16[256,512]{1,0:T(8,128)(2,1)S(1)}, u32[]{:S(2)}, u32[]{:S(2)}) collective-permute-start(bf16[256,512]{1,0:T(8,128)(2,1)S(1)} %get-tuple-element.71), channel_id=1, source_target_pairs={{0,3},{1,0},{2,1},{3,2},{4,7},{5,4},{6,5},{7,6},{8,11},{9,8},{10,9... | collective-permute-start | bytes 786440 | tf_op jit(solution)/shard_map/ppermute | solution.py:32
  16.4 17.3 %collective-permute-start.12 = (bf16[256,512]{1,0:T(8,128)(2,1)S(1)}, bf16[256,512]{1,0:T(8,128)(2,1)S(1)}, u32[]{:S(2)}, u32[]{:S(2)}) collective-permute-start(bf16[256,512]{1,0:T(8,128)(2,1)S(1)} %get-tuple-element.70), channel_id=1, source_target_pairs={{0,7},{1,4},{2,5},{3,6},{4,3},{5,0},{6,1},{7,2},{8,15},{9,12},{10,... | collective-permute-start | bytes 786440 | tf_op jit(solution)/shard_map/ppermute | solution.py:32
  18.9 14.8 %collective-permute-start.10 = (bf16[256,512]{1,0:T(8,128)(2,1)S(1)}, bf16[256,512]{1,0:T(8,128)(2,1)S(1)}, u32[]{:S(2)}, u32[]{:S(2)}) collective-permute-start(bf16[256,512]{1,0:T(8,128)(2,1)S(1)} %dynamic-slice_bitcast_fusion.2), channel_id=1, source_target_pairs={{0,4},{4,0},{8,12},{12,8},{16,20},{20,16},{24,28},{28,24},{1,5},{5... | collective-permute-start | bytes 786440 | tf_op jit(solution)/shard_map/ppermute | solution.py:27
  19.6 14.1 %collective-permute-start.9 = (bf16[256,512]{1,0:T(8,128)(2,1)S(1)}, bf16[256,512]{1,0:T(8,128)(2,1)S(1)}, u32[]{:S(2)}, u32[]{:S(2)}) collective-permute-start(bf16[256,512]{1,0:T(8,128)(2,1)S(1)} %dynamic-slice_bitcast_fusion.3), channel_id=1, source_target_pairs={{0,4},{4,0},{8,12},{12,8},{16,20},{20,16},{24,28},{28,24},{1,5},{5... | collective-permute-start | bytes 786440 | tf_op jit(solution)/shard_map/ppermute | solution.py:27
  23.1 10.6 %collective-permute-start.6 = (bf16[128,1024]{1,0:T(8,128)(2,1)S(1)}, bf16[128,1024]{1,0:T(8,128)(2,1)S(1)}, u32[]{:S(2)}, u32[]{:S(2)}) collective-permute-start(bf16[128,1024]{1,0:T(8,128)(2,1)S(1)} %collective-permute-done.2.refs_1_.refs_2_), channel_id=1, source_target_pairs={{0,16},{4,20},{8,24},{12,28},{16,0},{20,4},{24,8},{28,12},{1,17},{... | collective-permute-start | bytes 786440 | tf_op jit(solution)/shard_map/ppermute | solution.py:27
  24.6 9.1 %collective-permute-start.7 = (bf16[128,1024]{1,0:T(8,128)(2,1)S(1)}, bf16[128,1024]{1,0:T(8,128)(2,1)S(1)}, u32[]{:S(2)}, u32[]{:S(2)}) collective-permute-start(bf16[128,1024]{1,0:T(8,128)(2,1)S(1)} %collective-permute-done.5.refs_4_.refs_5_), channel_id=1, source_target_pairs={{0,8},{4,12},{8,0},{12,4},{16,24},{20,28},{24,16},{28,20},{1,9},{5... | collective-permute-start | bytes 786440 | tf_op jit(solution)/shard_map/ppermute | solution.py:27
  28.5 1.3 %copy-start.1 = (f32[512,1024]{1,0:T(8,128)}, f32[512,1024]{1,0:T(8,128)S(1)}, u32[]{:S(2)}) copy-start(f32[512,1024]{1,0:T(8,128)S(1)} %shard_map.94.refs_0_) | copy-start | bytes 6291460
  32.3 1.3 %copy-start = (f32[512,1024]{1,0:T(8,128)}, f32[512,1024]{1,0:T(8,128)S(1)}, u32[]{:S(2)}) copy-start(f32[512,1024]{1,0:T(8,128)S(1)} %shard_map.95.prev) | copy-start | bytes 6291460
  39.6 1.0 %copy-start.6 = (bf16[8,256,256]{2,1,0:T(8,128)(2,1)}, bf16[8,256,256]{2,1,0:T(8,128)(2,1)S(1)}, u32[]{:S(2)}) copy-start(bf16[8,256,256]{2,1,0:T(8,128)(2,1)S(1)} %get-tuple-element.39.prob) | copy-start | bytes 3145732
  40.5 1.0 %copy-start.5 = (bf16[512,1024]{1,0:T(8,128)(2,1)}, bf16[512,1024]{1,0:T(8,128)(2,1)S(1)}, u32[]{:S(2)}) copy-start(bf16[512,1024]{1,0:T(8,128)(2,1)S(1)} %get-tuple-element.37.act) | copy-start | bytes 3145732
  40.5 1.2 %collective-permute-start.13 = (f32[8,512]{1,0:T(8,128)S(1)}, f32[8,512]{1,0:T(8,128)S(1)}, u32[]{:S(2)}, u32[]{:S(2)}) collective-permute-start(f32[8,512]{1,0:T(8,128)S(1)} %get-tuple-element.42.mine), channel_id=1, source_target_pairs={{0,4},{4,0},{8,12},{12,8},{16,20},{20,16},{24,28},{28,24},{1,5},{5... | collective-permute-start | bytes 49160 | tf_op jit(solution)/shard_map/ppermute | solution.py:27
  47.4 12.4 %collective-permute-start.30 = (bf16[128,512]{1,0:T(8,128)(2,1)S(1)}, bf16[128,512]{1,0:T(8,128)(2,1)S(1)}, u32[]{:S(2)}, u32[]{:S(2)}) collective-permute-start(bf16[128,512]{1,0:T(8,128)(2,1)S(1)} %get-tuple-element.68), channel_id=1, source_target_pairs={{0,16},{4,20},{8,24},{12,28},{16,0},{20,4},{24,8},{28,12},{1,17},{... | collective-permute-start | bytes 393224 | tf_op jit(solution)/shard_map/ppermute | solution.py:27
  48.0 12.0 %collective-permute-start.27 = (bf16[128,512]{1,0:T(8,128)(2,1)S(1)}, bf16[128,512]{1,0:T(8,128)(2,1)S(1)}, u32[]{:S(2)}, u32[]{:S(2)}) collective-permute-start(bf16[128,512]{1,0:T(8,128)(2,1)S(1)} %get-tuple-element.65), channel_id=1, source_target_pairs={{0,8},{4,12},{8,0},{12,4},{16,24},{20,28},{24,16},{28,20},{1,9},{5... | collective-permute-start | bytes 393224 | tf_op jit(solution)/shard_map/ppermute | solution.py:27
  54.3 6.5 %collective-permute-start.23 = (bf16[128,512]{1,0:T(8,128)(2,1)S(1)}, bf16[128,512]{1,0:T(8,128)(2,1)S(1)}, u32[]{:S(2)}, u32[]{:S(2)}) collective-permute-start(bf16[128,512]{1,0:T(8,128)(2,1)S(1)} %get-tuple-element.60), channel_id=1, source_target_pairs={{0,16},{4,20},{8,24},{12,28},{16,0},{20,4},{24,8},{28,12},{1,17},{... | collective-permute-start | bytes 393224 | tf_op jit(solution)/shard_map/ppermute | solution.py:27
  55.9 6.2 %collective-permute-start.20 = (bf16[128,512]{1,0:T(8,128)(2,1)S(1)}, bf16[128,512]{1,0:T(8,128)(2,1)S(1)}, u32[]{:S(2)}, u32[]{:S(2)}) collective-permute-start(bf16[128,512]{1,0:T(8,128)(2,1)S(1)} %get-tuple-element.57), channel_id=1, source_target_pairs={{0,8},{4,12},{8,0},{12,4},{16,24},{20,28},{24,16},{28,20},{1,9},{5... | collective-permute-start | bytes 393224 | tf_op jit(solution)/shard_map/ppermute | solution.py:27
  57.3 6.2 %collective-permute-start.26 = (bf16[128,512]{1,0:T(8,128)(2,1)S(1)}, bf16[128,512]{1,0:T(8,128)(2,1)S(1)}, u32[]{:S(2)}, u32[]{:S(2)}) collective-permute-start(bf16[128,512]{1,0:T(8,128)(2,1)S(1)} %get-tuple-element.63), channel_id=1, source_target_pairs={{0,8},{4,12},{8,0},{12,4},{16,24},{20,28},{24,16},{28,20},{1,9},{5... | collective-permute-start | bytes 393224 | tf_op jit(solution)/shard_map/ppermute | solution.py:27
  59.9 3.7 %collective-permute-start.29 = (bf16[128,512]{1,0:T(8,128)(2,1)S(1)}, bf16[128,512]{1,0:T(8,128)(2,1)S(1)}, u32[]{:S(2)}, u32[]{:S(2)}) collective-permute-start(bf16[128,512]{1,0:T(8,128)(2,1)S(1)} %get-tuple-element.66), channel_id=1, source_target_pairs={{0,4},{4,0},{8,12},{12,8},{16,20},{20,16},{24,28},{28,24},{1,5},{5... | collective-permute-start | bytes 393224 | tf_op jit(solution)/shard_map/ppermute | solution.py:27
  60.0 5.2 %collective-permute-start.32 = (bf16[128,512]{1,0:T(8,128)(2,1)S(1)}, bf16[128,512]{1,0:T(8,128)(2,1)S(1)}, u32[]{:S(2)}, u32[]{:S(2)}) collective-permute-start(bf16[128,512]{1,0:T(8,128)(2,1)S(1)} %get-tuple-element.69), channel_id=1, source_target_pairs={{0,20},{4,16},{8,28},{12,24},{16,4},{20,0},{24,12},{28,8},{1,21},{... | collective-permute-start | bytes 393224 | tf_op jit(solution)/shard_map/ppermute | solution.py:27
  60.7 16.2 %collective-permute-start.14 = (bf16[256,1024]{1,0:T(8,128)(2,1)S(1)}, bf16[256,1024]{1,0:T(8,128)(2,1)S(1)}, u32[]{:S(2)}, u32[]{:S(2)}) collective-permute-start(bf16[256,1024]{1,0:T(8,128)(2,1)S(1)} %get-tuple-element.46), channel_id=1, source_target_pairs={{0,4},{4,0},{8,12},{12,8},{16,20},{20,16},{24,28},{28,24},{1,5},{5... | collective-permute-start | bytes 1572872 | tf_op jit(solution)/shard_map/ppermute | solution.py:27
  62.1 5.0 %collective-permute-start.19 = (bf16[128,512]{1,0:T(8,128)(2,1)S(1)}, bf16[128,512]{1,0:T(8,128)(2,1)S(1)}, u32[]{:S(2)}, u32[]{:S(2)}) collective-permute-start(bf16[128,512]{1,0:T(8,128)(2,1)S(1)} %get-tuple-element.55), channel_id=1, source_target_pairs={{0,8},{4,12},{8,0},{12,4},{16,24},{20,28},{24,16},{28,20},{1,9},{5... | collective-permute-start | bytes 393224 | tf_op jit(solution)/shard_map/ppermute | solution.py:27
  63.5 4.8 %collective-permute-start.22 = (bf16[128,512]{1,0:T(8,128)(2,1)S(1)}, bf16[128,512]{1,0:T(8,128)(2,1)S(1)}, u32[]{:S(2)}, u32[]{:S(2)}) collective-permute-start(bf16[128,512]{1,0:T(8,128)(2,1)S(1)} %get-tuple-element.58), channel_id=1, source_target_pairs={{0,4},{4,0},{8,12},{12,8},{16,20},{20,16},{24,28},{28,24},{1,5},{5... | collective-permute-start | bytes 393224 | tf_op jit(solution)/shard_map/ppermute | solution.py:27
  63.5 5.3 %collective-permute-start.25 = (bf16[128,512]{1,0:T(8,128)(2,1)S(1)}, bf16[128,512]{1,0:T(8,128)(2,1)S(1)}, u32[]{:S(2)}, u32[]{:S(2)}) collective-permute-start(bf16[128,512]{1,0:T(8,128)(2,1)S(1)} %get-tuple-element.61), channel_id=1, source_target_pairs={{0,20},{4,16},{8,28},{12,24},{16,4},{20,0},{24,12},{28,8},{1,21},{... | collective-permute-start | bytes 393224 | tf_op jit(solution)/shard_map/ppermute | solution.py:27
  65.3 5.1 %collective-permute-start.31 = (bf16[128,512]{1,0:T(8,128)(2,1)S(1)}, bf16[128,512]{1,0:T(8,128)(2,1)S(1)}, u32[]{:S(2)}, u32[]{:S(2)}) collective-permute-start(bf16[128,512]{1,0:T(8,128)(2,1)S(1)} %add_convert_fusion), channel_id=1, source_target_pairs={{0,12},{4,8},{8,4},{12,0},{16,28},{20,24},{24,20},{28,16},{1,13},{... | collective-permute-start | bytes 393224 | tf_op jit(solution)/shard_map/ppermute | solution.py:27
  67.1 5.2 %collective-permute-start.28 = (bf16[128,512]{1,0:T(8,128)(2,1)S(1)}, bf16[128,512]{1,0:T(8,128)(2,1)S(1)}, u32[]{:S(2)}, u32[]{:S(2)}) collective-permute-start(bf16[128,512]{1,0:T(8,128)(2,1)S(1)} %add_convert_fusion.1), channel_id=1, source_target_pairs={{0,16},{4,20},{8,24},{12,28},{16,0},{20,4},{24,8},{28,12},{1,17},{... | collective-permute-start | bytes 393224 | tf_op jit(solution)/shard_map/ppermute | solution.py:27
  68.3 5.8 %collective-permute-start.24 = (bf16[128,512]{1,0:T(8,128)(2,1)S(1)}, bf16[128,512]{1,0:T(8,128)(2,1)S(1)}, u32[]{:S(2)}, u32[]{:S(2)}) collective-permute-start(bf16[128,512]{1,0:T(8,128)(2,1)S(1)} %add_convert_fusion.2), channel_id=1, source_target_pairs={{0,12},{4,8},{8,4},{12,0},{16,28},{20,24},{24,20},{28,16},{1,13},{... | collective-permute-start | bytes 393224 | tf_op jit(solution)/shard_map/ppermute | solution.py:27
  68.8 6.2 %collective-permute-start.21 = (bf16[128,512]{1,0:T(8,128)(2,1)S(1)}, bf16[128,512]{1,0:T(8,128)(2,1)S(1)}, u32[]{:S(2)}, u32[]{:S(2)}) collective-permute-start(bf16[128,512]{1,0:T(8,128)(2,1)S(1)} %add_convert_fusion.3), channel_id=1, source_target_pairs={{0,16},{4,20},{8,24},{12,28},{16,0},{20,4},{24,8},{28,12},{1,17},{... | collective-permute-start | bytes 393224 | tf_op jit(solution)/shard_map/ppermute | solution.py:27
  70.3 6.6 %collective-permute-start.16 = (bf16[256,256]{1,0:T(8,128)(2,1)S(1)}, bf16[256,256]{1,0:T(8,128)(2,1)S(1)}, u32[]{:S(2)}, u32[]{:S(2)}) collective-permute-start(bf16[256,256]{1,0:T(8,128)(2,1)S(1)} %slice.29), channel_id=1, source_target_pairs={{0,4},{4,0},{8,12},{12,8},{16,20},{20,16},{24,28},{28,24},{1,5},{5... | collective-permute-start | bytes 393224 | tf_op jit(solution)/shard_map/ppermute | solution.py:27
  72.3 4.6 %collective-permute-start.18 = (bf16[256,256]{1,0:T(8,128)(2,1)S(1)}, bf16[256,256]{1,0:T(8,128)(2,1)S(1)}, u32[]{:S(2)}, u32[]{:S(2)}) collective-permute-start(bf16[256,256]{1,0:T(8,128)(2,1)S(1)} %slice.31), channel_id=1, source_target_pairs={{0,4},{4,0},{8,12},{12,8},{16,20},{20,16},{24,28},{28,24},{1,5},{5... | collective-permute-start | bytes 393224 | tf_op jit(solution)/shard_map/ppermute | solution.py:27
  74.1 2.8 %collective-permute-start.15 = (bf16[256,256]{1,0:T(8,128)(2,1)S(1)}, bf16[256,256]{1,0:T(8,128)(2,1)S(1)}, u32[]{:S(2)}, u32[]{:S(2)}) collective-permute-start(bf16[256,256]{1,0:T(8,128)(2,1)S(1)} %slice.28), channel_id=1, source_target_pairs={{0,4},{4,0},{8,12},{12,8},{16,20},{20,16},{24,28},{28,24},{1,5},{5... | collective-permute-start | bytes 393224 | tf_op jit(solution)/shard_map/ppermute | solution.py:27
  75.1 1.8 %collective-permute-start.17 = (bf16[256,256]{1,0:T(8,128)(2,1)S(1)}, bf16[256,256]{1,0:T(8,128)(2,1)S(1)}, u32[]{:S(2)}, u32[]{:S(2)}) collective-permute-start(bf16[256,256]{1,0:T(8,128)(2,1)S(1)} %slice.30), channel_id=1, source_target_pairs={{0,4},{4,0},{8,12},{12,8},{16,20},{20,16},{24,28},{28,24},{1,5},{5... | collective-permute-start | bytes 393224 | tf_op jit(solution)/shard_map/ppermute | solution.py:27

commit v2 on v1

--- a/solution.py
+++ b/solution.py
@@ -14,6 +14,7 @@
 HL = H // 2
 SCALE = DH**-0.5
 EPS = 1e-05
+LOG2E = 1.4426950408889634
 BF = jnp.bfloat16
 F32 = jnp.float32
 GROUPS = ((0, 1), (2, 3))
@@ -43,7 +44,7 @@
         in_specs=[SMEM] + [VMEM] * (len(args) - 1),
         out_specs=jax.tree.map(lambda _: VMEM, out_shape),
         scratch_shapes=list(scratch),
-        compiler_params=pltpu.CompilerParams(vmem_limit_bytes=48 << 20),
+        compiler_params=pltpu.CompilerParams(vmem_limit_bytes=20 << 20),
     )(*args)
 
 
@@ -72,72 +73,90 @@
     xt[:, seq_len:] = xp[...].T
 
 
-def pre_part(me, blocks, xo, xp, piece_refs, block, pre, add):
-    rows = piece_refs[0].shape[0]
-    seq_len = xo.shape[0]
-    done = 0
-    for masks in blocks:
-        fill_block(me, masks, piece_refs[done : done + len(masks)], block)
-        done += len(masks)
-        cols = ds(block_start(me, masks, rows), len(masks) * rows, len(masks) * rows)
-        for s, x in ((0, xo), (1, xp)):
-            own = pl.ds(s * seq_len, seq_len)
-            part = dot(x[:, cols], block[...], 1, 0)
-            pre[own, :] = (pre[own, :] + part) if add else part
-        add = True
-
-
 def pre_kernel(blocks, has_prev, sc, xo, xp, *refs):
     me = sc[0]
     if has_prev:
         prev, refs = refs[0], refs[1:]
     *pieces, pre, block = refs
-    if has_prev:
-        pre[...] = prev[...]
-    pre_part(me, blocks, xo, xp, pieces, block, pre, has_prev)
-
-
-def forward_kernel(blocks, sc, xo, xp, prev, vo, vp, go, gp, co, cp, *refs):
-    *pieces, act, slope, prob, dprob, mixed, stats, pre, block = refs
+    rows = pieces[0].shape[0]
+    seq_len = xo.shape[0]
+    for i, masks in enumerate(blocks):
+        per = len(masks)
+        fill_block(me, masks, pieces[i * per : (i + 1) * per], block)
+        cols = ds(block_start(me, masks, rows), per * rows, per * rows)
+        for s, x in ((0, xo), (1, xp)):
+            own = pl.ds(s * seq_len, seq_len)
+            part = dot(x[:, cols], block[...], 1, 0)
+            if i > 0:
+                part = part + pre[own, :]
+            elif has_prev:
+                part = part + prev[own, :]
+            pre[own, :] = part
+
+
+def gate(raw, scale):
+    sig = pltpu.reciprocal(1.0 + jnp.exp2(raw * (-scale * LOG2E)), approx=True)
+    out = raw * sig
+    return out, sig + (out * scale if scale != 1.0 else out) * (1.0 - sig)
+
+
+def product_kernel(sc, go, gp, co, cp, prod):
+    core = lax.rem(sc[0], 2)
+    seq_len = co.shape[0]
+    prod[:seq_len, :] = go[:, ds(core * HALF, HALF, HALF)].astype(F32) * co[...].astype(F32)
+    prod[seq_len:, :] = gp[...].astype(F32) * cp[...].astype(F32)
+
+
+def forward_kernel(masks, sc, xo, xp, prev, vo, vp, prod, *refs):
+    *pieces, act, slope, prob, dprob, mixed, stats, block = refs
     me = sc[0]
     core = lax.rem(me, 2)
     seq_len = xo.shape[0]
-    pre[...] = prev[...]
-    pre_part(me, blocks, xo, xp, pieces, block, pre, True)
-    row_ids = lax.broadcasted_iota(jnp.int32, (seq_len, seq_len), 0)
-    col_ids = lax.broadcasted_iota(jnp.int32, (seq_len, seq_len), 1)
+    top = seq_len // 2
+    fill_block(me, masks, pieces, block)
+    rows = pieces[0].shape[0]
+    cols = ds(block_start(me, masks, rows), len(masks) * rows, len(masks) * rows)
+    for s, x in ((0, xo), (1, xp)):
+        own = pl.ds(s * seq_len, seq_len)
+        a, d = gate(prev[own, :] + dot(x[:, cols], block[...], 1, 0), 1.0)
+        act[own, :] = a.astype(BF)
+        slope[own, :] = d
+    causal = lax.broadcasted_iota(jnp.int32, (top, top), 1) <= lax.broadcasted_iota(jnp.int32, (top, top), 0)
+    none = jnp.zeros((top, top), BF)
+    units = [(s, h) for s in range(2) for h in range(HL)]
+    raws = []
+    for s, h in units:
+        own = pl.ds(s * seq_len, seq_len)
+        raws.append(dot(act[own, pl.ds(h * DH, DH)], act[own, pl.ds(HALF + h * DH, DH)], 1, 1))
+    probs = []
+    for (s, h), raw in zip(units, raws):
+        p0, d0 = gate(raw[:top, :top], SCALE)
+        p1, d1 = gate(raw[top:, :], SCALE)
+        p0, d0 = jnp.where(causal, p0, 0.0), jnp.where(causal, d0, 0.0)
+        p2, d2 = jnp.where(causal, p1[:, top:], 0.0), jnp.where(causal, d1[:, top:], 0.0)
+        whole = []
+        for upper, left, right in ((p0, p1, p2), (d0, d1, d2)):
+            whole.append(
+                jnp.concatenate(
+                    [
+                        jnp.concatenate([upper.astype(BF), none], 1),
+                        jnp.concatenate([left[:, :top].astype(BF), right.astype(BF)], 1),
+                    ],
+                    0,
+                )
+            )
+        probs.append(whole[0])
+        prob[s * HL + h] = whole[0]
+        dprob[s * HL + h] = whole[1]
+    for (s, h), p in zip(units, probs):
+        if s == 0:
+            val = vo[:, ds(core * HALF + h * DH, DH, DH)]
+        else:
+            val = vp[:, pl.ds(h * DH, DH)]
+        mixed[pl.ds(s * seq_len, seq_len), pl.ds(h * DH, DH)] = dot(p, val, 1, 0)
     for s in range(2):
-        length = sc[1 + s]
         own = pl.ds(s * seq_len, seq_len)
-        valid = (col_ids <= row_ids) & (row_ids < length)
-        for h in range(HL):
-            qk = []
-            for side in range(2):
-                at = pl.ds(side * HALF + h * DH, DH)
-                v = pre[own, at]
-                sig = 1.0 / (1.0 + jnp.exp(-v))
-                a = (v * sig).astype(BF)
-                act[own, at] = a
-                slope[own, at] = sig * (1.0 + v * (1.0 - sig))
-                qk.append(a)
-            score = dot(qk[0], qk[1], 1, 1) * SCALE
-            sig = 1.0 / (1.0 + jnp.exp(-score))
-            p = jnp.where(valid, score * sig, 0.0).astype(BF)
-            prob[s * HL + h] = p
-            dprob[s * HL + h] = jnp.where(valid, sig * (1.0 + score * (1.0 - sig)) * SCALE, 0.0).astype(BF)
-            if s == 0:
-                val = vo[:, ds(core * HALF + h * DH, DH, DH)]
-            else:
-                val = vp[:, pl.ds(h * DH, DH)]
-            mixed[own, pl.ds(h * DH, DH)] = dot(p, val, 1, 0)
-        live = lax.broadcasted_iota(jnp.int32, (seq_len, 1), 0) < length
-        if s == 0:
-            gate = go[:, ds(core * HALF, HALF, HALF)]
-            cot = co[...]
-        else:
-            gate = gp[...]
-            cot = cp[...]
-        grad = jnp.where(live, gate.astype(F32) * cot.astype(F32), 0.0)
+        grad = prod[own, :]
         m = mixed[own, :]
         total = jnp.sum(m, axis=1, keepdims=True)
         off = m - total * (1.0 / HALF)
@@ -154,49 +173,46 @@
         stats[:, own] = packed.T[:8, :]
 
 
-def backward_kernel(heads, nmask, sc, xt, act, slope, prob, dprob, mixed, mine, theirs, vo, vp, go, gp, co, cp, *refs):
+def backward_kernel(heads, nmask, sc, xt, act, slope, prob, dprob, mixed, mine, theirs, vo, vp, prod, co, cp, *refs):
     *terms, gpre, gval, ggate, whole = refs
     me = sc[0]
     core = lax.rem(me, 2)
     seq_len = vo.shape[0]
     width = len(heads) * DH
+    units = []
     for s in range(2):
-        length = sc[1 + s]
         own = pl.ds(s * seq_len, seq_len)
         other = pl.ds((1 - s) * seq_len, seq_len)
-        mt = mine[:, own].T
-        tt = theirs[:, other].T
-        mean = (mt[:, 0:1] + tt[:, 0:1]) * (1.0 / F)
-        mean_m = mt[:, 0:1] * (1.0 / HALF)
-        mean_t = tt[:, 0:1] * (1.0 / HALF)
-        gap = mean_m - mean_t
-        variance = (mt[:, 1:2] + tt[:, 1:2] + gap * gap * (HALF * 0.5)) * (1.0 / F)
-        rstd = lax.rsqrt(variance + EPS)
-        c1 = (mt[:, 2:3] + tt[:, 2:3]) * (1.0 / F)
-        cross = mt[:, 3:4] + tt[:, 3:4] + (mean_m - mean) * mt[:, 2:3] + (mean_t - mean) * tt[:, 2:3]
-        c2 = cross * rstd * (1.0 / F)
-        live = lax.broadcasted_iota(jnp.int32, (seq_len, 1), 0) < length
+        a, b = mine[:, own], theirs[:, other]
+        mean = (a[0:1] + b[0:1]) * (1.0 / F)
+        mean_a, mean_b = a[0:1] * (1.0 / HALF), b[0:1] * (1.0 / HALF)
+        gap = mean_a - mean_b
+        variance = (a[1:2] + b[1:2] + gap * gap * (HALF * 0.5)) * (1.0 / F)
+        live = lax.broadcasted_iota(jnp.int32, (1, seq_len), 1) < sc[1 + s]
+        rate = jnp.where(live, SCALE * lax.rsqrt(variance * (SCALE * SCALE) + EPS), 0.0)
+        c1 = (a[2:3] + b[2:3]) * (1.0 / F)
+        cross = a[3:4] + b[3:4] + (mean_a - mean) * a[2:3] + (mean_b - mean) * b[2:3]
+        c2 = cross * rate * (1.0 / F)
+        cols = jnp.concatenate([mean, rate, c1, c2, mean, rate, c1, c2], 0).T
+        mean, rate, c1, c2 = (cols[:, i : i + 1] for i in range(4))
         for i, h in enumerate(heads):
             local = pl.ds(h * DH, DH)
-            at = pl.ds(i * DH, DH)
             if s == 0:
-                far = ds(core * HALF + h * DH, DH, DH)
-                val, gate, cot = vo[:, far], go[:, far], co[:, local]
+                val, cot = vo[:, ds(core * HALF + h * DH, DH, DH)], co[:, local]
             else:
-                val, gate, cot = vp[:, local], gp[:, local], cp[:, local]
-            cot = cot.astype(F32)
-            grad = jnp.where(live, gate.astype(F32) * cot, 0.0)
-            normed = (mixed[own, local] - mean) * rstd
-            ggate[own, at] = jnp.where(live, normed * cot, 0.0).astype(BF)
-            dmix = (rstd * (grad - c1 - normed * c2)).astype(BF)
-            q, k = act[own, local], act[own, pl.ds(HALF + h * DH, DH)]
-            gval[own, at] = dot(prob[s * HL + h], dmix, 0, 0).astype(BF)
-            datt = dot(dmix, val, 1, 1)
-            dscore = (datt * dprob[s * HL + h].astype(F32)).astype(BF)
-            dq = dot(dscore, k, 1, 0)
-            dk = dot(dscore, q, 0, 0)
-            gpre[own, at] = (dq * slope[own, local]).astype(BF)
-            gpre[own, pl.ds(width + i * DH, DH)] = (dk * slope[own, pl.ds(HALF + h * DH, DH)]).astype(BF)
+                val, cot = vp[:, local], cp[:, local]
+            normed = (mixed[own, local] - mean) * rate
+            ggate[own, pl.ds(i * DH, DH)] = (normed * cot.astype(F32)).astype(BF)
+            dmix = (rate * (prod[own, local] - c1 - normed * c2)).astype(BF)
+            units.append((own, i, h, s * HL + h, val, dmix))
+    dscores = [dot(dmix, val, 1, 1).astype(BF) * dprob[u] for _, _, _, u, val, dmix in units]
+    for (own, i, h, u, _, dmix), dscore in zip(units, dscores):
+        gval[own, pl.ds(i * DH, DH)] = dot(prob[u], dmix, 0, 0).astype(BF)
+        q_at, k_at = pl.ds(h * DH, DH), pl.ds(HALF + h * DH, DH)
+        dq = dot(dscore, act[own, k_at], 1, 0)
+        dk = dot(dscore, act[own, q_at], 0, 0)
+        gpre[own, pl.ds(i * DH, DH)] = (dq * slope[own, q_at]).astype(BF)
+        gpre[own, pl.ds(width + i * DH, DH)] = (dk * slope[own, k_at]).astype(BF)
     whole[...] = dot(xt[...], gpre[...], 1, 0).astype(BF)
     rows = terms[0].shape[0]
     for m in range(nmask):
@@ -318,8 +334,9 @@
         *held(blocks[1:-1]),
         scratch=[block],
     )
+    prod = call(product_kernel, like((two, HALF), F32), sc, go, gp, co, cp)
     act, slope, prob, dprob, mixed, stats = call(
-        functools.partial(forward_kernel, blocks[-1:]),
+        functools.partial(forward_kernel, blocks[-1]),
         [
             like((two, F), BF),
             like((two, F), F32),
@@ -334,12 +351,9 @@
         pre,
         vo,
         vp,
-        go,
-        gp,
-        co,
-        cp,
+        prod,
         *held(blocks[-1:]),
-        scratch=[pltpu.VMEM((two, F), F32), block],
+        scratch=[block],
     )
     theirs = pair(stats, 1)
 
@@ -361,8 +375,7 @@
             theirs,
             vo,
             vp,
-            go,
-            gp,
+            prod,
             co,
             cp,
             scratch=[pltpu.VMEM((depth, width), BF)],

time: 79 us -> 67.9 us (0.86)
  Pallas kernels: 27.1 us -> 17.6 us
  local copies, waits for them, and re-layouts: 6.15 us -> 2.41 us
  waiting for transfers between devices: 16.5 us -> 19.5 us
    pallas_call x9 -> x10, Pallas kernels: 27.1 us -> 17.6 us  [call(): pl.pallas_call(body, out_shape=out_shape, in_specs=[SMEM] + [VMEM] * (len...]
    ppermute x2, waiting for transfers between devices: 3.52 us -> 8.42 us  [from_next(): lax.ppermute(x, ('dp', 'segment'), [(i * seg + s, (i ^ mask) * seg + (s -...]
    unnamed x14 -> x6, local copies, waits for them, and re-layouts: 3.76 us -> 0.01 us
    ppermute x31, waiting for transfers between devices: 13 us -> 11.1 us  [pair(): return lax.ppermute(x, 'dp', [(i, i ^ mask) for i in range(count)])]
  transfers between devices with their start and end apart: 33 -> 33, of which waited for: 12 -> 15; matrix products, arithmetic and copies ran while one was open for 3% -> 3% of each run, Pallas kernels for 17% -> 15%
where the time goes in v2:
time: 67.9 us; the launch traced here: 67.7 us
  starting transfers between devices  25.8 us (38%)
  waiting for transfers between devices  19.5 us (29%)
  Pallas kernels  17.6 us (26%)
  local copies, waits for them, and re-layouts  2.41 us (4%)
  between operations  1.55 us (2%)
  other arithmetic  0.94 us (1%)
    ppermute x31, starting transfers between devices, pair(): return lax.ppermute(x, 'dp', [(i, i ^ mask) for i in range(count)])  22 us
    pallas_call x10, Pallas kernels, call(): pl.pallas_call(body, out_shape=out_shape, in_specs=[SMEM] + [VMEM] * (len...  17.6 us
    ppermute x31, waiting for transfers between devices, pair(): return lax.ppermute(x, 'dp', [(i, i ^ mask) for i in range(count)])  11.1 us
    ppermute x2, waiting for transfers between devices, from_next(): lax.ppermute(x, ('dp', 'segment'), [(i * seg + s, (i ^ mask) * seg + (s -...  8.42 us
    ppermute x2, starting transfers between devices, from_next(): lax.ppermute(x, ('dp', 'segment'), [(i * seg + s, (i ^ mask) * seg + (s -...  3.77 us
  transfers between devices with their start and end apart: 33, of which 15 were waited for; matrix products, arithmetic and copies ran while one was open for 3% of the time, Pallas kernels for 15%

profile of v2, /device:TPU:0, one launch (start us, length us, event | category | flops | bytes accessed | tf_op | source)
XLA Modules:
  0.0 67.7 jit_solution(15973529429075206614)
XLA Ops:
  0.7 1.2 %fusion = (bf16[128,512]{1,0:T(8,128)(2,1)S(1)}, bf16[128,512]{1,0:T(8,128)(2,1)S(1)}, bf16[128,512]{1,0:T(8,128)(2,1)S(1)}, bf16[128,512]{1,0:T(8,128)(2,1)S(1)}) fusion(bf16[128,2048]{1,0:T(8,128)(2,1)} %bitcast.29), kind=kLoop, calls=%fused_computation.13 | loop fusion | bytes 1048576 | tf_op jit(solution)/shard_map/slice | solution.py:289
  2.0 0.5 collective-permute-start.1
  2.5 2.6 %collective-permute-start.2 = (bf16[128,1024]{1,0:T(8,128)(2,1)S(1)}, bf16[128,1024]{1,0:T(8,128)(2,1)S(1)}, u32[]{:S(2)}, u32[]{:S(2)}) collective-permute-start(bf16[128,1024]{1,0:T(8,128)(2,1)S(1)} %get-tuple-element.73.refs_0_), channel_id=1, source_target_pairs={{0,8},{4,12},{8,0},{12,4},{16,24},{20,28},{24,16},{28,20},{1,9},{5... | collective-permute-start | bytes 786440 | tf_op jit(solution)/shard_map/ppermute | solution.py:28
  5.3 1.5 %collective-permute-start.5 = (bf16[128,1024]{1,0:T(8,128)(2,1)S(1)}, bf16[128,1024]{1,0:T(8,128)(2,1)S(1)}, u32[]{:S(2)}, u32[]{:S(2)}) collective-permute-start(bf16[128,1024]{1,0:T(8,128)(2,1)S(1)} %get-tuple-element.72), channel_id=1, source_target_pairs={{0,20},{4,16},{8,28},{12,24},{16,4},{20,0},{24,12},{28,8},{1,21},{... | collective-permute-start | bytes 786440 | tf_op jit(solution)/shard_map/ppermute | solution.py:28
  6.8 0.2 collective-permute-start
  6.9 1.1 %dynamic-slice_bitcast_fusion = (bf16[256,512]{1,0:T(8,128)(2,1)S(1)}, bf16[256,512]{1,0:T(8,128)(2,1)S(1)}) fusion(bf16[1,1,256,1024]{3,2,1,0:T(8,128)(2,1)} %param.9, s32[]{:T(128)S(6)} %select_n.23, s32[]{:T(128)S(6)} %select_n.24), kind=kLoop, calls=%fused_computation.6 | loop fusion | bytes 1048584 | tf_op jit(solution)/shard_map/dynamic_slice | solution.py:287
  8.0 3.7 %collective-permute-start.11 = (bf16[256,512]{1,0:T(8,128)(2,1)S(1)}, bf16[256,512]{1,0:T(8,128)(2,1)S(1)}, u32[]{:S(2)}, u32[]{:S(2)}) collective-permute-start(bf16[256,512]{1,0:T(8,128)(2,1)S(1)} %get-tuple-element.71), channel_id=1, source_target_pairs={{0,3},{1,0},{2,1},{3,2},{4,7},{5,4},{6,5},{7,6},{8,11},{9,8},{10,9... | collective-permute-start | bytes 786440 | tf_op jit(solution)/shard_map/ppermute | solution.py:33
  11.8 0.2 collective-permute-done.2.refs_1_.refs_2_
  12.0 0.2 collective-permute-start.10
  12.3 1.2 %collective-permute-done.5.refs_4_.refs_5_ = bf16[128,1024]{1,0:T(8,128)(2,1)S(1)} collective-permute-done((bf16[128,1024]{1,0:T(8,128)(2,1)S(1)}, bf16[128,1024]{1,0:T(8,128)(2,1)S(1)}, u32[]{:S(2)}, u32[]{:S(2)}) %collective-permute-start.5) | collective-permute-done | bytes 262176 | tf_op jit(solution)/shard_map/ppermute | solution.py:28
  13.4 1.5 %collective-permute-start.4 = (bf16[128,1024]{1,0:T(8,128)(2,1)S(1)}, bf16[128,1024]{1,0:T(8,128)(2,1)S(1)}, u32[]{:S(2)}, u32[]{:S(2)}) collective-permute-start(bf16[128,1024]{1,0:T(8,128)(2,1)S(1)} %get-tuple-element.73.refs_0_), channel_id=1, source_target_pairs={{0,16},{4,20},{8,24},{12,28},{16,0},{20,4},{24,8},{28,12},{1,17},{... | collective-permute-start | bytes 786440 | tf_op jit(solution)/shard_map/ppermute | solution.py:28
  15.0 3.4 %collective-permute-done.11.co = bf16[256,512]{1,0:T(8,128)(2,1)S(1)} collective-permute-done((bf16[256,512]{1,0:T(8,128)(2,1)S(1)}, bf16[256,512]{1,0:T(8,128)(2,1)S(1)}, u32[]{:S(2)}, u32[]{:S(2)}) %collective-permute-start.11) | collective-permute-done | bytes 262176 | tf_op jit(solution)/shard_map/ppermute | solution.py:33
  18.3 5.0 %collective-permute-done.12.cp = bf16[256,512]{1,0:T(8,128)(2,1)S(1)} collective-permute-done((bf16[256,512]{1,0:T(8,128)(2,1)S(1)}, bf16[256,512]{1,0:T(8,128)(2,1)S(1)}, u32[]{:S(2)}, u32[]{:S(2)}) %collective-permute-start.12) | collective-permute-done | bytes 262176 | tf_op jit(solution)/shard_map/ppermute | solution.py:33
  23.4 0.5 collective-permute-start.6
  23.9 0.5 collective-permute-start.7
  25.1 0.7 %pad_add_fusion.sc = s32[3]{0:T(128)S(1)} fusion(s32[1]{0:T(128)} %collective-permute-done, s32[1]{0:T(128)} %bitcast.18, s32[1]{0:T(128)} %bitcast), kind=kLoop, calls=%fused_computation.12 | loop fusion | flops 6 | bytes 24 | tf_op jit(solution)/shard_map/concatenate | solution.py:313
  25.8 0.7 shard_map.96.prod
  26.4 1.0 %shard_map.94.refs_0_ = f32[512,1024]{1,0:T(8,128)S(1)} custom-call(s32[3]{0:T(128)S(1)} %pad_add_fusion.sc, bf16[256,1024]{1,0:T(8,128)(2,1)S(1)} %bitcast.20, bf16[256,1024]{1,0:T(8,128)(2,1)S(1)} %collective-permute-done.8.xp, bf16[128,1024]{1,0:T(8,128)(2,1)S(1)} %get-tuple-element.73.refs_0_, bf16[128,1024]{1,0:T(8,128)(2,1)S(1)} %collective-permute-done.1.refs_1_), custom_call_target="tpu_custom_call" | custom-call | tf_op jit(solution)/shard_map/pallas_call | solution.py:41
  27.5 1.4 %shard_map.95.prev = f32[512,1024]{1,0:T(8,128)S(1)} custom-call(s32[3]{0:T(128)S(1)} %pad_add_fusion.sc, bf16[256,1024]{1,0:T(8,128)(2,1)S(1)} %bitcast.21, bf16[256,1024]{1,0:T(8,128)(2,1)S(1)} %collective-permute-done.8.xp, f32[512,1024]{1,0:T(8,128)S(1)} %shard_map.94.refs_0_, bf16[128,1024]{1,0:T(8,128)(2,1)S(1)} %collective-permute-done.2.refs_1_.refs_2_, ...), custom_call_target="tpu_custom_call" | custom-call | tf_op jit(solution)/shard_map/pallas_call | solution.py:41
  28.9 3.2 %collective-permute-done.6.refs_0_.refs_6_ = bf16[128,1024]{1,0:T(8,128)(2,1)S(1)} collective-permute-done((bf16[128,1024]{1,0:T(8,128)(2,1)S(1)}, bf16[128,1024]{1,0:T(8,128)(2,1)S(1)}, u32[]{:S(2)}, u32[]{:S(2)}) %collective-permute-start.6) | collective-permute-done | bytes 262176 | tf_op jit(solution)/shard_map/ppermute | solution.py:28
  32.1 0.2 collective-permute-done.7.refs_1_.refs_7_
  32.3 3.2 %shard_map.97 = (bf16[512,1024]{1,0:T(8,128)(2,1)S(1)}, f32[512,1024]{1,0:T(8,128)S(1)}, bf16[8,256,256]{2,1,0:T(8,128)(2,1)S(1)}, bf16[8,256,256]{2,1,0:T(8,128...) custom-call(s32[3]{0:T(128)S(1)} %pad_add_fusion.sc, bf16[256,1024]{1,0:T(8,128)(2,1)S(1)} %bitcast.22, ...), custom_call_target="tpu_custom_call" | custom-call | tf_op jit(solution)/shard_map/pallas_call | solution.py:41
  35.6 0.9 %shard_map.93.xt = bf16[1024,512]{1,0:T(8,128)(2,1)S(1)} custom-call(s32[3]{0:T(128)S(1)} %pad_add_fusion.sc, bf16[256,1024]{1,0:T(8,128)(2,1)S(1)} %bitcast.23, bf16[256,1024]{1,0:T(8,128)(2,1)S(1)} %collective-permute-done.8.xp), custom_call_target="tpu_custom_call" | custom-call | tf_op jit(solution)/shard_map/pallas_call | solution.py:41
  36.4 0.3 collective-permute-done.13.theirs
  36.7 2.4 %shard_map.99 = (bf16[128,512]{1,0:T(8,128)(2,1)S(1)}, bf16[128,512]{1,0:T(8,128)(2,1)S(1)}, bf16[128,512]{1,0:T(8,128)(2,1)S(1)}, bf16[128,512]{1,0:T(8,128)(2,...) custom-call(s32[3]{0:T(128)S(1)} %pad_add_fusion.sc, ...), custom_call_target="tpu_custom_call" | custom-call | tf_op jit(solution)/shard_map/pallas_call | solution.py:41
  39.2 1.6 %collective-permute-start.30 = (bf16[128,512]{1,0:T(8,128)(2,1)S(1)}, bf16[128,512]{1,0:T(8,128)(2,1)S(1)}, u32[]{:S(2)}, u32[]{:S(2)}) collective-permute-start(bf16[128,512]{1,0:T(8,128)(2,1)S(1)} %get-tuple-element.68), channel_id=1, source_target_pairs={{0,16},{4,20},{8,24},{12,28},{16,0},{20,4},{24,8},{28,12},{1,17},{... | collective-permute-start | bytes 393224 | tf_op jit(solution)/shard_map/ppermute | solution.py:28
  40.8 0.5 collective-permute-start.27
  41.3 2.5 %shard_map.98 = (bf16[128,512]{1,0:T(8,128)(2,1)S(1)}, bf16[128,512]{1,0:T(8,128)(2,1)S(1)}, bf16[128,512]{1,0:T(8,128)(2,1)S(1)}, bf16[128,512]{1,0:T(8,128)(2,...) custom-call(s32[3]{0:T(128)S(1)} %pad_add_fusion.sc, ...), custom_call_target="tpu_custom_call" | custom-call | tf_op jit(solution)/shard_map/pallas_call | solution.py:41
  43.8 0.8 %collective-permute-start.23 = (bf16[128,512]{1,0:T(8,128)(2,1)S(1)}, bf16[128,512]{1,0:T(8,128)(2,1)S(1)}, u32[]{:S(2)}, u32[]{:S(2)}) collective-permute-start(bf16[128,512]{1,0:T(8,128)(2,1)S(1)} %get-tuple-element.60), channel_id=1, source_target_pairs={{0,16},{4,20},{8,24},{12,28},{16,0},{20,4},{24,8},{28,12},{1,17},{... | collective-permute-start | bytes 393224 | tf_op jit(solution)/shard_map/ppermute | solution.py:28
  44.6 1.3 %collective-permute-start.20 = (bf16[128,512]{1,0:T(8,128)(2,1)S(1)}, bf16[128,512]{1,0:T(8,128)(2,1)S(1)}, u32[]{:S(2)}, u32[]{:S(2)}) collective-permute-start(bf16[128,512]{1,0:T(8,128)(2,1)S(1)} %get-tuple-element.57), channel_id=1, source_target_pairs={{0,8},{4,12},{8,0},{12,4},{16,24},{20,28},{24,16},{28,20},{1,9},{5... | collective-permute-start | bytes 393224 | tf_op jit(solution)/shard_map/ppermute | solution.py:28
  45.9 0.8 %collective-permute-start.26 = (bf16[128,512]{1,0:T(8,128)(2,1)S(1)}, bf16[128,512]{1,0:T(8,128)(2,1)S(1)}, u32[]{:S(2)}, u32[]{:S(2)}) collective-permute-start(bf16[128,512]{1,0:T(8,128)(2,1)S(1)} %get-tuple-element.63), channel_id=1, source_target_pairs={{0,8},{4,12},{8,0},{12,4},{16,24},{20,28},{24,16},{28,20},{1,9},{5... | collective-permute-start | bytes 393224 | tf_op jit(solution)/shard_map/ppermute | solution.py:28
  46.6 2.0 %shard_map.100 = (f32[256,1024]{1,0:T(8,128)S(1)}, bf16[256,1024]{1,0:T(8,128)(2,1)S(1)}) custom-call(s32[3]{0:T(128)S(1)} %pad_add_fusion.sc, bf16[128,1024]{1,0:T(8,128)(2,1)S(1)} %get-tuple-element.73.refs_0_, bf16[128,1024]{1,0:T(8,128)(2,1)S(1)} %collective-permute-done.1.refs_1_, bf16[128,1024]{1,0:T(8,128)(2,1)S(1)} %collective-permute-done.2.refs_1_.refs_2_, ...), custom_call_target="tpu_custom_call" | custom-call | tf_op jit(solution)/shard_map/pallas_call | solution.py:41
  48.8 1.4 %collective-permute-start.32 = (bf16[128,512]{1,0:T(8,128)(2,1)S(1)}, bf16[128,512]{1,0:T(8,128)(2,1)S(1)}, u32[]{:S(2)}, u32[]{:S(2)}) collective-permute-start(bf16[128,512]{1,0:T(8,128)(2,1)S(1)} %get-tuple-element.69), channel_id=1, source_target_pairs={{0,20},{4,16},{8,28},{12,24},{16,4},{20,0},{24,12},{28,8},{1,21},{... | collective-permute-start | bytes 393224 | tf_op jit(solution)/shard_map/ppermute | solution.py:28
  50.4 0.4 collective-permute-done.20
  50.8 1.3 %collective-permute-start.19 = (bf16[128,512]{1,0:T(8,128)(2,1)S(1)}, bf16[128,512]{1,0:T(8,128)(2,1)S(1)}, u32[]{:S(2)}, u32[]{:S(2)}) collective-permute-start(bf16[128,512]{1,0:T(8,128)(2,1)S(1)} %get-tuple-element.55), channel_id=1, source_target_pairs={{0,8},{4,12},{8,0},{12,4},{16,24},{20,28},{24,16},{28,20},{1,9},{5... | collective-permute-start | bytes 393224 | tf_op jit(solution)/shard_map/ppermute | solution.py:28
  52.2 1.5 %collective-permute-start.25 = (bf16[128,512]{1,0:T(8,128)(2,1)S(1)}, bf16[128,512]{1,0:T(8,128)(2,1)S(1)}, u32[]{:S(2)}, u32[]{:S(2)}) collective-permute-start(bf16[128,512]{1,0:T(8,128)(2,1)S(1)} %get-tuple-element.61), channel_id=1, source_target_pairs={{0,20},{4,16},{8,28},{12,24},{16,4},{20,0},{24,12},{28,8},{1,21},{... | collective-permute-start | bytes 393224 | tf_op jit(solution)/shard_map/ppermute | solution.py:28
  53.7 0.3 collective-permute-done.32.refs_11_
  54.0 1.6 %collective-permute-start.31 = (bf16[128,512]{1,0:T(8,128)(2,1)S(1)}, bf16[128,512]{1,0:T(8,128)(2,1)S(1)}, u32[]{:S(2)}, u32[]{:S(2)}) collective-permute-start(bf16[128,512]{1,0:T(8,128)(2,1)S(1)} %add_convert_fusion), channel_id=1, source_target_pairs={{0,12},{4,8},{8,4},{12,0},{16,28},{20,24},{24,20},{28,16},{1,13},{... | collective-permute-start | bytes 393224 | tf_op jit(solution)/shard_map/ppermute | solution.py:28
  55.6 0.7 %collective-permute-done.19.refs_1_ = bf16[128,512]{1,0:T(8,128)(2,1)S(1)} collective-permute-done((bf16[128,512]{1,0:T(8,128)(2,1)S(1)}, bf16[128,512]{1,0:T(8,128)(2,1)S(1)}, u32[]{:S(2)}, u32[]{:S(2)}) %collective-permute-start.19) | collective-permute-done | bytes 131104 | tf_op jit(solution)/shard_map/ppermute | solution.py:28
  56.3 0.8 %collective-permute-start.28 = (bf16[128,512]{1,0:T(8,128)(2,1)S(1)}, bf16[128,512]{1,0:T(8,128)(2,1)S(1)}, u32[]{:S(2)}, u32[]{:S(2)}) collective-permute-start(bf16[128,512]{1,0:T(8,128)(2,1)S(1)} %add_convert_fusion.1), channel_id=1, source_target_pairs={{0,16},{4,20},{8,24},{12,28},{16,0},{20,4},{24,8},{28,12},{1,17},{... | collective-permute-start | bytes 393224 | tf_op jit(solution)/shard_map/ppermute | solution.py:28
  57.1 0.2 collective-permute-done.25.refs_5_
  57.4 1.5 %collective-permute-start.21 = (bf16[128,512]{1,0:T(8,128)(2,1)S(1)}, bf16[128,512]{1,0:T(8,128)(2,1)S(1)}, u32[]{:S(2)}, u32[]{:S(2)}) collective-permute-start(bf16[128,512]{1,0:T(8,128)(2,1)S(1)} %add_convert_fusion.3), channel_id=1, source_target_pairs={{0,16},{4,20},{8,24},{12,28},{16,0},{20,4},{24,8},{28,12},{1,17},{... | collective-permute-start | bytes 393224 | tf_op jit(solution)/shard_map/ppermute | solution.py:28
  58.9 0.9 %collective-permute-start.16 = (bf16[256,256]{1,0:T(8,128)(2,1)S(1)}, bf16[256,256]{1,0:T(8,128)(2,1)S(1)}, u32[]{:S(2)}, u32[]{:S(2)}) collective-permute-start(bf16[256,256]{1,0:T(8,128)(2,1)S(1)} %slice.29), channel_id=1, source_target_pairs={{0,4},{4,0},{8,12},{12,8},{16,20},{20,16},{24,28},{28,24},{1,5},{5... | collective-permute-start | bytes 393224 | tf_op jit(solution)/shard_map/ppermute | solution.py:28
  59.8 1.5 %collective-permute-done.28.refs_8_ = bf16[128,512]{1,0:T(8,128)(2,1)S(1)} collective-permute-done((bf16[128,512]{1,0:T(8,128)(2,1)S(1)}, bf16[128,512]{1,0:T(8,128)(2,1)S(1)}, u32[]{:S(2)}, u32[]{:S(2)}) %collective-permute-start.28) | collective-permute-done | bytes 131104 | tf_op jit(solution)/shard_map/ppermute | solution.py:28
  61.3 1.5 %collective-permute-done.24.refs_4_ = bf16[128,512]{1,0:T(8,128)(2,1)S(1)} collective-permute-done((bf16[128,512]{1,0:T(8,128)(2,1)S(1)}, bf16[128,512]{1,0:T(8,128)(2,1)S(1)}, u32[]{:S(2)}, u32[]{:S(2)}) %collective-permute-start.24) | collective-permute-done | bytes 131104 | tf_op jit(solution)/shard_map/ppermute | solution.py:28
  62.9 1.2 %collective-permute-done.21.refs_2_ = bf16[128,512]{1,0:T(8,128)(2,1)S(1)} collective-permute-done((bf16[128,512]{1,0:T(8,128)(2,1)S(1)}, bf16[128,512]{1,0:T(8,128)(2,1)S(1)}, u32[]{:S(2)}, u32[]{:S(2)}) %collective-permute-start.21) | collective-permute-done | bytes 131104 | tf_op jit(solution)/shard_map/ppermute | solution.py:28
  64.2 1.7 %shard_map.102 = f32[128,2048]{1,0:T(8,128)} custom-call(s32[3]{0:T(128)S(1)} %pad_add_fusion.sc, bf16[128,512]{1,0:T(8,128)(2,1)S(1)} %get-tuple-element.54.refs_0_, bf16[128,512]{1,0:T(8,128)(2,1)S(1)} %collective-permute-done.19.refs_1_, bf16[128,512]{1,0:T(8,128)(2,1)S(1)} %collective-permute-done.21.refs_2_, ...), custom_call_target="tpu_custom_call" | custom-call | tf_op jit(solution)/shard_map/pallas_call | solution.py:41
  65.9 1.8 %shard_map.101 = (bf16[256,1024]{1,0:T(8,128)(2,1)}, bf16[256,1024]{1,0:T(8,128)(2,1)}, bf16[256,1024]{1,0:T(8,128)(2,1)}) custom-call(s32[3]{0:T(128)S(1)} %pad_add_fusion.sc, f32[256,1024]{1,0:T(8,128)S(1)} %get-tuple-element.45.gi_o, bf16[256,1024]{1,0:T(8,128)(2,1)S(1)} %collective-permute-done.14.gi_r, bf16[512,256]{1,0:T(8,128)(2,1)S(1)} %get-tuple-element.47.v0, ...), custom_call_target="tpu_custom_call" | custom-call | tf_op jit(solution)/shard_map/pallas_call | solution.py:41
  (48 shorter events, 1.1 us)
Async XLA Ops:
  0.6 4.5 %copy-start = (bf16[1,1,256,1024]{3,2,1,0:T(8,128)(2,1)S(1)}, bf16[1,1,256,1024]{3,2,1,0:T(8,128)(2,1)}, u32[]{:S(2)}) copy-start(bf16[1,1,256,1024]{3,2,1,0:T(8,128)(2,1)} %param.6) | copy-start | bytes 1572868
  0.6 6.3 %copy-start.2 = (bf16[1,1,256,1024]{3,2,1,0:T(8,128)(2,1)S(1)}, bf16[1,1,256,1024]{3,2,1,0:T(8,128)(2,1)}, u32[]{:S(2)}) copy-start(bf16[1,1,256,1024]{3,2,1,0:T(8,128)(2,1)} %param.8) | copy-start | bytes 1572868
  0.7 11.6 %copy-start.1 = (bf16[1,1,256,1024]{3,2,1,0:T(8,128)(2,1)S(1)}, bf16[1,1,256,1024]{3,2,1,0:T(8,128)(2,1)}, u32[]{:S(2)}) copy-start(bf16[1,1,256,1024]{3,2,1,0:T(8,128)(2,1)} %param.7) | copy-start | bytes 1572868
  2.0 9.7 %collective-permute-start.1 = (bf16[128,1024]{1,0:T(8,128)(2,1)S(1)}, bf16[128,1024]{1,0:T(8,128)(2,1)S(1)}, u32[]{:S(2)}, u32[]{:S(2)}) collective-permute-start(bf16[128,1024]{1,0:T(8,128)(2,1)S(1)} %get-tuple-element.72), channel_id=1, source_target_pairs={{0,4},{4,0},{8,12},{12,8},{16,20},{20,16},{24,28},{28,24},{1,5},{5... | collective-permute-start | bytes 786440 | tf_op jit(solution)/shard_map/ppermute | solution.py:28
  2.5 9.5 %collective-permute-start.2 = (bf16[128,1024]{1,0:T(8,128)(2,1)S(1)}, bf16[128,1024]{1,0:T(8,128)(2,1)S(1)}, u32[]{:S(2)}, u32[]{:S(2)}) collective-permute-start(bf16[128,1024]{1,0:T(8,128)(2,1)S(1)} %get-tuple-element.73.refs_0_), channel_id=1, source_target_pairs={{0,8},{4,12},{8,0},{12,4},{16,24},{20,28},{24,16},{28,20},{1,9},{5... | collective-permute-start | bytes 786440 | tf_op jit(solution)/shard_map/ppermute | solution.py:28
  5.1 18.8 %collective-permute-start.8 = (bf16[256,1024]{1,0:T(8,128)(2,1)S(1)}, bf16[256,1024]{1,0:T(8,128)(2,1)S(1)}, u32[]{:S(2)}, u32[]{:S(2)}) collective-permute-start(bf16[256,1024]{1,0:T(8,128)(2,1)S(1)} %bitcast.19), channel_id=1, source_target_pairs={{0,4},{4,0},{8,12},{12,8},{16,20},{20,16},{24,28},{28,24},{1,5},{5... | collective-permute-start | bytes 1572872 | tf_op jit(solution)/shard_map/ppermute | solution.py:28
  5.3 8.2 %collective-permute-start.5 = (bf16[128,1024]{1,0:T(8,128)(2,1)S(1)}, bf16[128,1024]{1,0:T(8,128)(2,1)S(1)}, u32[]{:S(2)}, u32[]{:S(2)}) collective-permute-start(bf16[128,1024]{1,0:T(8,128)(2,1)S(1)} %get-tuple-element.72), channel_id=1, source_target_pairs={{0,20},{4,16},{8,28},{12,24},{16,4},{20,0},{24,12},{28,8},{1,21},{... | collective-permute-start | bytes 786440 | tf_op jit(solution)/shard_map/ppermute | solution.py:28
  6.8 1.3 %collective-permute-start = (s32[1]{0:T(128)}, s32[1]{0:T(128)}, u32[]{:S(2)}, u32[]{:S(2)}) collective-permute-start(s32[1]{0:T(128)} %bitcast.1), channel_id=1, source_target_pairs={{0,4},{4,0},{8,12},{12,8},{16,20},{20,16},{24,28},{28,24},{1,5},{5... | collective-permute-start | bytes 20 | tf_op jit(solution)/shard_map/ppermute | solution.py:28
  8.0 10.3 %collective-permute-start.11 = (bf16[256,512]{1,0:T(8,128)(2,1)S(1)}, bf16[256,512]{1,0:T(8,128)(2,1)S(1)}, u32[]{:S(2)}, u32[]{:S(2)}) collective-permute-start(bf16[256,512]{1,0:T(8,128)(2,1)S(1)} %get-tuple-element.71), channel_id=1, source_target_pairs={{0,3},{1,0},{2,1},{3,2},{4,7},{5,4},{6,5},{7,6},{8,11},{9,8},{10,9... | collective-permute-start | bytes 786440 | tf_op jit(solution)/shard_map/ppermute | solution.py:33
  11.7 11.7 %collective-permute-start.12 = (bf16[256,512]{1,0:T(8,128)(2,1)S(1)}, bf16[256,512]{1,0:T(8,128)(2,1)S(1)}, u32[]{:S(2)}, u32[]{:S(2)}) collective-permute-start(bf16[256,512]{1,0:T(8,128)(2,1)S(1)} %get-tuple-element.70), channel_id=1, source_target_pairs={{0,7},{1,4},{2,5},{3,6},{4,3},{5,0},{6,1},{7,2},{8,15},{9,12},{10,... | collective-permute-start | bytes 786440 | tf_op jit(solution)/shard_map/ppermute | solution.py:33
  12.0 11.4 %collective-permute-start.10 = (bf16[256,512]{1,0:T(8,128)(2,1)S(1)}, bf16[256,512]{1,0:T(8,128)(2,1)S(1)}, u32[]{:S(2)}, u32[]{:S(2)}) collective-permute-start(bf16[256,512]{1,0:T(8,128)(2,1)S(1)} %dynamic-slice_bitcast_fusion.2), channel_id=1, source_target_pairs={{0,4},{4,0},{8,12},{12,8},{16,20},{20,16},{24,28},{28,24},{1,5},{5... | collective-permute-start | bytes 786440 | tf_op jit(solution)/shard_map/ppermute | solution.py:28
  13.4 14.0 %collective-permute-start.4 = (bf16[128,1024]{1,0:T(8,128)(2,1)S(1)}, bf16[128,1024]{1,0:T(8,128)(2,1)S(1)}, u32[]{:S(2)}, u32[]{:S(2)}) collective-permute-start(bf16[128,1024]{1,0:T(8,128)(2,1)S(1)} %get-tuple-element.73.refs_0_), channel_id=1, source_target_pairs={{0,16},{4,20},{8,24},{12,28},{16,0},{20,4},{24,8},{28,12},{1,17},{... | collective-permute-start | bytes 786440 | tf_op jit(solution)/shard_map/ppermute | solution.py:28
  18.3 9.2 %collective-permute-start.3 = (bf16[128,1024]{1,0:T(8,128)(2,1)S(1)}, bf16[128,1024]{1,0:T(8,128)(2,1)S(1)}, u32[]{:S(2)}, u32[]{:S(2)}) collective-permute-start(bf16[128,1024]{1,0:T(8,128)(2,1)S(1)} %get-tuple-element.72), channel_id=1, source_target_pairs={{0,12},{4,8},{8,4},{12,0},{16,28},{20,24},{24,20},{28,16},{1,13},{... | collective-permute-start | bytes 786440 | tf_op jit(solution)/shard_map/ppermute | solution.py:28
  23.4 5.6 %collective-permute-start.9 = (bf16[256,512]{1,0:T(8,128)(2,1)S(1)}, bf16[256,512]{1,0:T(8,128)(2,1)S(1)}, u32[]{:S(2)}, u32[]{:S(2)}) collective-permute-start(bf16[256,512]{1,0:T(8,128)(2,1)S(1)} %dynamic-slice_bitcast_fusion.3), channel_id=1, source_target_pairs={{0,4},{4,0},{8,12},{12,8},{16,20},{20,16},{24,28},{28,24},{1,5},{5... | collective-permute-start | bytes 786440 | tf_op jit(solution)/shard_map/ppermute | solution.py:28
  23.4 8.7 %collective-permute-start.6 = (bf16[128,1024]{1,0:T(8,128)(2,1)S(1)}, bf16[128,1024]{1,0:T(8,128)(2,1)S(1)}, u32[]{:S(2)}, u32[]{:S(2)}) collective-permute-start(bf16[128,1024]{1,0:T(8,128)(2,1)S(1)} %collective-permute-done.2.refs_1_.refs_2_), channel_id=1, source_target_pairs={{0,16},{4,20},{8,24},{12,28},{16,0},{20,4},{24,8},{28,12},{1,17},{... | collective-permute-start | bytes 786440 | tf_op jit(solution)/shard_map/ppermute | solution.py:28
  23.9 8.4 %collective-permute-start.7 = (bf16[128,1024]{1,0:T(8,128)(2,1)S(1)}, bf16[128,1024]{1,0:T(8,128)(2,1)S(1)}, u32[]{:S(2)}, u32[]{:S(2)}) collective-permute-start(bf16[128,1024]{1,0:T(8,128)(2,1)S(1)} %collective-permute-done.5.refs_4_.refs_5_), channel_id=1, source_target_pairs={{0,8},{4,12},{8,0},{12,4},{16,24},{20,28},{24,16},{28,20},{1,9},{5... | collective-permute-start | bytes 786440 | tf_op jit(solution)/shard_map/ppermute | solution.py:28
  35.5 1.2 %collective-permute-start.13 = (f32[8,512]{1,0:T(8,128)S(1)}, f32[8,512]{1,0:T(8,128)S(1)}, u32[]{:S(2)}, u32[]{:S(2)}) collective-permute-start(f32[8,512]{1,0:T(8,128)S(1)} %get-tuple-element.42.mine), channel_id=1, source_target_pairs={{0,4},{4,0},{8,12},{12,8},{16,20},{20,16},{24,28},{28,24},{1,5},{5... | collective-permute-start | bytes 49160 | tf_op jit(solution)/shard_map/ppermute | solution.py:28
  39.2 9.4 %collective-permute-start.30 = (bf16[128,512]{1,0:T(8,128)(2,1)S(1)}, bf16[128,512]{1,0:T(8,128)(2,1)S(1)}, u32[]{:S(2)}, u32[]{:S(2)}) collective-permute-start(bf16[128,512]{1,0:T(8,128)(2,1)S(1)} %get-tuple-element.68), channel_id=1, source_target_pairs={{0,16},{4,20},{8,24},{12,28},{16,0},{20,4},{24,8},{28,12},{1,17},{... | collective-permute-start | bytes 393224 | tf_op jit(solution)/shard_map/ppermute | solution.py:28
  40.8 8.0 %collective-permute-start.27 = (bf16[128,512]{1,0:T(8,128)(2,1)S(1)}, bf16[128,512]{1,0:T(8,128)(2,1)S(1)}, u32[]{:S(2)}, u32[]{:S(2)}) collective-permute-start(bf16[128,512]{1,0:T(8,128)(2,1)S(1)} %get-tuple-element.65), channel_id=1, source_target_pairs={{0,8},{4,12},{8,0},{12,4},{16,24},{20,28},{24,16},{28,20},{1,9},{5... | collective-permute-start | bytes 393224 | tf_op jit(solution)/shard_map/ppermute | solution.py:28
  43.8 6.5 %collective-permute-start.23 = (bf16[128,512]{1,0:T(8,128)(2,1)S(1)}, bf16[128,512]{1,0:T(8,128)(2,1)S(1)}, u32[]{:S(2)}, u32[]{:S(2)}) collective-permute-start(bf16[128,512]{1,0:T(8,128)(2,1)S(1)} %get-tuple-element.60), channel_id=1, source_target_pairs={{0,16},{4,20},{8,24},{12,28},{16,0},{20,4},{24,8},{28,12},{1,17},{... | collective-permute-start | bytes 393224 | tf_op jit(solution)/shard_map/ppermute | solution.py:28
  44.6 6.2 %collective-permute-start.20 = (bf16[128,512]{1,0:T(8,128)(2,1)S(1)}, bf16[128,512]{1,0:T(8,128)(2,1)S(1)}, u32[]{:S(2)}, u32[]{:S(2)}) collective-permute-start(bf16[128,512]{1,0:T(8,128)(2,1)S(1)} %get-tuple-element.57), channel_id=1, source_target_pairs={{0,8},{4,12},{8,0},{12,4},{16,24},{20,28},{24,16},{28,20},{1,9},{5... | collective-permute-start | bytes 393224 | tf_op jit(solution)/shard_map/ppermute | solution.py:28
  45.9 6.3 %collective-permute-start.26 = (bf16[128,512]{1,0:T(8,128)(2,1)S(1)}, bf16[128,512]{1,0:T(8,128)(2,1)S(1)}, u32[]{:S(2)}, u32[]{:S(2)}) collective-permute-start(bf16[128,512]{1,0:T(8,128)(2,1)S(1)} %get-tuple-element.63), channel_id=1, source_target_pairs={{0,8},{4,12},{8,0},{12,4},{16,24},{20,28},{24,16},{28,20},{1,9},{5... | collective-permute-start | bytes 393224 | tf_op jit(solution)/shard_map/ppermute | solution.py:28
  48.6 3.5 %collective-permute-start.29 = (bf16[128,512]{1,0:T(8,128)(2,1)S(1)}, bf16[128,512]{1,0:T(8,128)(2,1)S(1)}, u32[]{:S(2)}, u32[]{:S(2)}) collective-permute-start(bf16[128,512]{1,0:T(8,128)(2,1)S(1)} %get-tuple-element.66), channel_id=1, source_target_pairs={{0,4},{4,0},{8,12},{12,8},{16,20},{20,16},{24,28},{28,24},{1,5},{5... | collective-permute-start | bytes 393224 | tf_op jit(solution)/shard_map/ppermute | solution.py:28
  48.8 5.2 %collective-permute-start.32 = (bf16[128,512]{1,0:T(8,128)(2,1)S(1)}, bf16[128,512]{1,0:T(8,128)(2,1)S(1)}, u32[]{:S(2)}, u32[]{:S(2)}) collective-permute-start(bf16[128,512]{1,0:T(8,128)(2,1)S(1)} %get-tuple-element.69), channel_id=1, source_target_pairs={{0,20},{4,16},{8,28},{12,24},{16,4},{20,0},{24,12},{28,8},{1,21},{... | collective-permute-start | bytes 393224 | tf_op jit(solution)/shard_map/ppermute | solution.py:28
  50.2 15.7 %collective-permute-start.14 = (bf16[256,1024]{1,0:T(8,128)(2,1)S(1)}, bf16[256,1024]{1,0:T(8,128)(2,1)S(1)}, u32[]{:S(2)}, u32[]{:S(2)}) collective-permute-start(bf16[256,1024]{1,0:T(8,128)(2,1)S(1)} %get-tuple-element.46), channel_id=1, source_target_pairs={{0,4},{4,0},{8,12},{12,8},{16,20},{20,16},{24,28},{28,24},{1,5},{5... | collective-permute-start | bytes 1572872 | tf_op jit(solution)/shard_map/ppermute | solution.py:28
  50.8 5.6 %collective-permute-start.19 = (bf16[128,512]{1,0:T(8,128)(2,1)S(1)}, bf16[128,512]{1,0:T(8,128)(2,1)S(1)}, u32[]{:S(2)}, u32[]{:S(2)}) collective-permute-start(bf16[128,512]{1,0:T(8,128)(2,1)S(1)} %get-tuple-element.55), channel_id=1, source_target_pairs={{0,8},{4,12},{8,0},{12,4},{16,24},{20,28},{24,16},{28,20},{1,9},{5... | collective-permute-start | bytes 393224 | tf_op jit(solution)/shard_map/ppermute | solution.py:28
  52.2 5.0 %collective-permute-start.22 = (bf16[128,512]{1,0:T(8,128)(2,1)S(1)}, bf16[128,512]{1,0:T(8,128)(2,1)S(1)}, u32[]{:S(2)}, u32[]{:S(2)}) collective-permute-start(bf16[128,512]{1,0:T(8,128)(2,1)S(1)} %get-tuple-element.58), channel_id=1, source_target_pairs={{0,4},{4,0},{8,12},{12,8},{16,20},{20,16},{24,28},{28,24},{1,5},{5... | collective-permute-start | bytes 393224 | tf_op jit(solution)/shard_map/ppermute | solution.py:28
  52.2 5.2 %collective-permute-start.25 = (bf16[128,512]{1,0:T(8,128)(2,1)S(1)}, bf16[128,512]{1,0:T(8,128)(2,1)S(1)}, u32[]{:S(2)}, u32[]{:S(2)}) collective-permute-start(bf16[128,512]{1,0:T(8,128)(2,1)S(1)} %get-tuple-element.61), channel_id=1, source_target_pairs={{0,20},{4,16},{8,28},{12,24},{16,4},{20,0},{24,12},{28,8},{1,21},{... | collective-permute-start | bytes 393224 | tf_op jit(solution)/shard_map/ppermute | solution.py:28
  54.0 4.9 %collective-permute-start.31 = (bf16[128,512]{1,0:T(8,128)(2,1)S(1)}, bf16[128,512]{1,0:T(8,128)(2,1)S(1)}, u32[]{:S(2)}, u32[]{:S(2)}) collective-permute-start(bf16[128,512]{1,0:T(8,128)(2,1)S(1)} %add_convert_fusion), channel_id=1, source_target_pairs={{0,12},{4,8},{8,4},{12,0},{16,28},{20,24},{24,20},{28,16},{1,13},{... | collective-permute-start | bytes 393224 | tf_op jit(solution)/shard_map/ppermute | solution.py:28
  56.3 5.0 %collective-permute-start.28 = (bf16[128,512]{1,0:T(8,128)(2,1)S(1)}, bf16[128,512]{1,0:T(8,128)(2,1)S(1)}, u32[]{:S(2)}, u32[]{:S(2)}) collective-permute-start(bf16[128,512]{1,0:T(8,128)(2,1)S(1)} %add_convert_fusion.1), channel_id=1, source_target_pairs={{0,16},{4,20},{8,24},{12,28},{16,0},{20,4},{24,8},{28,12},{1,17},{... | collective-permute-start | bytes 393224 | tf_op jit(solution)/shard_map/ppermute | solution.py:28
  57.1 5.7 %collective-permute-start.24 = (bf16[128,512]{1,0:T(8,128)(2,1)S(1)}, bf16[128,512]{1,0:T(8,128)(2,1)S(1)}, u32[]{:S(2)}, u32[]{:S(2)}) collective-permute-start(bf16[128,512]{1,0:T(8,128)(2,1)S(1)} %add_convert_fusion.2), channel_id=1, source_target_pairs={{0,12},{4,8},{8,4},{12,0},{16,28},{20,24},{24,20},{28,16},{1,13},{... | collective-permute-start | bytes 393224 | tf_op jit(solution)/shard_map/ppermute | solution.py:28
  57.4 6.8 %collective-permute-start.21 = (bf16[128,512]{1,0:T(8,128)(2,1)S(1)}, bf16[128,512]{1,0:T(8,128)(2,1)S(1)}, u32[]{:S(2)}, u32[]{:S(2)}) collective-permute-start(bf16[128,512]{1,0:T(8,128)(2,1)S(1)} %add_convert_fusion.3), channel_id=1, source_target_pairs={{0,16},{4,20},{8,24},{12,28},{16,0},{20,4},{24,8},{28,12},{1,17},{... | collective-permute-start | bytes 393224 | tf_op jit(solution)/shard_map/ppermute | solution.py:28
  58.9 7.0 %collective-permute-start.16 = (bf16[256,256]{1,0:T(8,128)(2,1)S(1)}, bf16[256,256]{1,0:T(8,128)(2,1)S(1)}, u32[]{:S(2)}, u32[]{:S(2)}) collective-permute-start(bf16[256,256]{1,0:T(8,128)(2,1)S(1)} %slice.29), channel_id=1, source_target_pairs={{0,4},{4,0},{8,12},{12,8},{16,20},{20,16},{24,28},{28,24},{1,5},{5... | collective-permute-start | bytes 393224 | tf_op jit(solution)/shard_map/ppermute | solution.py:28
  61.3 4.6 %collective-permute-start.18 = (bf16[256,256]{1,0:T(8,128)(2,1)S(1)}, bf16[256,256]{1,0:T(8,128)(2,1)S(1)}, u32[]{:S(2)}, u32[]{:S(2)}) collective-permute-start(bf16[256,256]{1,0:T(8,128)(2,1)S(1)} %slice.31), channel_id=1, source_target_pairs={{0,4},{4,0},{8,12},{12,8},{16,20},{20,16},{24,28},{28,24},{1,5},{5... | collective-permute-start | bytes 393224 | tf_op jit(solution)/shard_map/ppermute | solution.py:28
  62.9 3.0 %collective-permute-start.15 = (bf16[256,256]{1,0:T(8,128)(2,1)S(1)}, bf16[256,256]{1,0:T(8,128)(2,1)S(1)}, u32[]{:S(2)}, u32[]{:S(2)}) collective-permute-start(bf16[256,256]{1,0:T(8,128)(2,1)S(1)} %slice.28), channel_id=1, source_target_pairs={{0,4},{4,0},{8,12},{12,8},{16,20},{20,16},{24,28},{28,24},{1,5},{5... | collective-permute-start | bytes 393224 | tf_op jit(solution)/shard_map/ppermute | solution.py:28
  64.1 1.8 %collective-permute-start.17 = (bf16[256,256]{1,0:T(8,128)(2,1)S(1)}, bf16[256,256]{1,0:T(8,128)(2,1)S(1)}, u32[]{:S(2)}, u32[]{:S(2)}) collective-permute-start(bf16[256,256]{1,0:T(8,128)(2,1)S(1)} %slice.30), channel_id=1, source_target_pairs={{0,4},{4,0},{8,12},{12,8},{16,20},{20,16},{24,28},{28,24},{1,5},{5... | collective-permute-start | bytes 393224 | tf_op jit(solution)/shard_map/ppermute | solution.py:28

commit v3 on v2

v3 whole, which is shorter than its diff:
```python
import functools

import jax
import jax.numpy as jnp
from jax import lax
from jax.experimental import pallas as pl
from jax.experimental.pallas import tpu as pltpu
from jax.sharding import PartitionSpec as P

H = 8
DH = 128
F = H * DH
HALF = F // 2
HL = H // 2
SCALE = DH**-0.5
EPS = 1e-05
LOG2E = 1.4426950408889634
BF = jnp.bfloat16
F32 = jnp.float32
UNIT = 1e9

VMEM = pl.BlockSpec(memory_space=pltpu.VMEM)
SMEM = pl.BlockSpec(memory_space=pltpu.SMEM)


def pair(x, mask):
    count = lax.axis_size("dp")
    return lax.ppermute(x, "dp", [(i, i ^ mask) for i in range(count)])


def from_next(x, mask=0):
    dp, seg = lax.axis_size("dp"), lax.axis_size("segment")
    return lax.ppermute(
        x,
        ("dp", "segment"),
        [(i * seg + s, (i ^ mask) * seg + (s - 1) % seg) for i in range(dp) for s in range(seg)],
    )


def call(body, cost, out_shape, *args, scratch=()):
    return pl.pallas_call(
        body,
        out_shape=out_shape,
        in_specs=[SMEM if x.dtype == jnp.int32 else VMEM for x in args],
        out_specs=jax.tree.map(lambda _: VMEM, out_shape),
        scratch_shapes=list(scratch),
        cost_estimate=pl.CostEstimate(flops=int(cost * UNIT), bytes_accessed=int(cost * UNIT), transcendentals=0),
        compiler_params=pltpu.CompilerParams(vmem_limit_bytes=20 << 20),
    )(*args)


def dot(a, b, ca, cb):
    return lax.dot_general(a, b, (((ca,), (cb,)), ((), ())), preferred_element_type=F32)


def ds(start, size, align):
    return pl.ds(pl.multiple_of(start, align), size)


def after(x, *deps):
    return lax.optimization_barrier((x, *deps))[0]


def block_start(me, masks, rows):
    return lax.div(lax.bitwise_xor(me, masks[0]), len(masks)) * (len(masks) * rows)


def fill_block(me, masks, piece_refs, block):
    rows = piece_refs[0].shape[0]
    for m, ref in zip(masks, piece_refs):
        at = lax.rem(lax.bitwise_xor(me, m), len(masks)) * rows
        block[ds(at, rows, rows), :] = ref[...]


def pack_kernel(x, values, gates, x_copy, mine, other):
    core = lax.rem(lax.axis_index("dp"), 2)
    x_copy[...] = x[...]
    for i, ref in enumerate((values, gates)):
        at = pl.ds(i * HALF, HALF)
        mine[:, at] = ref[:, ds(core * HALF, HALF, HALF)]
        other[:, at] = ref[:, ds((1 - core) * HALF, HALF, HALF)]


def turn_kernel(count, xo, xp, xt, natural):
    seq_len, depth = xo.shape
    rows = depth // count
    natural[:, :seq_len] = xo[...].T
    natural[:, seq_len:] = xp[...].T
    for m in range(count):
        xt[m * rows : (m + 1) * rows, :] = natural[ds(lax.bitwise_xor(lax.axis_index("dp"), m) * rows, rows, rows), :]


def pre_kernel(blocks, has_prev, xo, xp, *refs):
    me = lax.axis_index("dp")
    if has_prev:
        prev, refs = refs[0], refs[1:]
    *pieces, pre, block = refs
    rows = pieces[0].shape[0]
    seq_len = xo.shape[0]
    for i, masks in enumerate(blocks):
        per = len(masks)
        fill_block(me, masks, pieces[i * per : (i + 1) * per], block)
        cols = ds(block_start(me, masks, rows), per * rows, per * rows)
        for s, x in ((0, xo), (1, xp)):
            own = pl.ds(s * seq_len, seq_len)
            part = dot(x[:, cols], block[...], 1, 0)
            if i > 0:
                part = part + pre[own, :]
            elif has_prev:
                part = part + prev[own, :]
            pre[own, :] = part


def gate(raw, scale):
    sig = pltpu.reciprocal(1.0 + jnp.exp2(raw * (-scale * LOG2E)), approx=True)
    out = raw * sig
    return out, sig + (out * scale if scale != 1.0 else out) * (1.0 - sig)


def forward_kernel(masks, xo, xp, prev, vgo, vgp, *refs):
    *pieces, act, slope, prob, dprob, mixed, block = refs
    me = lax.axis_index("dp")
    seq_len = xo.shape[0]
    top = seq_len // 2
    fill_block(me, masks, pieces, block)
    rows = pieces[0].shape[0]
    cols = ds(block_start(me, masks, rows), len(masks) * rows, len(masks) * rows)
    for s, x in ((0, xo), (1, xp)):
        own = pl.ds(s * seq_len, seq_len)
        a, d = gate(prev[own, :] + dot(x[:, cols], block[...], 1, 0), 1.0)
        act[own, :] = a.astype(BF)
        slope[own, :] = d
    causal = lax.broadcasted_iota(jnp.int32, (top, top), 1) <= lax.broadcasted_iota(jnp.int32, (top, top), 0)
    none = jnp.zeros((top, top), BF)
    units = [(s, h) for s in range(2) for h in range(HL)]
    raws = []
    for s, h in units:
        own = pl.ds(s * seq_len, seq_len)
        raws.append(dot(act[own, pl.ds(h * DH, DH)], act[own, pl.ds(HALF + h * DH, DH)], 1, 1))
    probs = []
    for (s, h), raw in zip(units, raws):
        p0, d0 = gate(raw[:top, :top], SCALE)
        p1, d1 = gate(raw[top:, :], SCALE)
        p0, d0 = jnp.where(causal, p0, 0.0), jnp.where(causal, d0, 0.0)
        p2, d2 = jnp.where(causal, p1[:, top:], 0.0), jnp.where(causal, d1[:, top:], 0.0)
        whole = []
        for upper, left, right in ((p0, p1, p2), (d0, d1, d2)):
            whole.append(
                jnp.concatenate(
                    [
                        jnp.concatenate([upper.astype(BF), none], 1),
                        jnp.concatenate([left[:, :top].astype(BF), right.astype(BF)], 1),
                    ],
                    0,
                )
            )
        probs.append(whole[0])
        prob[s * HL + h] = whole[0]
        dprob[s * HL + h] = whole[1]
    for (s, h), p in zip(units, probs):
        val = (vgp if s else vgo)[:, pl.ds(h * DH, DH)]
        mixed[pl.ds(s * seq_len, seq_len), pl.ds(h * DH, DH)] = dot(p, val, 1, 0)


def stats_kernel(length, mixed, vgo, vgp, co, cp, prod, stats):
    seq_len = co.shape[0]
    prod[:seq_len, :] = vgo[:, HALF:].astype(F32) * co[...].astype(F32)
    prod[seq_len:, :] = vgp[:, HALF:].astype(F32) * cp[...].astype(F32)
    lane = lax.broadcasted_iota(jnp.int32, (seq_len, 128), 1)
    row = lax.broadcasted_iota(jnp.int32, (seq_len, 128), 0)
    live = jnp.where(row < length[0, 0], 1.0, 0.0)
    for s in range(2):
        own = pl.ds(s * seq_len, seq_len)
        grad = prod[own, :]
        m = mixed[own, :]
        total = jnp.sum(m, axis=1, keepdims=True)
        off = m - total * (1.0 / HALF)
        cols = [
            total,
            jnp.sum(off * off, axis=1, keepdims=True),
            jnp.sum(grad, axis=1, keepdims=True),
            jnp.sum(grad * off, axis=1, keepdims=True),
        ]
        packed = live
        for i, col in enumerate(cols):
            packed = jnp.where(lane == i, col, packed)
        stats[:, own] = packed.T[:8, :]


def backward_kernel(far, xt, act, slope, prob, dprob, mixed, mine, theirs, vgo, vgp, prod, co, cp, *refs):
    gpre, own_grads, far_grads, *terms = refs
    seq_len = co.shape[0]
    grad_refs = own_grads, far_grads
    units = []
    for s in range(2):
        own = pl.ds(s * seq_len, seq_len)
        other = pl.ds((1 - s) * seq_len, seq_len)
        a, b = mine[:, own], theirs[:, other]
        mean = (a[0:1] + b[0:1]) * (1.0 / F)
        mean_a, mean_b = a[0:1] * (1.0 / HALF), b[0:1] * (1.0 / HALF)
        gap = mean_a - mean_b
        variance = (a[1:2] + b[1:2] + gap * gap * (HALF * 0.5)) * (1.0 / F)
        live = (b if s else a)[4:5] > 0.5
        rate = jnp.where(live, SCALE * lax.rsqrt(variance * (SCALE * SCALE) + EPS), 0.0)
        c1 = (a[2:3] + b[2:3]) * (1.0 / F)
        cross = a[3:4] + b[3:4] + (mean_a - mean) * a[2:3] + (mean_b - mean) * b[2:3]
        c2 = cross * rate * (1.0 / F)
        cols = jnp.concatenate([mean, rate, c1, c2, mean, rate, c1, c2], 0).T
        mean, rate, c1, c2 = (cols[:, i : i + 1] for i in range(4))
        for h in range(HL):
            local = pl.ds(h * DH, DH)
            val, cot = (vgp[:, local], cp[:, local]) if s else (vgo[:, local], co[:, local])
            normed = (mixed[own, local] - mean) * rate
            grad_refs[s][:, pl.ds(HALF + h * DH, DH)] = (normed * cot.astype(F32)).astype(BF)
            dmix = (rate * (prod[own, local] - c1 - normed * c2)).astype(BF)
            units.append((own, h, s * HL + h, val, dmix))
    dscores = [dot(dmix, val, 1, 1).astype(BF) * dprob[u] for _, _, u, val, dmix in units]
    for (own, h, u, _, dmix), dscore in zip(units, dscores):
        grad_refs[u // HL][:, pl.ds(h * DH, DH)] = dot(prob[u], dmix, 0, 0).astype(BF)
        q_at, k_at = pl.ds(h * DH, DH), pl.ds(HALF + h * DH, DH)
        dq = dot(dscore, act[own, k_at], 1, 0)
        dk = dot(dscore, act[own, q_at], 0, 0)
        gpre[own, q_at] = (dq * slope[own, q_at]).astype(BF)
        gpre[own, k_at] = (dk * slope[own, k_at]).astype(BF)
    rows = terms[0].shape[0]
    for m, term in zip(far, terms):
        term[...] = dot(xt[m * rows : (m + 1) * rows, :], gpre[...], 1, 0).astype(BF)


def term_kernel(near, xt, gpre, *terms):
    rows = terms[0].shape[0]
    for first in range(0, len(near), 2):
        m = near[first]
        both = dot(xt[m * rows : (m + 2) * rows, :], gpre[...], 1, 0).astype(BF)
        terms[first][...] = both[:rows, :]
        terms[first + 1][...] = both[rows:, :]


def fold_kernel(first, added, out):
    out[...] = (first[...].astype(F32) + added[...].astype(F32)).astype(BF)


def near_kernel(own, x, far, y, out_own, out_far):
    out_own[...] = own[...].astype(F32) + x[...].astype(F32)
    out_far[...] = far[...].astype(F32) + y[...].astype(F32)


def input_kernel(blocks, *refs):
    *pieces, gpre, own_out, other_out, block = refs
    me = lax.axis_index("dp")
    rows = pieces[0].shape[0]
    seq_len = own_out.shape[0]
    done = 0
    for masks in blocks:
        fill_block(me, masks, pieces[done : done + len(masks)], block)
        done += len(masks)
        cols = ds(block_start(me, masks, rows), len(masks) * rows, len(masks) * rows)
        for s, out in ((0, own_out), (1, other_out)):
            out[:, cols] = dot(gpre[pl.ds(s * seq_len, seq_len), :], block[...], 1, 1).astype(out.dtype)


def collect_kernel(gi_o, gi_r, own, far, gi, gv, gg):
    core = lax.rem(lax.axis_index("dp"), 2)
    gi[...] = (gi_o[...] + gi_r[...].astype(F32)).astype(BF)
    for c, ref in ((core, own), (1 - core, far)):
        for i, out in enumerate((gv, gg)):
            out[:, ds(c * HALF, HALF, HALF)] = ref[:, pl.ds(i * HALF, HALF)]


def weight_kernel(own, x, far, y, out):
    core = lax.rem(lax.axis_index("dp"), 2)
    for c, near, added in ((core, own, x), (1 - core, far, y)):
        for side in range(2):
            at = pl.ds(side * HALF, HALF)
            out[:, ds(side * F + c * HALF, HALF, HALF)] = near[:, at] + added[:, at].astype(F32)


def like(shape, kind):
    return jax.ShapeDtypeStruct(shape, kind)


def halve(terms, count):
    bit = count // 2
    while bit >= 8:
        terms = {
            m: (t.astype(F32) + pair(terms[m + bit], bit).astype(F32)).astype(BF) for m, t in terms.items() if m < bit
        }
        bit //= 2
    return terms


def on_device(inputs, values, gate_values, out_grad, lengths, qk_weight):
    count = lax.axis_size("dp")
    core = lax.rem(lax.axis_index("dp"), 2)
    xo, vo, go, grads = inputs[0, 0], values[0, 0], gate_values[0, 0], out_grad[0, 0]
    shard = qk_weight[0]
    rows, depth = shard.shape[0], xo.shape[1]
    seq_len = xo.shape[0]
    two = 2 * seq_len
    per = 256 // rows
    blocks = [tuple(range(b, b + per)) for b in range(0, count, per)]
    block = pltpu.VMEM((per * rows, F), BF)

    def half(x, c):
        return lax.dynamic_slice_in_dim(x, c * HALF, HALF, 1)

    def held(some):
        return [pieces[m] for masks in some for m in masks]

    low = jnp.concatenate([shard[:, :HALF], shard[:, F : F + HALF]], 1)
    high = jnp.concatenate([shard[:, HALF:F], shard[:, F + HALF :]], 1)
    mine = jnp.where(core == 0, low, high)
    other = jnp.where(core == 0, high, low)
    pieces = {0: mine}
    pieces[1] = pair(other, 1)
    pieces[2] = pair(mine, 2)
    pieces[5] = pair(other, 5)
    xp = pair(after(xo, mine), 1)
    xo, vgo, vgp = call(pack_kernel, 0.001, [like((seq_len, F), BF)] * 3, xo, vo, go)
    cp = from_next(half(after(grads, pieces[1]), 1 - core), 1)
    co = from_next(half(after(grads, pieces[1]), core))
    vgp = pair(vgp, 1)
    pieces[3] = pair(after(other, xp, pieces[1], vgp), 3)
    pieces[4] = pair(after(mine, xp, pieces[1], vgp), 4)

    xt = call(
        functools.partial(turn_kernel, count),
        10,
        like((depth, two), BF),
        xo,
        xp,
        scratch=[pltpu.VMEM((depth, two), BF)],
    )
    pieces[6] = pair(pieces[2], 4)
    pieces[7] = pair(pieces[5], 2)
    bit = 8
    while bit < count:
        for m in range(bit):
            pieces[m + bit] = pair(pieces[m], bit)
        bit *= 2
    first = functools.partial(pre_kernel, blocks[:1], False)
    pre = call(first, 0.001, like((two, F), F32), xo, xp, *held(blocks[:1]), scratch=[block])
    more = functools.partial(pre_kernel, blocks[1:-1], True)
    pre = call(more, 0.001, like((two, F), F32), xo, xp, pre, *held(blocks[1:-1]), scratch=[block])
    cp, pre = lax.optimization_barrier((cp, pre))
    act, slope, prob, dprob, mixed = call(
        functools.partial(forward_kernel, blocks[-1]),
        0.001,
        [
            like((two, F), BF),
            like((two, F), F32),
            like((2 * HL, seq_len, seq_len), BF),
            like((2 * HL, seq_len, seq_len), BF),
            like((two, HALF), F32),
        ],
        xo,
        xp,
        pre,
        vgo,
        vgp,
        *held(blocks[-1:]),
        scratch=[block],
    )
    prod, stats = call(
        stats_kernel,
        1, [like((two, HALF), F32), like((8, two), F32)], lengths, mixed, vgo, vgp, co, cp
    )
    theirs = pair(stats, 1)

    far = [m for m in range(count) if m % 8 >= 6]
    near = [m for m in range(count) if m % 8 < 6]
    gpre, own_g, far_g, *terms = call(
        functools.partial(backward_kernel, far),
        0.1,
        [like((two, F), BF)] + [like((seq_len, F), BF)] * 2 + [like((rows, F), BF)] * len(far),
        xt,
        act,
        slope,
        prob,
        dprob,
        mixed,
        stats,
        theirs,
        vgo,
        vgp,
        prod,
        co,
        cp,
    )
    diagonal = halve(dict(zip(far, terms)), count)
    far_g = pair(far_g, 1)
    by_x, by_y = lax.optimization_barrier((pair(diagonal[6], 2), pair(diagonal[7], 4)))
    terms = call(functools.partial(term_kernel, near), 0.1, [like((rows, F), BF)] * len(near), xt, gpre)
    t = halve(dict(zip(near, terms)), count)
    x_r, y_r = lax.optimization_barrier((pair(t[2], 2), pair(t[5], 5)))
    far_t = pair(after(t[1], far_g), 1)
    near_own, near_far = call(near_kernel, 0.001, [like((rows, F), F32)] * 2, t[0], x_r, far_t, y_r)
    gi_o, gi_other = call(
        functools.partial(input_kernel, blocks),
        10,
        [like((seq_len, depth), F32), like((seq_len, depth), BF)],
        *held(blocks),
        gpre,
        scratch=[block],
    )
    gi_r = pair(after(gi_other, far_t), 1)
    send_y = call(fold_kernel, 0.3, like((rows, F), BF), t[4], by_x)
    send_x = call(fold_kernel, 0.3, like((rows, F), BF), t[3], by_y)
    grad_in, grad_val, grad_gate = call(
        collect_kernel, 0.3, [like((seq_len, F), BF)] * 3, gi_o, gi_r, own_g, far_g
    )
    sums = [near_own, pair(send_y, 4), near_far, pair(send_x, 3)]
    sums, _ = lax.optimization_barrier((sums, (grad_in, grad_val, grad_gate)))
    grad_shard = call(weight_kernel, 1, like((rows, 2 * F), F32), *sums)
    return (grad_in[None, None], grad_val[None, None], grad_gate[None, None], grad_shard[None])


def solution(mesh):
    return jax.shard_map(
        on_device,
        mesh=mesh,
        in_specs=(
            P("segment", "dp", None, None),
            P("segment", "dp", None, None),
            P("segment", "dp", None, None),
            P("segment", "dp", None, None),
            P("segment", "dp"),
            P("segment", "dp", None),
        ),
        out_specs=(
            P("segment", "dp", None, None),
            P("segment", "dp", None, None),
            P("segment", "dp", None, None),
            P("segment", "dp", None),
        ),
        check_vma=False,
    )
```

time: 67.9 us -> 57 us (0.84)
  starting transfers between devices: 25.8 us -> 20 us
  Pallas kernels: 17.6 us -> 13.7 us
  waiting for transfers between devices: 19.5 us -> 18.5 us
    ppermute x31 -> x19, starting transfers between devices: 22 us -> 13.2 us  [pair(): return lax.ppermute(x, 'dp', [(i, i ^ mask) for i in range(count)])]
    ppermute x2, waiting for transfers between devices: 8.42 us -> 1.49 us  [from_next(): lax.ppermute(x, ('dp', 'segment'), [(i * seg + s, (i ^ mask) * seg + (s -...]
    ppermute x31 -> x19, waiting for transfers between devices: 11.1 us -> 17 us  [pair(): return lax.ppermute(x, 'dp', [(i, i ^ mask) for i in range(count)])]
    pallas_call x10 -> x14, Pallas kernels: 17.6 us -> 13.7 us  [call(): pl.pallas_call(body, out_shape=out_shape, in_specs=[SMEM if x.dtype == jn...]
    ppermute x2, starting transfers between devices: 3.77 us -> 6.87 us  [from_next(): lax.ppermute(x, ('dp', 'segment'), [(i * seg + s, (i ^ mask) * seg + (s -...]
    select_n x1, other arithmetic: 0.1 us -> 0.81 us  [on_device(): other = jnp.where(core == 0, high, low)]
    concatenate x1 -> x0, other arithmetic: 0.7 us -> none  [on_device(): jnp.concatenate([me.astype(jnp.int32)[None], lengths[0], pair(lengths[0],...]
  transfers between devices with their start and end apart: 33 -> 21, of which waited for: 15 -> 8; matrix products, arithmetic and copies ran while one was open for 3% -> 2% of each run, Pallas kernels for 15% -> 17%
where the time goes in v3:
time: 57 us; the launch traced here: 56.8 us
  starting transfers between devices  20 us (35%)
  waiting for transfers between devices  18.5 us (32%)
  Pallas kernels  13.7 us (24%)
  local copies, waits for them, and re-layouts  2.32 us (4%)
  between operations  1.47 us (3%)
  other arithmetic  0.81 us (1%)
    ppermute x19, waiting for transfers between devices, pair(): return lax.ppermute(x, 'dp', [(i, i ^ mask) for i in range(count)])  17 us
    pallas_call x14, Pallas kernels, call(): pl.pallas_call(body, out_shape=out_shape, in_specs=[SMEM if x.dtype == jn...  13.7 us
    ppermute x19, starting transfers between devices, pair(): return lax.ppermute(x, 'dp', [(i, i ^ mask) for i in range(count)])  13.2 us
    ppermute x2, starting transfers between devices, from_next(): lax.ppermute(x, ('dp', 'segment'), [(i * seg + s, (i ^ mask) * seg + (s -...  6.87 us
    ppermute x2, waiting for transfers between devices, from_next(): lax.ppermute(x, ('dp', 'segment'), [(i * seg + s, (i ^ mask) * seg + (s -...  1.49 us
    slice x1, local copies, waits for them, and re-layouts, on_device(): low = jnp.concatenate([shard[:, :HALF], shard[:, F:F + HALF]], 1)  1.25 us
  transfers between devices with their start and end apart: 21, of which 8 were waited for; matrix products, arithmetic and copies ran while one was open for 2% of the time, Pallas kernels for 17%

profile of v3, /device:TPU:0, one launch (start us, length us, event | category | flops | bytes accessed | tf_op | source)
XLA Modules:
  0.0 56.8 jit_solution(15101303178662768372)
XLA Ops:
  0.7 1.2 %fusion = (bf16[128,512]{1,0:T(8,128)(2,1)S(1)}, bf16[128,512]{1,0:T(8,128)(2,1)S(1)}, bf16[128,512]{1,0:T(8,128)(2,1)S(1)}, bf16[128,512]{1,0:T(8,128)(2,1)S(1)}) fusion(bf16[128,2048]{1,0:T(8,128)(2,1)} %bitcast.14), kind=kLoop, calls=%fused_computation.6 | loop fusion | bytes 1048576 | tf_op jit(solution)/shard_map/slice | solution.py:310
  1.9 0.8 %broadcast_select_fusion = (bf16[128,1024]{1,0:T(8,128)(2,1)}, bf16[128,1024]{1,0:T(8,128)(2,1)S(1)}) fusion(pred[]{:T(512)S(6)} %eq.4, bf16[128,512]{1,0:T(8,128)(2,1)S(1)} %get-tuple-element.97, bf16[128,512]{1,0:T(8,128)(2,1)S(1)} %get-tuple-element.98, bf16[128,512]{1,0:T(8,128)(2,1)S(1)} %get-tuple-element.99, bf16[128,512]{1,0:T(8,128)(2,1)S(1)} %get-tuple-element.96), kind=kLoop, calls=%fused_computation.2 | loop fusion | flops 1310720 | bytes 1048577 | tf_op jit(solution)/shard_map/jit(_where)/select_n | solution.py:313
  2.7 0.5 collective-permute-start.2
  3.2 0.1 shard_map.93
  3.3 0.1 collective-permute-start.3
  3.4 0.5 collective-permute-start
  3.9 2.6 %collective-permute-start.6 = (bf16[128,1024]{1,0:T(8,128)(2,1)}, bf16[128,1024]{1,0:T(8,128)(2,1)S(1)}, u32[]{:S(2)}, u32[]{:S(2)}) collective-permute-start(bf16[128,1024]{1,0:T(8,128)(2,1)} %get-tuple-element.50), channel_id=1, source_target_pairs={{0,20},{4,16},{8,28},{12,24},{16,4},{20,0},{24,12},{28,8},{1,21},{... | collective-permute-start | bytes 786440 | tf_op jit(solution)/shard_map/ppermute | solution.py:28
  6.5 1.5 %collective-permute-start.1 = (bf16[128,1024]{1,0:T(8,128)(2,1)S(1)}, bf16[128,1024]{1,0:T(8,128)(2,1)}, u32[]{:S(2)}, u32[]{:S(2)}) collective-permute-start(bf16[128,1024]{1,0:T(8,128)(2,1)S(1)} %get-tuple-element.51.refs_0_), channel_id=1, source_target_pairs={{0,8},{4,12},{8,0},{12,4},{16,24},{20,28},{24,16},{28,20},{1,9},{5... | collective-permute-start | bytes 786440 | tf_op jit(solution)/shard_map/ppermute | solution.py:28
  8.0 0.0 collective-permute-done.refs_1_
  8.0 0.0 collective-permute-done.2.xp
  8.0 0.5 collective-permute-start.4
  8.5 1.5 %collective-permute-start.5 = (bf16[128,1024]{1,0:T(8,128)(2,1)S(1)}, bf16[128,1024]{1,0:T(8,128)(2,1)S(1)}, u32[]{:S(2)}, u32[]{:S(2)}) collective-permute-start(bf16[128,1024]{1,0:T(8,128)(2,1)S(1)} %get-tuple-element.51.refs_0_), channel_id=1, source_target_pairs={{0,16},{4,20},{8,24},{12,28},{16,0},{20,4},{24,8},{28,12},{1,17},{... | collective-permute-start | bytes 786440 | tf_op jit(solution)/shard_map/ppermute | solution.py:28
  10.1 1.1 %constant_dynamic-slice_fusion = (bf16[256,512]{1,0:T(8,128)(2,1)S(1)}, bf16[256,512]{1,0:T(8,128)(2,1)S(1)}) fusion(bf16[256,1024]{1,0:T(8,128)(2,1)} %bitcast.13, s32[]{:T(128)S(6)} %select_n.22, s32[]{:T(128)S(6)} %select_n.21), kind=kLoop, calls=%fused_computation.4 | loop fusion | bytes 1048584 | tf_op jit(solution)/shard_map/dynamic_slice | solution.py:305
  11.1 3.3 %collective-permute-start.9 = (bf16[256,512]{1,0:T(8,128)(2,1)S(1)}, bf16[256,512]{1,0:T(8,128)(2,1)S(1)}, u32[]{:S(2)}, u32[]{:S(2)}) collective-permute-start(bf16[256,512]{1,0:T(8,128)(2,1)S(1)} %get-tuple-element.93), channel_id=1, source_target_pairs={{0,7},{1,4},{2,5},{3,6},{4,3},{5,0},{6,1},{7,2},{8,15},{9,12},{10,... | collective-permute-start | bytes 786440 | tf_op jit(solution)/shard_map/ppermute | solution.py:33
  14.4 0.6 %collective-permute-start.8 = (bf16[128,1024]{1,0:T(8,128)(2,1)S(1)}, bf16[128,1024]{1,0:T(8,128)(2,1)S(1)}, u32[]{:S(2)}, u32[]{:S(2)}) collective-permute-start(bf16[128,1024]{1,0:T(8,128)(2,1)S(1)} %collective-permute-done.6.refs_4_.refs_5_), channel_id=1, source_target_pairs={{0,8},{4,12},{8,0},{12,4},{16,24},{20,28},{24,16},{28,20},{1,9},{5... | collective-permute-start | bytes 786440 | tf_op jit(solution)/shard_map/ppermute | solution.py:28
  15.0 0.8 %collective-permute-done.1.refs_1_.refs_2_ = bf16[128,1024]{1,0:T(8,128)(2,1)} collective-permute-done((bf16[128,1024]{1,0:T(8,128)(2,1)S(1)}, bf16[128,1024]{1,0:T(8,128)(2,1)}, u32[]{:S(2)}, u32[]{:S(2)}) %collective-permute-start.1) | collective-permute-done | bytes 262176 | tf_op jit(solution)/shard_map/ppermute | solution.py:28
  15.8 0.5 collective-permute-start.7
  16.3 4.1 %collective-permute-done.4.refs_2_.refs_3_ = bf16[128,1024]{1,0:T(8,128)(2,1)S(1)} collective-permute-done((bf16[128,1024]{1,0:T(8,128)(2,1)}, bf16[128,1024]{1,0:T(8,128)(2,1)S(1)}, u32[]{:S(2)}, u32[]{:S(2)}) %collective-permute-start.4) | collective-permute-done | bytes 262176 | tf_op jit(solution)/shard_map/ppermute | solution.py:28
  20.4 3.6 %collective-permute-start.10 = (bf16[256,512]{1,0:T(8,128)(2,1)S(1)}, bf16[256,512]{1,0:T(8,128)(2,1)S(1)}, u32[]{:S(2)}, u32[]{:S(2)}) collective-permute-start(bf16[256,512]{1,0:T(8,128)(2,1)S(1)} %get-tuple-element.92), channel_id=1, source_target_pairs={{0,3},{1,0},{2,1},{3,2},{4,7},{5,4},{6,5},{7,6},{8,11},{9,8},{10,9... | collective-permute-start | bytes 786440 | tf_op jit(solution)/shard_map/ppermute | solution.py:33
  24.7 0.5 shard_map.95.refs_0_
  25.2 1.8 %shard_map.96.prev = f32[512,1024]{1,0:T(8,128)S(1)} custom-call(bf16[256,1024]{1,0:T(8,128)(2,1)S(1)} %get-tuple-element.52.xo, bf16[256,1024]{1,0:T(8,128)(2,1)S(1)} %collective-permute-done.2.xp, f32[512,1024]{1,0:T(8,128)S(1)} %shard_map.95.refs_0_, bf16[128,1024]{1,0:T(8,128)(2,1)} %collective-permute-done.1.refs_1_.refs_2_, ...), custom_call_target="tpu_custom_call" | custom-call | flops 1000000 | bytes 1000000 | tf_op jit(solution)/shard_map/pallas_call | solution.py:41
  27.0 2.2 %shard_map.97 = (bf16[512,1024]{1,0:T(8,128)(2,1)S(1)}, f32[512,1024]{1,0:T(8,128)S(1)}, bf16[8,256,256]{2,1,0:T(8,128)(2,1)S(1)}, bf16[8,256,256]{2,1,0:T(8,128)(2,1)S(1)}, f32[512,512]{1,0:T(8,128)S(1)}) custom-call(bf16[256,1024]{1,0:T(8,128)(2,1)S(1)} %get-tuple-element.52.xo, bf16[256,1024]{1,0:T(8,128)(2,1)S(1)} %collective-permute-done.2.xp, ...), custom_call_target="tpu_custom_call" | custom-call | flops 1000000 | bytes 1000000 | tf_op jit(solution)/shard_map/pallas_call | solution.py:41
  29.2 1.5 %collective-permute-done.10.co = bf16[256,512]{1,0:T(8,128)(2,1)S(1)} collective-permute-done((bf16[256,512]{1,0:T(8,128)(2,1)S(1)}, bf16[256,512]{1,0:T(8,128)(2,1)S(1)}, u32[]{:S(2)}, u32[]{:S(2)}) %collective-permute-start.10) | collective-permute-done | bytes 262176 | tf_op jit(solution)/shard_map/ppermute | solution.py:33
  30.7 0.6 %shard_map.98 = (f32[512,512]{1,0:T(8,128)S(1)}, f32[8,512]{1,0:T(8,128)S(1)}) custom-call(s32[1,1]{1,0:T(1,128)S(6)} %copy.10.length, f32[512,512]{1,0:T(8,128)S(1)} %get-tuple-element.60.mixed, bf16[256,1024]{1,0:T(8,128)(2,1)S(1)} %get-tuple-element.55.vgo, bf16[256,1024]{1,0:T(8,128)(2,1)S(1)} %collective-permute-done.3.vgp, ...), custom_call_target="tpu_custom_call" | custom-call | flops 1000000000 | bytes 1000000000 | tf_op jit(solution)/shard_map/pallas_call | solution.py:41
  31.3 0.2 collective-permute-start.11
  31.5 0.4 shard_map.94.xt
  31.9 0.6 %collective-permute-done.11.theirs = f32[8,512]{1,0:T(8,128)S(1)} collective-permute-done((f32[8,512]{1,0:T(8,128)S(1)}, f32[8,512]{1,0:T(8,128)S(1)}, u32[]{:S(2)}, u32[]{:S(2)}) %collective-permute-start.11) | collective-permute-done | bytes 16416 | tf_op jit(solution)/shard_map/ppermute | solution.py:28
  32.5 2.2 %shard_map.99 = (bf16[512,1024]{1,0:T(8,128)(2,1)S(1)}, bf16[256,1024]{1,0:T(8,128)(2,1)S(1)}, bf16[256,1024]{1,0:T(8,128)(2,1)S(1)}, bf16[128,1024]{1,0:T(8,128)(2,1)S(1)}, bf16[128,1024]{1,0:T(8,128)(2,1)S(1)}) custom-call(bf16[1024,512]{1,0:T(8,128)(2,1)S(1)} %shard_map.94.xt, bf16[512,1024]{1,0:T(8,128)(2,1)S(1)} %get-tuple-element.56.act, ...), custom_call_target="tpu_custom_call" | custom-call | flops 100000000 | bytes 100000000 | tf_op jit(solution)/shard_map/pallas_call | solution.py:41
  34.7 0.2 collective-permute-start.12
  35.0 0.6 collective-permute-start.17
  35.5 0.5 collective-permute-start.18
  36.0 1.0 %shard_map.101 = (bf16[128,1024]{1,0:T(8,128)(2,1)S(1)}, bf16[128,1024]{1,0:T(8,128)(2,1)S(1)}, bf16[128,1024]{1,0:T(8,128)(2,1)S(1)}, bf16[128,1024]{1,0:T(8,12...) custom-call(bf16[1024,512]{1,0:T(8,128)(2,1)S(1)} %shard_map.94.xt, ...), custom_call_target="tpu_custom_call" | custom-call | flops 100000000 | bytes 100000000 | tf_op jit(solution)/shard_map/pallas_call | solution.py:41
  37.0 0.1 collective-permute-start.13
  37.1 2.3 %shard_map.100 = (f32[256,1024]{1,0:T(8,128)S(1)}, bf16[256,1024]{1,0:T(8,128)(2,1)S(1)}) custom-call(bf16[128,1024]{1,0:T(8,128)(2,1)S(1)} %get-tuple-element.51.refs_0_, bf16[128,1024]{1,0:T(8,128)(2,1)S(1)} %collective-permute-done.refs_1_, bf16[128,1024]{1,0:T(8,128)(2,1)} %collective-permute-done.1.refs_1_.refs_2_, ...), custom_call_target="tpu_custom_call" | custom-call | flops 10000000000 | bytes 10000000000 | tf_op jit(solution)/shard_map/pallas_call | solution.py:41
  39.5 0.6 collective-permute-start.14
  40.0 1.5 %collective-permute-start.15 = (bf16[128,1024]{1,0:T(8,128)(2,1)S(1)}, bf16[128,1024]{1,0:T(8,128)(2,1)S(1)}, u32[]{:S(2)}, u32[]{:S(2)}) collective-permute-start(bf16[128,1024]{1,0:T(8,128)(2,1)S(1)} %get-tuple-element.76), channel_id=1, source_target_pairs={{0,8},{4,12},{8,0},{12,4},{16,24},{20,28},{24,16},{28,20},{1,9},{5... | collective-permute-start | bytes 786440 | tf_op jit(solution)/shard_map/ppermute | solution.py:28
  41.5 0.9 %collective-permute-start.16 = (bf16[128,1024]{1,0:T(8,128)(2,1)S(1)}, bf16[128,1024]{1,0:T(8,128)(2,1)S(1)}, u32[]{:S(2)}, u32[]{:S(2)}) collective-permute-start(bf16[128,1024]{1,0:T(8,128)(2,1)S(1)} %get-tuple-element.77), channel_id=1, source_target_pairs={{0,20},{4,16},{8,28},{12,24},{16,4},{20,0},{24,12},{28,8},{1,21},{... | collective-permute-start | bytes 786440 | tf_op jit(solution)/shard_map/ppermute | solution.py:28
  42.4 1.7 %collective-permute-done.17.added = bf16[128,1024]{1,0:T(8,128)(2,1)S(1)} collective-permute-done((bf16[128,1024]{1,0:T(8,128)(2,1)S(1)}, bf16[128,1024]{1,0:T(8,128)(2,1)S(1)}, u32[]{:S(2)}, u32[]{:S(2)}) %collective-permute-start.17) | collective-permute-done | bytes 262176 | tf_op jit(solution)/shard_map/ppermute | solution.py:28
  44.1 0.1 shard_map.104
  44.1 0.1 collective-permute-start.19
  44.3 0.1 shard_map.105
  44.3 0.2 collective-permute-start.20
  44.5 5.2 %collective-permute-done.15.x = bf16[128,1024]{1,0:T(8,128)(2,1)S(1)} collective-permute-done((bf16[128,1024]{1,0:T(8,128)(2,1)S(1)}, bf16[128,1024]{1,0:T(8,128)(2,1)S(1)}, u32[]{:S(2)}, u32[]{:S(2)}) %collective-permute-start.15) | collective-permute-done | bytes 262176 | tf_op jit(solution)/shard_map/ppermute | solution.py:28
  49.7 0.3 collective-permute-done.16.y
  50.0 0.1 shard_map.103
  50.1 1.3 %shard_map.102 = (bf16[256,1024]{1,0:T(8,128)(2,1)}, bf16[256,1024]{1,0:T(8,128)(2,1)}, bf16[256,1024]{1,0:T(8,128)(2,1)}) custom-call(f32[256,1024]{1,0:T(8,128)S(1)} %get-tuple-element.65.gi_o, bf16[256,1024]{1,0:T(8,128)(2,1)S(1)} %collective-permute-done.14.gi_r, bf16[256,1024]{1,0:T(8,128)(2,1)S(1)} %get-tuple-element.71.own, ...), custom_call_target="tpu_custom_call" | custom-call | flops 300000000 | bytes 300000000 | tf_op jit(solution)/shard_map/pallas_call | solution.py:41
  51.4 4.3 %collective-permute-done.19.x = bf16[128,1024]{1,0:T(8,128)(2,1)S(1)} collective-permute-done((bf16[128,1024]{1,0:T(8,128)(2,1)S(1)}, bf16[128,1024]{1,0:T(8,128)(2,1)S(1)}, u32[]{:S(2)}, u32[]{:S(2)}) %collective-permute-start.19) | collective-permute-done | bytes 262176 | tf_op jit(solution)/shard_map/ppermute | solution.py:28
  55.7 1.1 %shard_map.106 = f32[128,2048]{1,0:T(8,128)} custom-call(f32[128,1024]{1,0:T(8,128)S(1)} %get-tuple-element.88.own, bf16[128,1024]{1,0:T(8,128)(2,1)S(1)} %collective-permute-done.19.x, f32[128,1024]{1,0:T(8,128)S(1)} %get-tuple-element.90.far, bf16[128,1024]{1,0:T(8,128)(2,1)S(1)} %collective-permute-done.20.y), custom_call_target="tpu_custom_call" | custom-call | flops 1000000000 | bytes 1000000000 | tf_op jit(solution)/shard_map/pallas_call | solution.py:41
  (17 shorter events, 0.0 us)
Async XLA Ops:
  0.6 2.1 %copy-start.2 = (bf16[1,1,256,1024]{3,2,1,0:T(8,128)(2,1)S(1)}, bf16[1,1,256,1024]{3,2,1,0:T(8,128)(2,1)}, u32[]{:S(2)}) copy-start(bf16[1,1,256,1024]{3,2,1,0:T(8,128)(2,1)} %param.6) | copy-start | bytes 1572868
  0.6 2.5 %copy-start.1 = (bf16[1,1,256,1024]{3,2,1,0:T(8,128)(2,1)S(1)}, bf16[1,1,256,1024]{3,2,1,0:T(8,128)(2,1)}, u32[]{:S(2)}) copy-start(bf16[1,1,256,1024]{3,2,1,0:T(8,128)(2,1)} %param.8) | copy-start | bytes 1572868
  0.7 2.5 %copy-start = (bf16[1,1,256,1024]{3,2,1,0:T(8,128)(2,1)S(1)}, bf16[1,1,256,1024]{3,2,1,0:T(8,128)(2,1)}, u32[]{:S(2)}) copy-start(bf16[1,1,256,1024]{3,2,1,0:T(8,128)(2,1)} %param.7) | copy-start | bytes 1572868
  2.7 5.3 %collective-permute-start.2 = (bf16[256,1024]{1,0:T(8,128)(2,1)S(1)}, bf16[256,1024]{1,0:T(8,128)(2,1)S(1)}, u32[]{:S(2)}, u32[]{:S(2)}) collective-permute-start(bf16[256,1024]{1,0:T(8,128)(2,1)S(1)} %bitcast.11), channel_id=1, source_target_pairs={{0,4},{4,0},{8,12},{12,8},{16,20},{20,16},{24,28},{28,24},{1,5},{5... | collective-permute-start | bytes 1572872 | tf_op jit(solution)/shard_map/ppermute | solution.py:28
  3.3 4.7 %collective-permute-start.3 = (bf16[256,1024]{1,0:T(8,128)(2,1)S(1)}, bf16[256,1024]{1,0:T(8,128)(2,1)S(1)}, u32[]{:S(2)}, u32[]{:S(2)}) collective-permute-start(bf16[256,1024]{1,0:T(8,128)(2,1)S(1)} %get-tuple-element.49), channel_id=1, source_target_pairs={{0,4},{4,0},{8,12},{12,8},{16,20},{20,16},{24,28},{28,24},{1,5},{5... | collective-permute-start | bytes 1572872 | tf_op jit(solution)/shard_map/ppermute | solution.py:28
  3.4 4.6 %collective-permute-start = (bf16[128,1024]{1,0:T(8,128)(2,1)}, bf16[128,1024]{1,0:T(8,128)(2,1)S(1)}, u32[]{:S(2)}, u32[]{:S(2)}) collective-permute-start(bf16[128,1024]{1,0:T(8,128)(2,1)} %get-tuple-element.50), channel_id=1, source_target_pairs={{0,4},{4,0},{8,12},{12,8},{16,20},{20,16},{24,28},{28,24},{1,5},{5... | collective-permute-start | bytes 786440 | tf_op jit(solution)/shard_map/ppermute | solution.py:28
  3.9 10.5 %collective-permute-start.6 = (bf16[128,1024]{1,0:T(8,128)(2,1)}, bf16[128,1024]{1,0:T(8,128)(2,1)S(1)}, u32[]{:S(2)}, u32[]{:S(2)}) collective-permute-start(bf16[128,1024]{1,0:T(8,128)(2,1)} %get-tuple-element.50), channel_id=1, source_target_pairs={{0,20},{4,16},{8,28},{12,24},{16,4},{20,0},{24,12},{28,8},{1,21},{... | collective-permute-start | bytes 786440 | tf_op jit(solution)/shard_map/ppermute | solution.py:28
  6.5 9.3 %collective-permute-start.1 = (bf16[128,1024]{1,0:T(8,128)(2,1)S(1)}, bf16[128,1024]{1,0:T(8,128)(2,1)}, u32[]{:S(2)}, u32[]{:S(2)}) collective-permute-start(bf16[128,1024]{1,0:T(8,128)(2,1)S(1)} %get-tuple-element.51.refs_0_), channel_id=1, source_target_pairs={{0,8},{4,12},{8,0},{12,4},{16,24},{20,28},{24,16},{28,20},{1,9},{5... | collective-permute-start | bytes 786440 | tf_op jit(solution)/shard_map/ppermute | solution.py:28
  8.0 12.4 %collective-permute-start.4 = (bf16[128,1024]{1,0:T(8,128)(2,1)}, bf16[128,1024]{1,0:T(8,128)(2,1)S(1)}, u32[]{:S(2)}, u32[]{:S(2)}) collective-permute-start(bf16[128,1024]{1,0:T(8,128)(2,1)} %get-tuple-element.50), channel_id=1, source_target_pairs={{0,12},{4,8},{8,4},{12,0},{16,28},{20,24},{24,20},{28,16},{1,13},{... | collective-permute-start | bytes 786440 | tf_op jit(solution)/shard_map/ppermute | solution.py:28
  8.5 16.6 %collective-permute-start.5 = (bf16[128,1024]{1,0:T(8,128)(2,1)S(1)}, bf16[128,1024]{1,0:T(8,128)(2,1)S(1)}, u32[]{:S(2)}, u32[]{:S(2)}) collective-permute-start(bf16[128,1024]{1,0:T(8,128)(2,1)S(1)} %get-tuple-element.51.refs_0_), channel_id=1, source_target_pairs={{0,16},{4,20},{8,24},{12,28},{16,0},{20,4},{24,8},{28,12},{1,17},{... | collective-permute-start | bytes 786440 | tf_op jit(solution)/shard_map/ppermute | solution.py:28
  11.1 15.9 %collective-permute-start.9 = (bf16[256,512]{1,0:T(8,128)(2,1)S(1)}, bf16[256,512]{1,0:T(8,128)(2,1)S(1)}, u32[]{:S(2)}, u32[]{:S(2)}) collective-permute-start(bf16[256,512]{1,0:T(8,128)(2,1)S(1)} %get-tuple-element.93), channel_id=1, source_target_pairs={{0,7},{1,4},{2,5},{3,6},{4,3},{5,0},{6,1},{7,2},{8,15},{9,12},{10,... | collective-permute-start | bytes 786440 | tf_op jit(solution)/shard_map/ppermute | solution.py:33
  14.4 12.6 %collective-permute-start.8 = (bf16[128,1024]{1,0:T(8,128)(2,1)S(1)}, bf16[128,1024]{1,0:T(8,128)(2,1)S(1)}, u32[]{:S(2)}, u32[]{:S(2)}) collective-permute-start(bf16[128,1024]{1,0:T(8,128)(2,1)S(1)} %collective-permute-done.6.refs_4_.refs_5_), channel_id=1, source_target_pairs={{0,8},{4,12},{8,0},{12,4},{16,24},{20,28},{24,16},{28,20},{1,9},{5... | collective-permute-start | bytes 786440 | tf_op jit(solution)/shard_map/ppermute | solution.py:28
  15.8 11.2 %collective-permute-start.7 = (bf16[128,1024]{1,0:T(8,128)(2,1)}, bf16[128,1024]{1,0:T(8,128)(2,1)S(1)}, u32[]{:S(2)}, u32[]{:S(2)}) collective-permute-start(bf16[128,1024]{1,0:T(8,128)(2,1)} %collective-permute-done.1.refs_1_.refs_2_), channel_id=1, source_target_pairs={{0,16},{4,20},{8,24},{12,28},{16,0},{20,4},{24,8},{28,12},{1,17},{... | collective-permute-start | bytes 786440 | tf_op jit(solution)/shard_map/ppermute | solution.py:28
  20.4 10.3 %collective-permute-start.10 = (bf16[256,512]{1,0:T(8,128)(2,1)S(1)}, bf16[256,512]{1,0:T(8,128)(2,1)S(1)}, u32[]{:S(2)}, u32[]{:S(2)}) collective-permute-start(bf16[256,512]{1,0:T(8,128)(2,1)S(1)} %get-tuple-element.92), channel_id=1, source_target_pairs={{0,3},{1,0},{2,1},{3,2},{4,7},{5,4},{6,5},{7,6},{8,11},{9,8},{10,9... | collective-permute-start | bytes 786440 | tf_op jit(solution)/shard_map/ppermute | solution.py:33
  31.3 1.2 %collective-permute-start.11 = (f32[8,512]{1,0:T(8,128)S(1)}, f32[8,512]{1,0:T(8,128)S(1)}, u32[]{:S(2)}, u32[]{:S(2)}) collective-permute-start(f32[8,512]{1,0:T(8,128)S(1)} %get-tuple-element.62.mine), channel_id=1, source_target_pairs={{0,4},{4,0},{8,12},{12,8},{16,20},{20,16},{24,28},{28,24},{1,5},{5... | collective-permute-start | bytes 49160 | tf_op jit(solution)/shard_map/ppermute | solution.py:28
  34.7 2.3 %collective-permute-start.12 = (bf16[256,1024]{1,0:T(8,128)(2,1)S(1)}, bf16[256,1024]{1,0:T(8,128)(2,1)S(1)}, u32[]{:S(2)}, u32[]{:S(2)}) collective-permute-start(bf16[256,1024]{1,0:T(8,128)(2,1)S(1)} %get-tuple-element.68), channel_id=1, source_target_pairs={{0,4},{4,0},{8,12},{12,8},{16,20},{20,16},{24,28},{28,24},{1,5},{5... | collective-permute-start | bytes 1572872 | tf_op jit(solution)/shard_map/ppermute | solution.py:28
  35.0 9.1 %collective-permute-start.17 = (bf16[128,1024]{1,0:T(8,128)(2,1)S(1)}, bf16[128,1024]{1,0:T(8,128)(2,1)S(1)}, u32[]{:S(2)}, u32[]{:S(2)}) collective-permute-start(bf16[128,1024]{1,0:T(8,128)(2,1)S(1)} %get-tuple-element.82), channel_id=1, source_target_pairs={{0,8},{4,12},{8,0},{12,4},{16,24},{20,28},{24,16},{28,20},{1,9},{5... | collective-permute-start | bytes 786440 | tf_op jit(solution)/shard_map/ppermute | solution.py:28
  35.5 8.6 %collective-permute-start.18 = (bf16[128,1024]{1,0:T(8,128)(2,1)S(1)}, bf16[128,1024]{1,0:T(8,128)(2,1)S(1)}, u32[]{:S(2)}, u32[]{:S(2)}) collective-permute-start(bf16[128,1024]{1,0:T(8,128)(2,1)S(1)} %get-tuple-element.83), channel_id=1, source_target_pairs={{0,16},{4,20},{8,24},{12,28},{16,0},{20,4},{24,8},{28,12},{1,17},{... | collective-permute-start | bytes 786440 | tf_op jit(solution)/shard_map/ppermute | solution.py:28
  37.0 2.4 %collective-permute-start.13 = (bf16[128,1024]{1,0:T(8,128)(2,1)S(1)}, bf16[128,1024]{1,0:T(8,128)(2,1)S(1)}, u32[]{:S(2)}, u32[]{:S(2)}) collective-permute-start(bf16[128,1024]{1,0:T(8,128)(2,1)S(1)} %get-tuple-element.69), channel_id=1, source_target_pairs={{0,4},{4,0},{8,12},{12,8},{16,20},{20,16},{24,28},{28,24},{1,5},{5... | collective-permute-start | bytes 786440 | tf_op jit(solution)/shard_map/ppermute | solution.py:28
  39.5 10.7 %collective-permute-start.14 = (bf16[256,1024]{1,0:T(8,128)(2,1)S(1)}, bf16[256,1024]{1,0:T(8,128)(2,1)S(1)}, u32[]{:S(2)}, u32[]{:S(2)}) collective-permute-start(bf16[256,1024]{1,0:T(8,128)(2,1)S(1)} %get-tuple-element.70), channel_id=1, source_target_pairs={{0,4},{4,0},{8,12},{12,8},{16,20},{20,16},{24,28},{28,24},{1,5},{5... | collective-permute-start | bytes 1572872 | tf_op jit(solution)/shard_map/ppermute | solution.py:28
  40.0 9.7 %collective-permute-start.15 = (bf16[128,1024]{1,0:T(8,128)(2,1)S(1)}, bf16[128,1024]{1,0:T(8,128)(2,1)S(1)}, u32[]{:S(2)}, u32[]{:S(2)}) collective-permute-start(bf16[128,1024]{1,0:T(8,128)(2,1)S(1)} %get-tuple-element.76), channel_id=1, source_target_pairs={{0,8},{4,12},{8,0},{12,4},{16,24},{20,28},{24,16},{28,20},{1,9},{5... | collective-permute-start | bytes 786440 | tf_op jit(solution)/shard_map/ppermute | solution.py:28
  41.5 8.5 %collective-permute-start.16 = (bf16[128,1024]{1,0:T(8,128)(2,1)S(1)}, bf16[128,1024]{1,0:T(8,128)(2,1)S(1)}, u32[]{:S(2)}, u32[]{:S(2)}) collective-permute-start(bf16[128,1024]{1,0:T(8,128)(2,1)S(1)} %get-tuple-element.77), channel_id=1, source_target_pairs={{0,20},{4,16},{8,28},{12,24},{16,4},{20,0},{24,12},{28,8},{1,21},{... | collective-permute-start | bytes 786440 | tf_op jit(solution)/shard_map/ppermute | solution.py:28
  44.1 11.6 %collective-permute-start.19 = (bf16[128,1024]{1,0:T(8,128)(2,1)S(1)}, bf16[128,1024]{1,0:T(8,128)(2,1)S(1)}, u32[]{:S(2)}, u32[]{:S(2)}) collective-permute-start(bf16[128,1024]{1,0:T(8,128)(2,1)S(1)} %shard_map.104), channel_id=1, source_target_pairs={{0,16},{4,20},{8,24},{12,28},{16,0},{20,4},{24,8},{28,12},{1,17},{... | collective-permute-start | bytes 786440 | tf_op jit(solution)/shard_map/ppermute | solution.py:28
  44.3 11.4 %collective-permute-start.20 = (bf16[128,1024]{1,0:T(8,128)(2,1)S(1)}, bf16[128,1024]{1,0:T(8,128)(2,1)S(1)}, u32[]{:S(2)}, u32[]{:S(2)}) collective-permute-start(bf16[128,1024]{1,0:T(8,128)(2,1)S(1)} %shard_map.105), channel_id=1, source_target_pairs={{0,12},{4,8},{8,4},{12,0},{16,28},{20,24},{24,20},{28,16},{1,13},{... | collective-permute-start | bytes 786440 | tf_op jit(solution)/shard_map/ppermute | solution.py:28

commit v4 on v3

--- a/solution.py
+++ b/solution.py
@@ -72,38 +72,42 @@
         block[ds(at, rows, rows), :] = ref[...]
 
 
-def pack_kernel(x, values, gates, x_copy, mine, other):
+def pack_kernel(other, x, values, gates, bundle, vg):
     core = lax.rem(lax.axis_index("dp"), 2)
-    x_copy[...] = x[...]
+    seq_len, rows = x.shape[0], other.shape[0]
+    bundle[:seq_len, :] = x[...]
+    bundle[pl.ds(2 * seq_len, rows), :] = other[...]
     for i, ref in enumerate((values, gates)):
         at = pl.ds(i * HALF, HALF)
-        mine[:, at] = ref[:, ds(core * HALF, HALF, HALF)]
-        other[:, at] = ref[:, ds((1 - core) * HALF, HALF, HALF)]
-
-
-def turn_kernel(count, xo, xp, xt, natural):
-    seq_len, depth = xo.shape
+        vg[:, at] = ref[:, ds(core * HALF, HALF, HALF)]
+        bundle[pl.ds(seq_len, seq_len), at] = ref[:, ds((1 - core) * HALF, HALF, HALF)]
+
+
+def turn_kernel(count, bo, bp, xt, natural):
+    depth, seq_len = xt.shape[0], xt.shape[1] // 2
     rows = depth // count
-    natural[:, :seq_len] = xo[...].T
-    natural[:, seq_len:] = xp[...].T
+    natural[:, :seq_len] = bo[:seq_len, :].T
+    natural[:, seq_len:] = bp[:seq_len, :].T
     for m in range(count):
         xt[m * rows : (m + 1) * rows, :] = natural[ds(lax.bitwise_xor(lax.axis_index("dp"), m) * rows, rows, rows), :]
 
 
-def pre_kernel(blocks, has_prev, xo, xp, *refs):
+def pre_kernel(blocks, has_prev, bo, bp, *refs):
     me = lax.axis_index("dp")
     if has_prev:
         prev, refs = refs[0], refs[1:]
     *pieces, pre, block = refs
-    rows = pieces[0].shape[0]
-    seq_len = xo.shape[0]
+    seq_len = pre.shape[0] // 2
+    rows = block.shape[0] // len(blocks[0])
+    if not has_prev:
+        pieces[1:1] = [bp.at[pl.ds(2 * seq_len, rows), :]]
     for i, masks in enumerate(blocks):
         per = len(masks)
         fill_block(me, masks, pieces[i * per : (i + 1) * per], block)
         cols = ds(block_start(me, masks, rows), per * rows, per * rows)
-        for s, x in ((0, xo), (1, xp)):
+        for s, x in ((0, bo), (1, bp)):
             own = pl.ds(s * seq_len, seq_len)
-            part = dot(x[:, cols], block[...], 1, 0)
+            part = dot(x[:seq_len, cols], block[...], 1, 0)
             if i > 0:
                 part = part + pre[own, :]
             elif has_prev:
@@ -117,17 +121,18 @@
     return out, sig + (out * scale if scale != 1.0 else out) * (1.0 - sig)
 
 
-def forward_kernel(masks, xo, xp, prev, vgo, vgp, *refs):
+def forward_kernel(masks, bo, bp, prev, vgo, *refs):
     *pieces, act, slope, prob, dprob, mixed, block = refs
     me = lax.axis_index("dp")
-    seq_len = xo.shape[0]
+    seq_len = vgo.shape[0]
     top = seq_len // 2
+    far = pl.ds(seq_len, seq_len)
     fill_block(me, masks, pieces, block)
     rows = pieces[0].shape[0]
     cols = ds(block_start(me, masks, rows), len(masks) * rows, len(masks) * rows)
-    for s, x in ((0, xo), (1, xp)):
+    for s, x in ((0, bo), (1, bp)):
         own = pl.ds(s * seq_len, seq_len)
-        a, d = gate(prev[own, :] + dot(x[:, cols], block[...], 1, 0), 1.0)
+        a, d = gate(prev[own, :] + dot(x[:seq_len, cols], block[...], 1, 0), 1.0)
         act[own, :] = a.astype(BF)
         slope[own, :] = d
     causal = lax.broadcasted_iota(jnp.int32, (top, top), 1) <= lax.broadcasted_iota(jnp.int32, (top, top), 0)
@@ -158,14 +163,15 @@
         prob[s * HL + h] = whole[0]
         dprob[s * HL + h] = whole[1]
     for (s, h), p in zip(units, probs):
-        val = (vgp if s else vgo)[:, pl.ds(h * DH, DH)]
+        at = pl.ds(h * DH, DH)
+        val = bp[far, at] if s else vgo[:, at]
         mixed[pl.ds(s * seq_len, seq_len), pl.ds(h * DH, DH)] = dot(p, val, 1, 0)
 
 
-def stats_kernel(length, mixed, vgo, vgp, co, cp, prod, stats):
+def stats_kernel(length, mixed, vgo, bp, co, cp, prod, stats):
     seq_len = co.shape[0]
     prod[:seq_len, :] = vgo[:, HALF:].astype(F32) * co[...].astype(F32)
-    prod[seq_len:, :] = vgp[:, HALF:].astype(F32) * cp[...].astype(F32)
+    prod[seq_len:, :] = bp[seq_len : 2 * seq_len, HALF:].astype(F32) * cp[...].astype(F32)
     lane = lax.broadcasted_iota(jnp.int32, (seq_len, 128), 1)
     row = lax.broadcasted_iota(jnp.int32, (seq_len, 128), 0)
     live = jnp.where(row < length[0, 0], 1.0, 0.0)
@@ -187,7 +193,7 @@
         stats[:, own] = packed.T[:8, :]
 
 
-def backward_kernel(far, xt, act, slope, prob, dprob, mixed, mine, theirs, vgo, vgp, prod, co, cp, *refs):
+def backward_kernel(far, xt, act, slope, prob, dprob, mixed, mine, theirs, vgo, bp, prod, co, cp, *refs):
     gpre, own_grads, far_grads, *terms = refs
     seq_len = co.shape[0]
     grad_refs = own_grads, far_grads
@@ -209,7 +215,7 @@
         mean, rate, c1, c2 = (cols[:, i : i + 1] for i in range(4))
         for h in range(HL):
             local = pl.ds(h * DH, DH)
-            val, cot = (vgp[:, local], cp[:, local]) if s else (vgo[:, local], co[:, local])
+            val, cot = (bp[pl.ds(seq_len, seq_len), local], cp[:, local]) if s else (vgo[:, local], co[:, local])
             normed = (mixed[own, local] - mean) * rate
             grad_refs[s][:, pl.ds(HALF + h * DH, DH)] = (normed * cot.astype(F32)).astype(BF)
             dmix = (rate * (prod[own, local] - c1 - normed * c2)).astype(BF)
@@ -245,11 +251,12 @@
     out_far[...] = far[...].astype(F32) + y[...].astype(F32)
 
 
-def input_kernel(blocks, *refs):
+def input_kernel(blocks, mine, bp, *refs):
     *pieces, gpre, own_out, other_out, block = refs
     me = lax.axis_index("dp")
-    rows = pieces[0].shape[0]
+    rows = mine.shape[0]
     seq_len = own_out.shape[0]
+    pieces = [mine, bp.at[pl.ds(2 * seq_len, rows), :], *pieces]
     done = 0
     for masks in blocks:
         fill_block(me, masks, pieces[done : done + len(masks)], block)
@@ -305,44 +312,41 @@
         return lax.dynamic_slice_in_dim(x, c * HALF, HALF, 1)
 
     def held(some):
-        return [pieces[m] for masks in some for m in masks]
-
-    low = jnp.concatenate([shard[:, :HALF], shard[:, F : F + HALF]], 1)
-    high = jnp.concatenate([shard[:, HALF:F], shard[:, F + HALF :]], 1)
-    mine = jnp.where(core == 0, low, high)
-    other = jnp.where(core == 0, high, low)
+        return [pieces[m] for masks in some for m in masks if m != 1]
+
+    mine, other = (jnp.concatenate([half(shard[:, :F], c), half(shard[:, F:], c)], 1) for c in (core, 1 - core))
+    bundle, vgo = call(
+        pack_kernel, 0.001, [like((two + rows, F), BF), like((seq_len, F), BF)], other, xo, vo, go
+    )
     pieces = {0: mine}
-    pieces[1] = pair(other, 1)
     pieces[2] = pair(mine, 2)
     pieces[5] = pair(other, 5)
-    xp = pair(after(xo, mine), 1)
-    xo, vgo, vgp = call(pack_kernel, 0.001, [like((seq_len, F), BF)] * 3, xo, vo, go)
-    cp = from_next(half(after(grads, pieces[1]), 1 - core), 1)
-    co = from_next(half(after(grads, pieces[1]), core))
-    vgp = pair(vgp, 1)
-    pieces[3] = pair(after(other, xp, pieces[1], vgp), 3)
-    pieces[4] = pair(after(mine, xp, pieces[1], vgp), 4)
-
+    partner = pair(after(bundle, mine), 1)
+    cp = from_next(half(after(grads, partner), 1 - core), 1)
+    co = from_next(half(after(grads, partner), core))
+    pieces[3] = pair(after(other, partner), 3)
+    pieces[4] = pair(after(mine, partner), 4)
     xt = call(
         functools.partial(turn_kernel, count),
         10,
         like((depth, two), BF),
-        xo,
-        xp,
+        bundle,
+        partner,
         scratch=[pltpu.VMEM((depth, two), BF)],
     )
     pieces[6] = pair(pieces[2], 4)
     pieces[7] = pair(pieces[5], 2)
+    pieces[1] = partner[two:]
     bit = 8
     while bit < count:
         for m in range(bit):
             pieces[m + bit] = pair(pieces[m], bit)
         bit *= 2
     first = functools.partial(pre_kernel, blocks[:1], False)
-    pre = call(first, 0.001, like((two, F), F32), xo, xp, *held(blocks[:1]), scratch=[block])
+    pre = call(first, 0.001, like((two, F), F32), bundle, partner, *held(blocks[:1]), scratch=[block])
     more = functools.partial(pre_kernel, blocks[1:-1], True)
-    pre = call(more, 0.001, like((two, F), F32), xo, xp, pre, *held(blocks[1:-1]), scratch=[block])
-    cp, pre = lax.optimization_barrier((cp, pre))
+    pre = call(more, 0.001, like((two, F), F32), bundle, partner, pre, *held(blocks[1:-1]), scratch=[block])
+    co, pre = lax.optimization_barrier((co, pre))
     act, slope, prob, dprob, mixed = call(
         functools.partial(forward_kernel, blocks[-1]),
         0.001,
@@ -353,17 +357,16 @@
             like((2 * HL, seq_len, seq_len), BF),
             like((two, HALF), F32),
         ],
-        xo,
-        xp,
+        bundle,
+        partner,
         pre,
         vgo,
-        vgp,
         *held(blocks[-1:]),
         scratch=[block],
     )
     prod, stats = call(
         stats_kernel,
-        1, [like((two, HALF), F32), like((8, two), F32)], lengths, mixed, vgo, vgp, co, cp
+        1, [like((two, HALF), F32), like((8, two), F32)], lengths, mixed, vgo, partner, co, cp
     )
     theirs = pair(stats, 1)
 
@@ -382,7 +385,7 @@
         stats,
         theirs,
         vgo,
-        vgp,
+        partner,
         prod,
         co,
         cp,
@@ -390,7 +393,7 @@
     diagonal = halve(dict(zip(far, terms)), count)
     far_g = pair(far_g, 1)
     by_x, by_y = lax.optimization_barrier((pair(diagonal[6], 2), pair(diagonal[7], 4)))
-    terms = call(functools.partial(term_kernel, near), 0.1, [like((rows, F), BF)] * len(near), xt, gpre)
+    terms = call(functools.partial(term_kernel, near), 1, [like((rows, F), BF)] * len(near), xt, gpre)
     t = halve(dict(zip(near, terms)), count)
     x_r, y_r = lax.optimization_barrier((pair(t[2], 2), pair(t[5], 5)))
     far_t = pair(after(t[1], far_g), 1)
@@ -399,7 +402,9 @@
         functools.partial(input_kernel, blocks),
         10,
         [like((seq_len, depth), F32), like((seq_len, depth), BF)],
-        *held(blocks),
+        mine,
+        partner,
+        *held(blocks)[1:],
         gpre,
         scratch=[block],
     )

time: 57 us -> 53.9 us (0.946)
  starting transfers between devices: 20 us -> 24.7 us
  waiting for transfers between devices: 18.5 us -> 14.3 us
  Pallas kernels: 13.7 us -> 11.8 us
  local copies, waits for them, and re-layouts: 2.32 us -> 1.43 us
  other arithmetic: 0.81 us -> 0.04 us
    ppermute x19 -> x17, starting transfers between devices: 13.2 us -> 16.8 us  [pair(): return lax.ppermute(x, 'dp', [(i, i ^ mask) for i in range(count)])]
    ppermute x19 -> x17, waiting for transfers between devices: 17 us -> 14.2 us  [pair(): return lax.ppermute(x, 'dp', [(i, i ^ mask) for i in range(count)])]
    pallas_call x14, Pallas kernels: 13.7 us -> 11.8 us  [call(): pl.pallas_call(body, out_shape=out_shape, in_specs=[SMEM if x.dtype == jn...]
    ppermute x2, waiting for transfers between devices: 1.49 us -> 0.03 us  [from_next(): lax.ppermute(x, ('dp', 'segment'), [(i * seg + s, (i ^ mask) * seg + (s -...]
    ppermute x2, starting transfers between devices: 6.87 us -> 7.96 us  [from_next(): lax.ppermute(x, ('dp', 'segment'), [(i * seg + s, (i ^ mask) * seg + (s -...]
    dynamic_slice x1 -> x2, local copies, waits for them, and re-layouts: 1.06 us -> 0.08 us  [half(): return lax.dynamic_slice_in_dim(x, c * HALF, HALF, 1)]
    select_n x1 -> x0, other arithmetic: 0.81 us -> none  [on_device(): other = jnp.where(core == 0, high, low)]
  transfers between devices with their start and end apart: 21 -> 19, of which waited for: 8 -> 9; matrix products, arithmetic and copies ran while one was open for 2% -> 0% of each run, Pallas kernels for 17% -> 15%
where the time goes in v4:
time: 53.9 us; the launch traced here: 53.7 us
  starting transfers between devices  24.7 us (46%)
  waiting for transfers between devices  14.3 us (27%)
  Pallas kernels  11.8 us (22%)
  between operations  1.51 us (3%)
  local copies, waits for them, and re-layouts  1.43 us (3%)
    ppermute x17, starting transfers between devices, pair(): return lax.ppermute(x, 'dp', [(i, i ^ mask) for i in range(count)])  16.8 us
    ppermute x17, waiting for transfers between devices, pair(): return lax.ppermute(x, 'dp', [(i, i ^ mask) for i in range(count)])  14.2 us
    pallas_call x14, Pallas kernels, call(): pl.pallas_call(body, out_shape=out_shape, in_specs=[SMEM if x.dtype == jn...  11.8 us
    ppermute x2, starting transfers between devices, from_next(): lax.ppermute(x, ('dp', 'segment'), [(i * seg + s, (i ^ mask) * seg + (s -...  7.96 us
    slice x1, local copies, waits for them, and re-layouts, on_device(): shard[:, :F]  1.18 us
  transfers between devices with their start and end apart: 19, of which 9 were waited for; matrix products, arithmetic and copies ran while one was open for 0% of the time, Pallas kernels for 15%

profile of v4, /device:TPU:0, one launch (start us, length us, event | category | flops | bytes accessed | tf_op | source)
XLA Modules:
  0.0 53.7 jit_solution(3822712550631657600)
XLA Ops:
  0.7 1.2 %fusion = (bf16[128,1024]{1,0:T(8,128)(2,1)S(1)}, bf16[128,1024]{1,0:T(8,128)(2,1)S(1)}) fusion(bf16[128,2048]{1,0:T(8,128)(2,1)} %bitcast.13), kind=kLoop, calls=%fused_computation.8 | loop fusion | bytes 1048576 | tf_op jit(solution)/shard_map/slice | solution.py:317
  1.9 0.0 copy-start.3
  2.0 0.0 copy-done.1
  2.0 0.2 copy-done
  2.2 0.1 shard_map.93
  2.3 0.5 collective-permute-start
  2.8 2.6 %collective-permute-start.1 = (bf16[128,1024]{1,0:T(8,128)(2,1)S(1)}, bf16[128,1024]{1,0:T(8,128)(2,1)S(1)}, u32[]{:S(2)}, u32[]{:S(2)}) collective-permute-start(bf16[128,1024]{1,0:T(8,128)(2,1)S(1)} %pad_maximum_fusion.refs_0_.mine), channel_id=1, source_target_pairs={{0,8},{4,12},{8,0},{12,4},{16,24},{20,28},{24,16},{28,20},{1,9},{5... | collective-permute-start | bytes 786440 | tf_op jit(solution)/shard_map/ppermute | solution.py:28
  5.4 1.3 %collective-permute-start.4 = (bf16[128,1024]{1,0:T(8,128)(2,1)S(1)}, bf16[128,1024]{1,0:T(8,128)(2,1)S(1)}, u32[]{:S(2)}, u32[]{:S(2)}) collective-permute-start(bf16[128,1024]{1,0:T(8,128)(2,1)S(1)} %pad_maximum_fusion.1.other), channel_id=1, source_target_pairs={{0,20},{4,16},{8,28},{12,24},{16,4},{20,0},{24,12},{28,8},{1,21},{... | collective-permute-start | bytes 786440 | tf_op jit(solution)/shard_map/ppermute | solution.py:28
  6.6 1.4 %collective-permute-start.2 = (bf16[128,1024]{1,0:T(8,128)(2,1)S(1)}, bf16[128,1024]{1,0:T(8,128)(2,1)S(1)}, u32[]{:S(2)}, u32[]{:S(2)}) collective-permute-start(bf16[128,1024]{1,0:T(8,128)(2,1)S(1)} %pad_maximum_fusion.1.other), channel_id=1, source_target_pairs={{0,12},{4,8},{8,4},{12,0},{16,28},{20,24},{24,20},{28,16},{1,13},{... | collective-permute-start | bytes 786440 | tf_op jit(solution)/shard_map/ppermute | solution.py:28
  8.1 1.5 %collective-permute-start.3 = (bf16[128,1024]{1,0:T(8,128)(2,1)S(1)}, bf16[128,1024]{1,0:T(8,128)(2,1)S(1)}, u32[]{:S(2)}, u32[]{:S(2)}) collective-permute-start(bf16[128,1024]{1,0:T(8,128)(2,1)S(1)} %pad_maximum_fusion.refs_0_.mine), channel_id=1, source_target_pairs={{0,16},{4,20},{8,24},{12,28},{16,0},{20,4},{24,8},{28,12},{1,17},{... | collective-permute-start | bytes 786440 | tf_op jit(solution)/shard_map/ppermute | solution.py:28
  9.6 3.7 %collective-permute-start.7 = (bf16[256,512]{1,0:T(8,128)(2,1)S(1)}, bf16[256,512]{1,0:T(8,128)(2,1)S(1)}, u32[]{:S(2)}, u32[]{:S(2)}) collective-permute-start(bf16[256,512]{1,0:T(8,128)(2,1)S(1)} %get-tuple-element.91), channel_id=1, source_target_pairs={{0,3},{1,0},{2,1},{3,2},{4,7},{5,4},{6,5},{7,6},{8,11},{9,8},{10,9... | collective-permute-start | bytes 786440 | tf_op jit(solution)/shard_map/ppermute | solution.py:33
  13.3 1.2 %collective-permute-start.5 = (bf16[128,1024]{1,0:T(8,128)(2,1)S(1)}, bf16[128,1024]{1,0:T(8,128)(2,1)S(1)}, u32[]{:S(2)}, u32[]{:S(2)}) collective-permute-start(bf16[128,1024]{1,0:T(8,128)(2,1)S(1)} %collective-permute-done.1.refs_1_.refs_0_), channel_id=1, source_target_pairs={{0,16},{4,20},{8,24},{12,28},{16,0},{20,4},{24,8},{28,12},{1,17},{... | collective-permute-start | bytes 786440 | tf_op jit(solution)/shard_map/ppermute | solution.py:28
  14.5 1.5 %collective-permute-start.6 = (bf16[128,1024]{1,0:T(8,128)(2,1)S(1)}, bf16[128,1024]{1,0:T(8,128)(2,1)S(1)}, u32[]{:S(2)}, u32[]{:S(2)}) collective-permute-start(bf16[128,1024]{1,0:T(8,128)(2,1)S(1)} %collective-permute-done.4.refs_4_.refs_3_), channel_id=1, source_target_pairs={{0,8},{4,12},{8,0},{12,4},{16,24},{20,28},{24,16},{28,20},{1,9},{5... | collective-permute-start | bytes 786440 | tf_op jit(solution)/shard_map/ppermute | solution.py:28
  16.0 1.6 %collective-permute-done.2.refs_2_.refs_1_ = bf16[128,1024]{1,0:T(8,128)(2,1)S(1)} collective-permute-done((bf16[128,1024]{1,0:T(8,128)(2,1)S(1)}, bf16[128,1024]{1,0:T(8,128)(2,1)S(1)}, u32[]{:S(2)}, u32[]{:S(2)}) %collective-permute-start.2) | collective-permute-done | bytes 262176 | tf_op jit(solution)/shard_map/ppermute | solution.py:28
  17.6 4.3 %collective-permute-start.8 = (bf16[256,512]{1,0:T(8,128)(2,1)S(1)}, bf16[256,512]{1,0:T(8,128)(2,1)S(1)}, u32[]{:S(2)}, u32[]{:S(2)}) collective-permute-start(bf16[256,512]{1,0:T(8,128)(2,1)S(1)} %get-tuple-element.90), channel_id=1, source_target_pairs={{0,7},{1,4},{2,5},{3,6},{4,3},{5,0},{6,1},{7,2},{8,15},{9,12},{10,... | collective-permute-start | bytes 786440 | tf_op jit(solution)/shard_map/ppermute | solution.py:33
  22.6 0.5 shard_map.95.refs_0_
  23.1 0.9 %shard_map.96.prev = f32[512,1024]{1,0:T(8,128)S(1)} custom-call(bf16[640,1024]{1,0:T(8,128)(2,1)S(1)} %get-tuple-element.48.bo, bf16[640,1024]{1,0:T(8,128)(2,1)S(1)} %collective-permute-done.bp, f32[512,1024]{1,0:T(8,128)S(1)} %shard_map.95.refs_0_, bf16[128,1024]{1,0:T(8,128)(2,1)S(1)} %collective-permute-done.1.refs_1_.refs_0_, ...), custom_call_target="tpu_custom_call" | custom-call | flops 1000000 | bytes 1000000 | tf_op jit(solution)/shard_map/pallas_call | solution.py:41
  23.9 0.0 collective-permute-done.7.co
  23.9 1.3 %collective-permute-done.5.refs_0_.refs_4_ = bf16[128,1024]{1,0:T(8,128)(2,1)S(1)} collective-permute-done((bf16[128,1024]{1,0:T(8,128)(2,1)S(1)}, bf16[128,1024]{1,0:T(8,128)(2,1)S(1)}, u32[]{:S(2)}, u32[]{:S(2)}) %collective-permute-start.5) | collective-permute-done | bytes 262176 | tf_op jit(solution)/shard_map/ppermute | solution.py:28
  25.2 2.2 %shard_map.97 = (bf16[512,1024]{1,0:T(8,128)(2,1)S(1)}, f32[512,1024]{1,0:T(8,128)S(1)}, bf16[8,256,256]{2,1,0:T(8,128)(2,1)S(1)}, bf16[8,256,256]{2,1,0:T(8,128)(2,1)S(1)}, f32[512,512]{1,0:T(8,128)S(1)}) custom-call(bf16[640,1024]{1,0:T(8,128)(2,1)S(1)} %get-tuple-element.48.bo, bf16[640,1024]{1,0:T(8,128)(2,1)S(1)} %collective-permute-done.bp, ...), custom_call_target="tpu_custom_call" | custom-call | flops 1000000 | bytes 1000000 | tf_op jit(solution)/shard_map/pallas_call | solution.py:41
  27.4 0.0 collective-permute-done.8.cp
  27.4 0.6 %shard_map.98 = (f32[512,512]{1,0:T(8,128)S(1)}, f32[8,512]{1,0:T(8,128)S(1)}) custom-call(s32[1,1]{1,0:T(1,128)S(6)} %copy.10.length, f32[512,512]{1,0:T(8,128)S(1)} %get-tuple-element.58.mixed, bf16[256,1024]{1,0:T(8,128)(2,1)S(1)} %get-tuple-element.53.vgo, bf16[640,1024]{1,0:T(8,128)(2,1)S(1)} %collective-permute-done.bp, ...), custom_call_target="tpu_custom_call" | custom-call | flops 1000000000 | bytes 1000000000 | tf_op jit(solution)/shard_map/pallas_call | solution.py:41
  28.0 0.0 collective-permute-start.9
  28.0 0.4 shard_map.94.xt
  28.4 0.8 %collective-permute-done.9.theirs = f32[8,512]{1,0:T(8,128)S(1)} collective-permute-done((f32[8,512]{1,0:T(8,128)S(1)}, f32[8,512]{1,0:T(8,128)S(1)}, u32[]{:S(2)}, u32[]{:S(2)}) %collective-permute-start.9) | collective-permute-done | bytes 16416 | tf_op jit(solution)/shard_map/ppermute | solution.py:28
  29.2 2.2 %shard_map.99 = (bf16[512,1024]{1,0:T(8,128)(2,1)S(1)}, bf16[256,1024]{1,0:T(8,128)(2,1)S(1)}, bf16[256,1024]{1,0:T(8,128)(2,1)S(1)}, bf16[128,1024]{1,0:T(8,128)(2,1)S(1)}, bf16[128,1024]{1,0:T(8,128)(2,1)S(1)}) custom-call(bf16[1024,512]{1,0:T(8,128)(2,1)S(1)} %shard_map.94.xt, bf16[512,1024]{1,0:T(8,128)(2,1)S(1)} %get-tuple-element.54.act, ...), custom_call_target="tpu_custom_call" | custom-call | flops 100000000 | bytes 100000000 | tf_op jit(solution)/shard_map/pallas_call | solution.py:41
  31.4 0.2 collective-permute-start.10
  31.7 1.5 %collective-permute-start.15 = (bf16[128,1024]{1,0:T(8,128)(2,1)S(1)}, bf16[128,1024]{1,0:T(8,128)(2,1)S(1)}, u32[]{:S(2)}, u32[]{:S(2)}) collective-permute-start(bf16[128,1024]{1,0:T(8,128)(2,1)S(1)} %get-tuple-element.80), channel_id=1, source_target_pairs={{0,8},{4,12},{8,0},{12,4},{16,24},{20,28},{24,16},{28,20},{1,9},{5... | collective-permute-start | bytes 786440 | tf_op jit(solution)/shard_map/ppermute | solution.py:28
  33.2 1.5 %collective-permute-start.16 = (bf16[128,1024]{1,0:T(8,128)(2,1)S(1)}, bf16[128,1024]{1,0:T(8,128)(2,1)S(1)}, u32[]{:S(2)}, u32[]{:S(2)}) collective-permute-start(bf16[128,1024]{1,0:T(8,128)(2,1)S(1)} %get-tuple-element.81), channel_id=1, source_target_pairs={{0,16},{4,20},{8,24},{12,28},{16,0},{20,4},{24,8},{28,12},{1,17},{... | collective-permute-start | bytes 786440 | tf_op jit(solution)/shard_map/ppermute | solution.py:28
  34.7 1.0 %shard_map.101 = (bf16[128,1024]{1,0:T(8,128)(2,1)S(1)}, bf16[128,1024]{1,0:T(8,128)(2,1)S(1)}, bf16[128,1024]{1,0:T(8,128)(2,1)S(1)}, bf16[128,1024]{1,0:T(8,12...) custom-call(bf16[1024,512]{1,0:T(8,128)(2,1)S(1)} %shard_map.94.xt, ...), custom_call_target="tpu_custom_call" | custom-call | flops 1000000000 | bytes 1000000000 | tf_op jit(solution)/shard_map/pallas_call | solution.py:41
  35.7 0.1 collective-permute-start.11
  35.7 1.4 %shard_map.100 = (f32[256,1024]{1,0:T(8,128)S(1)}, bf16[256,1024]{1,0:T(8,128)(2,1)S(1)}) custom-call(bf16[128,1024]{1,0:T(8,128)(2,1)S(1)} %pad_maximum_fusion.refs_0_.mine, bf16[640,1024]{1,0:T(8,128)(2,1)S(1)} %collective-permute-done.bp, bf16[128,1024]{1,0:T(8,128)(2,1)S(1)} %collective-permute-done.1.refs_1_.refs_0_, ...), custom_call_target="tpu_custom_call" | custom-call | flops 10000000000 | bytes 10000000000 | tf_op jit(solution)/shard_map/pallas_call | solution.py:41
  37.2 0.1 collective-permute-done.11.far
  37.3 0.4 collective-permute-start.12
  37.7 0.5 collective-permute-start.13
  38.3 2.0 %collective-permute-done.15.added = bf16[128,1024]{1,0:T(8,128)(2,1)S(1)} collective-permute-done((bf16[128,1024]{1,0:T(8,128)(2,1)S(1)}, bf16[128,1024]{1,0:T(8,128)(2,1)S(1)}, u32[]{:S(2)}, u32[]{:S(2)}) %collective-permute-start.15) | collective-permute-done | bytes 262176 | tf_op jit(solution)/shard_map/ppermute | solution.py:28
  40.2 1.3 %collective-permute-done.16.added = bf16[128,1024]{1,0:T(8,128)(2,1)S(1)} collective-permute-done((bf16[128,1024]{1,0:T(8,128)(2,1)S(1)}, bf16[128,1024]{1,0:T(8,128)(2,1)S(1)}, u32[]{:S(2)}, u32[]{:S(2)}) %collective-permute-start.16) | collective-permute-done | bytes 262176 | tf_op jit(solution)/shard_map/ppermute | solution.py:28
  41.6 0.1 shard_map.104
  41.6 2.3 %collective-permute-start.17 = (bf16[128,1024]{1,0:T(8,128)(2,1)S(1)}, bf16[128,1024]{1,0:T(8,128)(2,1)S(1)}, u32[]{:S(2)}, u32[]{:S(2)}) collective-permute-start(bf16[128,1024]{1,0:T(8,128)(2,1)S(1)} %shard_map.104), channel_id=1, source_target_pairs={{0,16},{4,20},{8,24},{12,28},{16,0},{20,4},{24,8},{28,12},{1,17},{... | collective-permute-start | bytes 786440 | tf_op jit(solution)/shard_map/ppermute | solution.py:28
  44.0 0.1 shard_map.105
  44.0 0.1 collective-permute-start.18
  44.1 1.9 %collective-permute-done.13.x = bf16[128,1024]{1,0:T(8,128)(2,1)S(1)} collective-permute-done((bf16[128,1024]{1,0:T(8,128)(2,1)S(1)}, bf16[128,1024]{1,0:T(8,128)(2,1)S(1)}, u32[]{:S(2)}, u32[]{:S(2)}) %collective-permute-start.13) | collective-permute-done | bytes 262176 | tf_op jit(solution)/shard_map/ppermute | solution.py:28
  46.0 1.0 %collective-permute-done.14.y = bf16[128,1024]{1,0:T(8,128)(2,1)S(1)} collective-permute-done((bf16[128,1024]{1,0:T(8,128)(2,1)S(1)}, bf16[128,1024]{1,0:T(8,128)(2,1)S(1)}, u32[]{:S(2)}, u32[]{:S(2)}) %collective-permute-start.14) | collective-permute-done | bytes 262176 | tf_op jit(solution)/shard_map/ppermute | solution.py:28
  47.0 0.1 shard_map.103
  47.1 1.3 %shard_map.102 = (bf16[256,1024]{1,0:T(8,128)(2,1)}, bf16[256,1024]{1,0:T(8,128)(2,1)}, bf16[256,1024]{1,0:T(8,128)(2,1)}) custom-call(f32[256,1024]{1,0:T(8,128)S(1)} %get-tuple-element.63.gi_o, bf16[256,1024]{1,0:T(8,128)(2,1)S(1)} %collective-permute-done.12.gi_r, bf16[256,1024]{1,0:T(8,128)(2,1)S(1)} %get-tuple-element.69.own, ...), custom_call_target="tpu_custom_call" | custom-call | flops 300000000 | bytes 300000000 | tf_op jit(solution)/shard_map/pallas_call | solution.py:41
  48.4 4.3 %collective-permute-done.17.x = bf16[128,1024]{1,0:T(8,128)(2,1)S(1)} collective-permute-done((bf16[128,1024]{1,0:T(8,128)(2,1)S(1)}, bf16[128,1024]{1,0:T(8,128)(2,1)S(1)}, u32[]{:S(2)}, u32[]{:S(2)}) %collective-permute-start.17) | collective-permute-done | bytes 262176 | tf_op jit(solution)/shard_map/ppermute | solution.py:28
  52.7 0.0 collective-permute-done.18.y
  52.7 1.1 %shard_map.106 = f32[128,2048]{1,0:T(8,128)} custom-call(f32[128,1024]{1,0:T(8,128)S(1)} %get-tuple-element.86.own, bf16[128,1024]{1,0:T(8,128)(2,1)S(1)} %collective-permute-done.17.x, f32[128,1024]{1,0:T(8,128)S(1)} %get-tuple-element.88.far, bf16[128,1024]{1,0:T(8,128)(2,1)S(1)} %collective-permute-done.18.y), custom_call_target="tpu_custom_call" | custom-call | flops 1000000000 | bytes 1000000000 | tf_op jit(solution)/shard_map/pallas_call | solution.py:41
  (17 shorter events, 0.2 us)
Async XLA Ops:
  0.6 1.3 %copy-start.2 = (bf16[1,1,256,1024]{3,2,1,0:T(8,128)(2,1)S(1)}, bf16[1,1,256,1024]{3,2,1,0:T(8,128)(2,1)}, u32[]{:S(2)}) copy-start(bf16[1,1,256,1024]{3,2,1,0:T(8,128)(2,1)} %param.8) | copy-start | bytes 1572868
  0.6 1.3 %copy-start.1 = (bf16[1,1,256,1024]{3,2,1,0:T(8,128)(2,1)S(1)}, bf16[1,1,256,1024]{3,2,1,0:T(8,128)(2,1)}, u32[]{:S(2)}) copy-start(bf16[1,1,256,1024]{3,2,1,0:T(8,128)(2,1)} %param.7) | copy-start | bytes 1572868
  0.7 1.5 %copy-start = (bf16[1,1,256,1024]{3,2,1,0:T(8,128)(2,1)S(1)}, bf16[1,1,256,1024]{3,2,1,0:T(8,128)(2,1)}, u32[]{:S(2)}) copy-start(bf16[1,1,256,1024]{3,2,1,0:T(8,128)(2,1)} %param.6) | copy-start | bytes 1572868
  1.9 7.7 %copy-start.3 = (bf16[1,1,256,1024]{3,2,1,0:T(8,128)(2,1)S(1)}, bf16[1,1,256,1024]{3,2,1,0:T(8,128)(2,1)}, u32[]{:S(2)}) copy-start(bf16[1,1,256,1024]{3,2,1,0:T(8,128)(2,1)} %param.9) | copy-start | bytes 1572868
  2.3 4.4 %collective-permute-start = (bf16[640,1024]{1,0:T(8,128)(2,1)S(1)}, bf16[640,1024]{1,0:T(8,128)(2,1)S(1)}, u32[]{:S(2)}, u32[]{:S(2)}) collective-permute-start(bf16[640,1024]{1,0:T(8,128)(2,1)S(1)} %get-tuple-element.48.bo), channel_id=1, source_target_pairs={{0,4},{4,0},{8,12},{12,8},{16,20},{20,16},{24,28},{28,24},{1,5},{5... | collective-permute-start | bytes 3932168 | tf_op jit(solution)/shard_map/ppermute | solution.py:28
  2.8 10.5 %collective-permute-start.1 = (bf16[128,1024]{1,0:T(8,128)(2,1)S(1)}, bf16[128,1024]{1,0:T(8,128)(2,1)S(1)}, u32[]{:S(2)}, u32[]{:S(2)}) collective-permute-start(bf16[128,1024]{1,0:T(8,128)(2,1)S(1)} %pad_maximum_fusion.refs_0_.mine), channel_id=1, source_target_pairs={{0,8},{4,12},{8,0},{12,4},{16,24},{20,28},{24,16},{28,20},{1,9},{5... | collective-permute-start | bytes 786440 | tf_op jit(solution)/shard_map/ppermute | solution.py:28
  5.4 9.1 %collective-permute-start.4 = (bf16[128,1024]{1,0:T(8,128)(2,1)S(1)}, bf16[128,1024]{1,0:T(8,128)(2,1)S(1)}, u32[]{:S(2)}, u32[]{:S(2)}) collective-permute-start(bf16[128,1024]{1,0:T(8,128)(2,1)S(1)} %pad_maximum_fusion.1.other), channel_id=1, source_target_pairs={{0,20},{4,16},{8,28},{12,24},{16,4},{20,0},{24,12},{28,8},{1,21},{... | collective-permute-start | bytes 786440 | tf_op jit(solution)/shard_map/ppermute | solution.py:28
  6.6 11.0 %collective-permute-start.2 = (bf16[128,1024]{1,0:T(8,128)(2,1)S(1)}, bf16[128,1024]{1,0:T(8,128)(2,1)S(1)}, u32[]{:S(2)}, u32[]{:S(2)}) collective-permute-start(bf16[128,1024]{1,0:T(8,128)(2,1)S(1)} %pad_maximum_fusion.1.other), channel_id=1, source_target_pairs={{0,12},{4,8},{8,4},{12,0},{16,28},{20,24},{24,20},{28,16},{1,13},{... | collective-permute-start | bytes 786440 | tf_op jit(solution)/shard_map/ppermute | solution.py:28
  8.1 15.0 %collective-permute-start.3 = (bf16[128,1024]{1,0:T(8,128)(2,1)S(1)}, bf16[128,1024]{1,0:T(8,128)(2,1)S(1)}, u32[]{:S(2)}, u32[]{:S(2)}) collective-permute-start(bf16[128,1024]{1,0:T(8,128)(2,1)S(1)} %pad_maximum_fusion.refs_0_.mine), channel_id=1, source_target_pairs={{0,16},{4,20},{8,24},{12,28},{16,0},{20,4},{24,8},{28,12},{1,17},{... | collective-permute-start | bytes 786440 | tf_op jit(solution)/shard_map/ppermute | solution.py:28
  9.6 14.3 %collective-permute-start.7 = (bf16[256,512]{1,0:T(8,128)(2,1)S(1)}, bf16[256,512]{1,0:T(8,128)(2,1)S(1)}, u32[]{:S(2)}, u32[]{:S(2)}) collective-permute-start(bf16[256,512]{1,0:T(8,128)(2,1)S(1)} %get-tuple-element.91), channel_id=1, source_target_pairs={{0,3},{1,0},{2,1},{3,2},{4,7},{5,4},{6,5},{7,6},{8,11},{9,8},{10,9... | collective-permute-start | bytes 786440 | tf_op jit(solution)/shard_map/ppermute | solution.py:33
  13.3 11.9 %collective-permute-start.5 = (bf16[128,1024]{1,0:T(8,128)(2,1)S(1)}, bf16[128,1024]{1,0:T(8,128)(2,1)S(1)}, u32[]{:S(2)}, u32[]{:S(2)}) collective-permute-start(bf16[128,1024]{1,0:T(8,128)(2,1)S(1)} %collective-permute-done.1.refs_1_.refs_0_), channel_id=1, source_target_pairs={{0,16},{4,20},{8,24},{12,28},{16,0},{20,4},{24,8},{28,12},{1,17},{... | collective-permute-start | bytes 786440 | tf_op jit(solution)/shard_map/ppermute | solution.py:28
  14.5 10.7 %collective-permute-start.6 = (bf16[128,1024]{1,0:T(8,128)(2,1)S(1)}, bf16[128,1024]{1,0:T(8,128)(2,1)S(1)}, u32[]{:S(2)}, u32[]{:S(2)}) collective-permute-start(bf16[128,1024]{1,0:T(8,128)(2,1)S(1)} %collective-permute-done.4.refs_4_.refs_3_), channel_id=1, source_target_pairs={{0,8},{4,12},{8,0},{12,4},{16,24},{20,28},{24,16},{28,20},{1,9},{5... | collective-permute-start | bytes 786440 | tf_op jit(solution)/shard_map/ppermute | solution.py:28
  17.6 9.8 %collective-permute-start.8 = (bf16[256,512]{1,0:T(8,128)(2,1)S(1)}, bf16[256,512]{1,0:T(8,128)(2,1)S(1)}, u32[]{:S(2)}, u32[]{:S(2)}) collective-permute-start(bf16[256,512]{1,0:T(8,128)(2,1)S(1)} %get-tuple-element.90), channel_id=1, source_target_pairs={{0,7},{1,4},{2,5},{3,6},{4,3},{5,0},{6,1},{7,2},{8,15},{9,12},{10,... | collective-permute-start | bytes 786440 | tf_op jit(solution)/shard_map/ppermute | solution.py:33
  28.0 1.2 %collective-permute-start.9 = (f32[8,512]{1,0:T(8,128)S(1)}, f32[8,512]{1,0:T(8,128)S(1)}, u32[]{:S(2)}, u32[]{:S(2)}) collective-permute-start(f32[8,512]{1,0:T(8,128)S(1)} %get-tuple-element.60.mine), channel_id=1, source_target_pairs={{0,4},{4,0},{8,12},{12,8},{16,20},{20,16},{24,28},{28,24},{1,5},{5... | collective-permute-start | bytes 49160 | tf_op jit(solution)/shard_map/ppermute | solution.py:28
  31.4 4.2 %collective-permute-start.10 = (bf16[256,1024]{1,0:T(8,128)(2,1)S(1)}, bf16[256,1024]{1,0:T(8,128)(2,1)S(1)}, u32[]{:S(2)}, u32[]{:S(2)}) collective-permute-start(bf16[256,1024]{1,0:T(8,128)(2,1)S(1)} %get-tuple-element.66), channel_id=1, source_target_pairs={{0,4},{4,0},{8,12},{12,8},{16,20},{20,16},{24,28},{28,24},{1,5},{5... | collective-permute-start | bytes 1572872 | tf_op jit(solution)/shard_map/ppermute | solution.py:28
  31.7 8.6 %collective-permute-start.15 = (bf16[128,1024]{1,0:T(8,128)(2,1)S(1)}, bf16[128,1024]{1,0:T(8,128)(2,1)S(1)}, u32[]{:S(2)}, u32[]{:S(2)}) collective-permute-start(bf16[128,1024]{1,0:T(8,128)(2,1)S(1)} %get-tuple-element.80), channel_id=1, source_target_pairs={{0,8},{4,12},{8,0},{12,4},{16,24},{20,28},{24,16},{28,20},{1,9},{5... | collective-permute-start | bytes 786440 | tf_op jit(solution)/shard_map/ppermute | solution.py:28
  33.2 8.4 %collective-permute-start.16 = (bf16[128,1024]{1,0:T(8,128)(2,1)S(1)}, bf16[128,1024]{1,0:T(8,128)(2,1)S(1)}, u32[]{:S(2)}, u32[]{:S(2)}) collective-permute-start(bf16[128,1024]{1,0:T(8,128)(2,1)S(1)} %get-tuple-element.81), channel_id=1, source_target_pairs={{0,16},{4,20},{8,24},{12,28},{16,0},{20,4},{24,8},{28,12},{1,17},{... | collective-permute-start | bytes 786440 | tf_op jit(solution)/shard_map/ppermute | solution.py:28
  35.7 1.6 %collective-permute-start.11 = (bf16[128,1024]{1,0:T(8,128)(2,1)S(1)}, bf16[128,1024]{1,0:T(8,128)(2,1)S(1)}, u32[]{:S(2)}, u32[]{:S(2)}) collective-permute-start(bf16[128,1024]{1,0:T(8,128)(2,1)S(1)} %get-tuple-element.67), channel_id=1, source_target_pairs={{0,4},{4,0},{8,12},{12,8},{16,20},{20,16},{24,28},{28,24},{1,5},{5... | collective-permute-start | bytes 786440 | tf_op jit(solution)/shard_map/ppermute | solution.py:28
  37.3 9.8 %collective-permute-start.12 = (bf16[256,1024]{1,0:T(8,128)(2,1)S(1)}, bf16[256,1024]{1,0:T(8,128)(2,1)S(1)}, u32[]{:S(2)}, u32[]{:S(2)}) collective-permute-start(bf16[256,1024]{1,0:T(8,128)(2,1)S(1)} %get-tuple-element.68), channel_id=1, source_target_pairs={{0,4},{4,0},{8,12},{12,8},{16,20},{20,16},{24,28},{28,24},{1,5},{5... | collective-permute-start | bytes 1572872 | tf_op jit(solution)/shard_map/ppermute | solution.py:28
  37.7 8.3 %collective-permute-start.13 = (bf16[128,1024]{1,0:T(8,128)(2,1)S(1)}, bf16[128,1024]{1,0:T(8,128)(2,1)S(1)}, u32[]{:S(2)}, u32[]{:S(2)}) collective-permute-start(bf16[128,1024]{1,0:T(8,128)(2,1)S(1)} %get-tuple-element.74), channel_id=1, source_target_pairs={{0,8},{4,12},{8,0},{12,4},{16,24},{20,28},{24,16},{28,20},{1,9},{5... | collective-permute-start | bytes 786440 | tf_op jit(solution)/shard_map/ppermute | solution.py:28
  38.3 8.7 %collective-permute-start.14 = (bf16[128,1024]{1,0:T(8,128)(2,1)S(1)}, bf16[128,1024]{1,0:T(8,128)(2,1)S(1)}, u32[]{:S(2)}, u32[]{:S(2)}) collective-permute-start(bf16[128,1024]{1,0:T(8,128)(2,1)S(1)} %get-tuple-element.75), channel_id=1, source_target_pairs={{0,20},{4,16},{8,28},{12,24},{16,4},{20,0},{24,12},{28,8},{1,21},{... | collective-permute-start | bytes 786440 | tf_op jit(solution)/shard_map/ppermute | solution.py:28
  41.6 11.0 %collective-permute-start.17 = (bf16[128,1024]{1,0:T(8,128)(2,1)S(1)}, bf16[128,1024]{1,0:T(8,128)(2,1)S(1)}, u32[]{:S(2)}, u32[]{:S(2)}) collective-permute-start(bf16[128,1024]{1,0:T(8,128)(2,1)S(1)} %shard_map.104), channel_id=1, source_target_pairs={{0,16},{4,20},{8,24},{12,28},{16,0},{20,4},{24,8},{28,12},{1,17},{... | collective-permute-start | bytes 786440 | tf_op jit(solution)/shard_map/ppermute | solution.py:28
  44.0 8.6 %collective-permute-start.18 = (bf16[128,1024]{1,0:T(8,128)(2,1)S(1)}, bf16[128,1024]{1,0:T(8,128)(2,1)S(1)}, u32[]{:S(2)}, u32[]{:S(2)}) collective-permute-start(bf16[128,1024]{1,0:T(8,128)(2,1)S(1)} %shard_map.105), channel_id=1, source_target_pairs={{0,12},{4,8},{8,4},{12,0},{16,28},{20,24},{24,20},{28,16},{1,13},{... | collective-permute-start | bytes 786440 | tf_op jit(solution)/shard_map/ppermute | solution.py:28

commit v5 on v4

--- a/solution.py
+++ b/solution.py
@@ -18,6 +18,7 @@
 BF = jnp.bfloat16
 F32 = jnp.float32
 UNIT = 1e9
+PARTS = 4
 
 VMEM = pl.BlockSpec(memory_space=pltpu.VMEM)
 SMEM = pl.BlockSpec(memory_space=pltpu.SMEM)
@@ -115,14 +116,30 @@
             pre[own, :] = part
 
 
-def gate(raw, scale):
-    sig = pltpu.reciprocal(1.0 + jnp.exp2(raw * (-scale * LOG2E)), approx=True)
-    out = raw * sig
-    return out, sig + (out * scale if scale != 1.0 else out) * (1.0 - sig)
+def sigmoid(raw, scale):
+    return pltpu.reciprocal(1.0 + jnp.exp2(raw * (-scale * LOG2E)), approx=True)
+
+
+def lower_half(upper, lower, causal):
+    top = causal.shape[0]
+    upper = jnp.where(causal, upper, 0.0).astype(BF)
+    right = jnp.where(causal, lower[:, top:], 0.0).astype(BF)
+    return jnp.concatenate(
+        [
+            jnp.concatenate([upper, jnp.zeros((top, top), BF)], 1),
+            jnp.concatenate([lower[:, :top].astype(BF), right], 1),
+        ],
+        0,
+    )
+
+
+def slope_kernel(act, sig, slope):
+    s = sig[...]
+    slope[...] = s + act[...].astype(F32) * (1.0 - s)
 
 
 def forward_kernel(masks, bo, bp, prev, vgo, *refs):
-    *pieces, act, slope, prob, dprob, mixed, block = refs
+    *pieces, act, sigs, prob, dprob, mixed, block = refs
     me = lax.axis_index("dp")
     seq_len = vgo.shape[0]
     top = seq_len // 2
@@ -132,11 +149,11 @@
     cols = ds(block_start(me, masks, rows), len(masks) * rows, len(masks) * rows)
     for s, x in ((0, bo), (1, bp)):
         own = pl.ds(s * seq_len, seq_len)
-        a, d = gate(prev[own, :] + dot(x[:seq_len, cols], block[...], 1, 0), 1.0)
-        act[own, :] = a.astype(BF)
-        slope[own, :] = d
+        v = prev[own, :] + dot(x[:seq_len, cols], block[...], 1, 0)
+        sig = sigmoid(v, 1.0)
+        sigs[own, :] = sig
+        act[own, :] = (v * sig).astype(BF)
     causal = lax.broadcasted_iota(jnp.int32, (top, top), 1) <= lax.broadcasted_iota(jnp.int32, (top, top), 0)
-    none = jnp.zeros((top, top), BF)
     units = [(s, h) for s in range(2) for h in range(HL)]
     raws = []
     for s, h in units:
@@ -144,24 +161,13 @@
         raws.append(dot(act[own, pl.ds(h * DH, DH)], act[own, pl.ds(HALF + h * DH, DH)], 1, 1))
     probs = []
     for (s, h), raw in zip(units, raws):
-        p0, d0 = gate(raw[:top, :top], SCALE)
-        p1, d1 = gate(raw[top:, :], SCALE)
-        p0, d0 = jnp.where(causal, p0, 0.0), jnp.where(causal, d0, 0.0)
-        p2, d2 = jnp.where(causal, p1[:, top:], 0.0), jnp.where(causal, d1[:, top:], 0.0)
-        whole = []
-        for upper, left, right in ((p0, p1, p2), (d0, d1, d2)):
-            whole.append(
-                jnp.concatenate(
-                    [
-                        jnp.concatenate([upper.astype(BF), none], 1),
-                        jnp.concatenate([left[:, :top].astype(BF), right.astype(BF)], 1),
-                    ],
-                    0,
-                )
-            )
-        probs.append(whole[0])
-        prob[s * HL + h] = whole[0]
-        dprob[s * HL + h] = whole[1]
+        halves = raw[:top, :top], raw[top:, :]
+        sigs_h = [sigmoid(x, SCALE) for x in halves]
+        outs = [x * sig for x, sig in zip(halves, sigs_h)]
+        p = lower_half(*outs, causal)
+        probs.append(p)
+        prob[s * HL + h] = p
+        dprob[s * HL + h] = lower_half(*(sig + o * SCALE * (1.0 - sig) for o, sig in zip(outs, sigs_h)), causal)
     for (s, h), p in zip(units, probs):
         at = pl.ds(h * DH, DH)
         val = bp[far, at] if s else vgo[:, at]
@@ -193,36 +199,38 @@
         stats[:, own] = packed.T[:8, :]
 
 
-def backward_kernel(far, xt, act, slope, prob, dprob, mixed, mine, theirs, vgo, bp, prod, co, cp, *refs):
-    gpre, own_grads, far_grads, *terms = refs
-    seq_len = co.shape[0]
-    grad_refs = own_grads, far_grads
+def row_factors(mine, theirs, s):
+    seq_len = mine.shape[1] // 2
+    a, b = mine[:, pl.ds(s * seq_len, seq_len)], theirs[:, pl.ds((1 - s) * seq_len, seq_len)]
+    mean = (a[0:1] + b[0:1]) * (1.0 / F)
+    mean_a, mean_b = a[0:1] * (1.0 / HALF), b[0:1] * (1.0 / HALF)
+    gap = mean_a - mean_b
+    variance = (a[1:2] + b[1:2] + gap * gap * (HALF * 0.5)) * (1.0 / F)
+    live = (b if s else a)[4:5] > 0.5
+    rate = jnp.where(live, SCALE * lax.rsqrt(variance * (SCALE * SCALE) + EPS), 0.0)
+    c1 = (a[2:3] + b[2:3]) * (1.0 / F)
+    cross = a[3:4] + b[3:4] + (mean_a - mean) * a[2:3] + (mean_b - mean) * b[2:3]
+    c2 = cross * rate * (1.0 / F)
+    cols = jnp.concatenate([mean, rate, c1, c2, mean, rate, c1, c2], 0).T
+    return [cols[:, i : i + 1] for i in range(4)]
+
+
+def backward_kernel(far, xt, act, slope, prob_slope, mixed, mine, theirs, vgo, bp, prod, *refs):
+    gpre, dmixed, *terms = refs
+    seq_len = vgo.shape[0]
     units = []
     for s in range(2):
         own = pl.ds(s * seq_len, seq_len)
-        other = pl.ds((1 - s) * seq_len, seq_len)
-        a, b = mine[:, own], theirs[:, other]
-        mean = (a[0:1] + b[0:1]) * (1.0 / F)
-        mean_a, mean_b = a[0:1] * (1.0 / HALF), b[0:1] * (1.0 / HALF)
-        gap = mean_a - mean_b
-        variance = (a[1:2] + b[1:2] + gap * gap * (HALF * 0.5)) * (1.0 / F)
-        live = (b if s else a)[4:5] > 0.5
-        rate = jnp.where(live, SCALE * lax.rsqrt(variance * (SCALE * SCALE) + EPS), 0.0)
-        c1 = (a[2:3] + b[2:3]) * (1.0 / F)
-        cross = a[3:4] + b[3:4] + (mean_a - mean) * a[2:3] + (mean_b - mean) * b[2:3]
-        c2 = cross * rate * (1.0 / F)
-        cols = jnp.concatenate([mean, rate, c1, c2, mean, rate, c1, c2], 0).T
-        mean, rate, c1, c2 = (cols[:, i : i + 1] for i in range(4))
+        mean, rate, c1, c2 = row_factors(mine, theirs, s)
         for h in range(HL):
             local = pl.ds(h * DH, DH)
-            val, cot = (bp[pl.ds(seq_len, seq_len), local], cp[:, local]) if s else (vgo[:, local], co[:, local])
+            val = bp[pl.ds(seq_len, seq_len), local] if s else vgo[:, local]
             normed = (mixed[own, local] - mean) * rate
-            grad_refs[s][:, pl.ds(HALF + h * DH, DH)] = (normed * cot.astype(F32)).astype(BF)
             dmix = (rate * (prod[own, local] - c1 - normed * c2)).astype(BF)
+            dmixed[own, local] = dmix
             units.append((own, h, s * HL + h, val, dmix))
-    dscores = [dot(dmix, val, 1, 1).astype(BF) * dprob[u] for _, _, u, val, dmix in units]
-    for (own, h, u, _, dmix), dscore in zip(units, dscores):
-        grad_refs[u // HL][:, pl.ds(h * DH, DH)] = dot(prob[u], dmix, 0, 0).astype(BF)
+    dscores = [dot(dmix, val, 1, 1).astype(BF) * prob_slope[u] for _, _, u, val, dmix in units]
+    for (own, h, _, _, _), dscore in zip(units, dscores):
         q_at, k_at = pl.ds(h * DH, DH), pl.ds(HALF + h * DH, DH)
         dq = dot(dscore, act[own, k_at], 1, 0)
         dk = dot(dscore, act[own, q_at], 0, 0)
@@ -231,6 +239,17 @@
     rows = terms[0].shape[0]
     for m, term in zip(far, terms):
         term[...] = dot(xt[m * rows : (m + 1) * rows, :], gpre[...], 1, 0).astype(BF)
+
+
+def grad_kernel(prob, dmixed, mixed, mine, theirs, co, cp, own_grads, far_grads):
+    seq_len = co.shape[0]
+    for s, (cot, out) in enumerate(((co, own_grads), (cp, far_grads))):
+        own = pl.ds(s * seq_len, seq_len)
+        mean, rate, _, _ = row_factors(mine, theirs, s)
+        out[:, HALF:] = ((mixed[own, :] - mean) * rate * cot[...].astype(F32)).astype(BF)
+        for h in range(HL):
+            at = pl.ds(h * DH, DH)
+            out[:, at] = dot(prob[s * HL + h], dmixed[own, at], 0, 0).astype(BF)
 
 
 def term_kernel(near, xt, gpre, *terms):
@@ -274,12 +293,20 @@
             out[:, ds(c * HALF, HALF, HALF)] = ref[:, pl.ds(i * HALF, HALF)]
 
 
-def weight_kernel(own, x, far, y, out):
+def weight_kernel(own, x, far, y, out, whole, sems):
     core = lax.rem(lax.axis_index("dp"), 2)
-    for c, near, added in ((core, own, x), (1 - core, far, y)):
-        for side in range(2):
-            at = pl.ds(side * HALF, HALF)
-            out[:, ds(side * F + c * HALF, HALF, HALF)] = near[:, at] + added[:, at].astype(F32)
+    rows = own.shape[0] // PARTS
+    copies = []
+    for i in range(PARTS):
+        block = pl.ds(i * rows, rows)
+        for c, near, added in ((core, own, x), (1 - core, far, y)):
+            for side in range(2):
+                at = pl.ds(side * HALF, HALF)
+                whole[block, ds(side * F + c * HALF, HALF, HALF)] = near[block, at] + added[block, at].astype(F32)
+        copies.append(pltpu.make_async_copy(whole.at[block, :], out.at[block, :], sems.at[i]))
+        copies[-1].start()
+    for copy in copies:
+        copy.wait()
 
 
 def like(shape, kind):
@@ -328,7 +355,7 @@
     pieces[4] = pair(after(mine, partner), 4)
     xt = call(
         functools.partial(turn_kernel, count),
-        10,
+        1,
         like((depth, two), BF),
         bundle,
         partner,
@@ -345,9 +372,9 @@
     first = functools.partial(pre_kernel, blocks[:1], False)
     pre = call(first, 0.001, like((two, F), F32), bundle, partner, *held(blocks[:1]), scratch=[block])
     more = functools.partial(pre_kernel, blocks[1:-1], True)
-    pre = call(more, 0.001, like((two, F), F32), bundle, partner, pre, *held(blocks[1:-1]), scratch=[block])
+    pre = call(more, 0.001, like((two, F), F32), bundle, partner, after(pre, xt), *held(blocks[1:-1]), scratch=[block])
     co, pre = lax.optimization_barrier((co, pre))
-    act, slope, prob, dprob, mixed = call(
+    act, sigs, prob, prob_slope, mixed = call(
         functools.partial(forward_kernel, blocks[-1]),
         0.001,
         [
@@ -369,35 +396,36 @@
         1, [like((two, HALF), F32), like((8, two), F32)], lengths, mixed, vgo, partner, co, cp
     )
     theirs = pair(stats, 1)
+    slope = call(slope_kernel, 0.3, like((two, F), F32), act, after(sigs, stats))
 
     far = [m for m in range(count) if m % 8 >= 6]
     near = [m for m in range(count) if m % 8 < 6]
-    gpre, own_g, far_g, *terms = call(
+    gpre, dmixed, *terms = call(
         functools.partial(backward_kernel, far),
         0.1,
-        [like((two, F), BF)] + [like((seq_len, F), BF)] * 2 + [like((rows, F), BF)] * len(far),
+        [like((two, F), BF), like((two, HALF), BF)] + [like((rows, F), BF)] * len(far),
         xt,
         act,
         slope,
-        prob,
-        dprob,
+        prob_slope,
         mixed,
         stats,
         theirs,
         vgo,
         partner,
         prod,
-        co,
-        cp,
     )
     diagonal = halve(dict(zip(far, terms)), count)
+    by_x, by_y = lax.optimization_barrier((pair(diagonal[6], 2), pair(diagonal[7], 4)))
+    terms = call(functools.partial(term_kernel, near), 10, [like((rows, F), BF)] * len(near), xt, gpre)
+    t = halve(dict(zip(near, terms)), count)
+    own_g, far_g = call(
+        grad_kernel, 3, [like((seq_len, F), BF)] * 2, prob, dmixed, mixed, stats, theirs, co, cp
+    )
     far_g = pair(far_g, 1)
-    by_x, by_y = lax.optimization_barrier((pair(diagonal[6], 2), pair(diagonal[7], 4)))
-    terms = call(functools.partial(term_kernel, near), 1, [like((rows, F), BF)] * len(near), xt, gpre)
-    t = halve(dict(zip(near, terms)), count)
     x_r, y_r = lax.optimization_barrier((pair(t[2], 2), pair(t[5], 5)))
     far_t = pair(after(t[1], far_g), 1)
-    near_own, near_far = call(near_kernel, 0.001, [like((rows, F), F32)] * 2, t[0], x_r, far_t, y_r)
+    near_own, near_far = call(near_kernel, 3, [like((rows, F), F32)] * 2, t[0], x_r, far_t, y_r)
     gi_o, gi_other = call(
         functools.partial(input_kernel, blocks),
         10,
@@ -416,7 +444,14 @@
     )
     sums = [near_own, pair(send_y, 4), near_far, pair(send_x, 3)]
     sums, _ = lax.optimization_barrier((sums, (grad_in, grad_val, grad_gate)))
-    grad_shard = call(weight_kernel, 1, like((rows, 2 * F), F32), *sums)
+    grad_shard = pl.pallas_call(
+        weight_kernel,
+        out_shape=like((rows, 2 * F), F32),
+        in_specs=[VMEM] * 4,
+        out_specs=pl.BlockSpec(memory_space=pl.ANY),
+        scratch_shapes=[pltpu.VMEM((rows, 2 * F), F32), pltpu.SemaphoreType.DMA((PARTS,))],
+        compiler_params=pltpu.CompilerParams(vmem_limit_bytes=20 << 20),
+    )(*sums)
     return (grad_in[None, None], grad_val[None, None], grad_gate[None, None], grad_shard[None])
 
 

time: 53.9 us -> 53.3 us (0.989)
  starting transfers between devices: 24.7 us -> 21.3 us
  waiting for transfers between devices: 14.3 us -> 16.6 us
    ppermute x17, waiting for transfers between devices: 14.2 us -> 16.6 us  [pair(): return lax.ppermute(x, 'dp', [(i, i ^ mask) for i in range(count)])]
    ppermute x17, starting transfers between devices: 16.8 us -> 15 us  [pair(): return lax.ppermute(x, 'dp', [(i, i ^ mask) for i in range(count)])]
    ppermute x2, starting transfers between devices: 7.96 us -> 6.33 us  [from_next(): lax.ppermute(x, ('dp', 'segment'), [(i * seg + s, (i ^ mask) * seg + (s -...]
    pallas_call x0 -> x1, Pallas kernels: none -> 1.03 us  [on_device(): pl.pallas_call(weight_kernel, out_shape=like((rows, 2 * F), F32), in_spec...]
    pallas_call x14 -> x15, Pallas kernels: 11.8 us -> 11.2 us  [call(): pl.pallas_call(body, out_shape=out_shape, in_specs=[SMEM if x.dtype == jn...]
  transfers between devices with their start and end apart: 19 -> 19, of which waited for: 9 -> 10; matrix products, arithmetic and copies ran while one was open for 0% -> 0% of each run, Pallas kernels for 15% -> 16%
where the time goes in v5:
time: 53.3 us; the launch traced here: 53.1 us
  starting transfers between devices  21.3 us (40%)
  waiting for transfers between devices  16.6 us (31%)
  Pallas kernels  12.2 us (23%)
  between operations  1.53 us (3%)
  local copies, waits for them, and re-layouts  1.43 us (3%)
    ppermute x17, waiting for transfers between devices, pair(): return lax.ppermute(x, 'dp', [(i, i ^ mask) for i in range(count)])  16.6 us
    ppermute x17, starting transfers between devices, pair(): return lax.ppermute(x, 'dp', [(i, i ^ mask) for i in range(count)])  15 us
    pallas_call x15, Pallas kernels, call(): pl.pallas_call(body, out_shape=out_shape, in_specs=[SMEM if x.dtype == jn...  11.2 us
    ppermute x2, starting transfers between devices, from_next(): lax.ppermute(x, ('dp', 'segment'), [(i * seg + s, (i ^ mask) * seg + (s -...  6.33 us
    slice x1, local copies, waits for them, and re-layouts, on_device(): shard[:, :F]  1.18 us
  transfers between devices with their start and end apart: 19, of which 10 were waited for; matrix products, arithmetic and copies ran while one was open for 0% of the time, Pallas kernels for 16%

profile of v5, /device:TPU:0, one launch (start us, length us, event | category | flops | bytes accessed | tf_op | source)
XLA Modules:
  0.0 53.1 jit_solution(11622821622328282849)
XLA Ops:
  0.7 1.2 %fusion = (bf16[128,1024]{1,0:T(8,128)(2,1)S(1)}, bf16[128,1024]{1,0:T(8,128)(2,1)S(1)}) fusion(bf16[128,2048]{1,0:T(8,128)(2,1)} %bitcast.14), kind=kLoop, calls=%fused_computation.8 | loop fusion | bytes 1048576 | tf_op jit(solution)/shard_map/slice | solution.py:344
  1.9 0.0 copy-start.3
  2.0 0.2 copy-done.2
  2.2 0.1 shard_map.93
  2.3 0.5 collective-permute-start
  2.8 2.6 %collective-permute-start.4 = (bf16[128,1024]{1,0:T(8,128)(2,1)S(1)}, bf16[128,1024]{1,0:T(8,128)(2,1)S(1)}, u32[]{:S(2)}, u32[]{:S(2)}) collective-permute-start(bf16[128,1024]{1,0:T(8,128)(2,1)S(1)} %pad_maximum_fusion.1.other), channel_id=1, source_target_pairs={{0,20},{4,16},{8,28},{12,24},{16,4},{20,0},{24,12},{28,8},{1,21},{... | collective-permute-start | bytes 786440 | tf_op jit(solution)/shard_map/ppermute | solution.py:29
  5.4 1.5 %collective-permute-start.1 = (bf16[128,1024]{1,0:T(8,128)(2,1)S(1)}, bf16[128,1024]{1,0:T(8,128)(2,1)S(1)}, u32[]{:S(2)}, u32[]{:S(2)}) collective-permute-start(bf16[128,1024]{1,0:T(8,128)(2,1)S(1)} %pad_maximum_fusion.refs_0_.mine), channel_id=1, source_target_pairs={{0,8},{4,12},{8,0},{12,4},{16,24},{20,28},{24,16},{28,20},{1,9},{5... | collective-permute-start | bytes 786440 | tf_op jit(solution)/shard_map/ppermute | solution.py:29
  6.9 1.4 %collective-permute-start.3 = (bf16[128,1024]{1,0:T(8,128)(2,1)S(1)}, bf16[128,1024]{1,0:T(8,128)(2,1)S(1)}, u32[]{:S(2)}, u32[]{:S(2)}) collective-permute-start(bf16[128,1024]{1,0:T(8,128)(2,1)S(1)} %pad_maximum_fusion.refs_0_.mine), channel_id=1, source_target_pairs={{0,16},{4,20},{8,24},{12,28},{16,0},{20,4},{24,8},{28,12},{1,17},{... | collective-permute-start | bytes 786440 | tf_op jit(solution)/shard_map/ppermute | solution.py:29
  8.3 1.0 %collective-permute-start.2 = (bf16[128,1024]{1,0:T(8,128)(2,1)S(1)}, bf16[128,1024]{1,0:T(8,128)(2,1)S(1)}, u32[]{:S(2)}, u32[]{:S(2)}) collective-permute-start(bf16[128,1024]{1,0:T(8,128)(2,1)S(1)} %pad_maximum_fusion.1.other), channel_id=1, source_target_pairs={{0,12},{4,8},{8,4},{12,0},{16,28},{20,24},{24,20},{28,16},{1,13},{... | collective-permute-start | bytes 786440 | tf_op jit(solution)/shard_map/ppermute | solution.py:29
  9.3 3.7 %collective-permute-start.7 = (bf16[256,512]{1,0:T(8,128)(2,1)S(1)}, bf16[256,512]{1,0:T(8,128)(2,1)S(1)}, u32[]{:S(2)}, u32[]{:S(2)}) collective-permute-start(bf16[256,512]{1,0:T(8,128)(2,1)S(1)} %get-tuple-element.97), channel_id=1, source_target_pairs={{0,3},{1,0},{2,1},{3,2},{4,7},{5,4},{6,5},{7,6},{8,11},{9,8},{10,9... | collective-permute-start | bytes 786440 | tf_op jit(solution)/shard_map/ppermute | solution.py:34
  13.0 0.6 %collective-permute-start.6 = (bf16[128,1024]{1,0:T(8,128)(2,1)S(1)}, bf16[128,1024]{1,0:T(8,128)(2,1)S(1)}, u32[]{:S(2)}, u32[]{:S(2)}) collective-permute-start(bf16[128,1024]{1,0:T(8,128)(2,1)S(1)} %collective-permute-done.4.refs_4_.refs_3_), channel_id=1, source_target_pairs={{0,8},{4,12},{8,0},{12,4},{16,24},{20,28},{24,16},{28,20},{1,9},{5... | collective-permute-start | bytes 786440 | tf_op jit(solution)/shard_map/ppermute | solution.py:29
  13.6 1.0 %collective-permute-done.1.refs_1_.refs_0_ = bf16[128,1024]{1,0:T(8,128)(2,1)S(1)} collective-permute-done((bf16[128,1024]{1,0:T(8,128)(2,1)S(1)}, bf16[128,1024]{1,0:T(8,128)(2,1)S(1)}, u32[]{:S(2)}, u32[]{:S(2)}) %collective-permute-start.1) | collective-permute-done | bytes 262176 | tf_op jit(solution)/shard_map/ppermute | solution.py:29
  14.6 0.3 collective-permute-start.5
  14.9 3.2 %collective-permute-done.3.refs_3_.refs_2_ = bf16[128,1024]{1,0:T(8,128)(2,1)S(1)} collective-permute-done((bf16[128,1024]{1,0:T(8,128)(2,1)S(1)}, bf16[128,1024]{1,0:T(8,128)(2,1)S(1)}, u32[]{:S(2)}, u32[]{:S(2)}) %collective-permute-start.3) | collective-permute-done | bytes 262176 | tf_op jit(solution)/shard_map/ppermute | solution.py:29
  18.2 2.7 %collective-permute-start.8 = (bf16[256,512]{1,0:T(8,128)(2,1)S(1)}, bf16[256,512]{1,0:T(8,128)(2,1)S(1)}, u32[]{:S(2)}, u32[]{:S(2)}) collective-permute-start(bf16[256,512]{1,0:T(8,128)(2,1)S(1)} %get-tuple-element.96), channel_id=1, source_target_pairs={{0,7},{1,4},{2,5},{3,6},{4,3},{5,0},{6,1},{7,2},{8,15},{9,12},{10,... | collective-permute-start | bytes 786440 | tf_op jit(solution)/shard_map/ppermute | solution.py:34
  21.5 0.5 shard_map.95.refs_0_
  22.0 0.4 shard_map.94.xt
  22.4 0.9 %shard_map.96.prev = f32[512,1024]{1,0:T(8,128)S(1)} custom-call(bf16[640,1024]{1,0:T(8,128)(2,1)S(1)} %get-tuple-element.51.bo, bf16[640,1024]{1,0:T(8,128)(2,1)S(1)} %collective-permute-done.bp, f32[512,1024]{1,0:T(8,128)S(1)} %shard_map.95.refs_0_, bf16[128,1024]{1,0:T(8,128)(2,1)S(1)} %collective-permute-done.1.refs_1_.refs_0_, ...), custom_call_target="tpu_custom_call" | custom-call | flops 1000000 | bytes 1000000 | tf_op jit(solution)/shard_map/pallas_call | solution.py:42
  23.3 1.7 %collective-permute-done.6.refs_1_.refs_5_ = bf16[128,1024]{1,0:T(8,128)(2,1)S(1)} collective-permute-done((bf16[128,1024]{1,0:T(8,128)(2,1)S(1)}, bf16[128,1024]{1,0:T(8,128)(2,1)S(1)}, u32[]{:S(2)}, u32[]{:S(2)}) %collective-permute-start.6) | collective-permute-done | bytes 262176 | tf_op jit(solution)/shard_map/ppermute | solution.py:29
  24.9 2.0 %shard_map.97 = (bf16[512,1024]{1,0:T(8,128)(2,1)S(1)}, f32[512,1024]{1,0:T(8,128)S(1)}, bf16[8,256,256]{2,1,0:T(8,128)(2,1)S(1)}, bf16[8,256,256]{2,1,0:T(8,128)(2,1)S(1)}, f32[512,512]{1,0:T(8,128)S(1)}) custom-call(bf16[640,1024]{1,0:T(8,128)(2,1)S(1)} %get-tuple-element.51.bo, bf16[640,1024]{1,0:T(8,128)(2,1)S(1)} %collective-permute-done.bp, ...), custom_call_target="tpu_custom_call" | custom-call | flops 1000000 | bytes 1000000 | tf_op jit(solution)/shard_map/pallas_call | solution.py:42
  26.9 0.6 %shard_map.98 = (f32[512,512]{1,0:T(8,128)S(1)}, f32[8,512]{1,0:T(8,128)S(1)}) custom-call(s32[1,1]{1,0:T(1,128)S(6)} %copy.10.length, f32[512,512]{1,0:T(8,128)S(1)} %get-tuple-element.60.mixed, bf16[256,1024]{1,0:T(8,128)(2,1)S(1)} %get-tuple-element.57.vgo, bf16[640,1024]{1,0:T(8,128)(2,1)S(1)} %collective-permute-done.bp, ...), custom_call_target="tpu_custom_call" | custom-call | flops 1000000000 | bytes 1000000000 | tf_op jit(solution)/shard_map/pallas_call | solution.py:42
  27.5 0.8 %collective-permute-start.9 = (f32[8,512]{1,0:T(8,128)S(1)}, f32[8,512]{1,0:T(8,128)S(1)}, u32[]{:S(2)}, u32[]{:S(2)}) collective-permute-start(f32[8,512]{1,0:T(8,128)S(1)} %get-tuple-element.62.mine), channel_id=1, source_target_pairs={{0,4},{4,0},{8,12},{12,8},{16,20},{20,16},{24,28},{28,24},{1,5},{5... | collective-permute-start | bytes 49160 | tf_op jit(solution)/shard_map/ppermute | solution.py:29
  28.3 0.3 shard_map.99.slope
  28.5 0.6 %collective-permute-done.9.theirs = f32[8,512]{1,0:T(8,128)S(1)} collective-permute-done((f32[8,512]{1,0:T(8,128)S(1)}, f32[8,512]{1,0:T(8,128)S(1)}, u32[]{:S(2)}, u32[]{:S(2)}) %collective-permute-start.9) | collective-permute-done | bytes 16416 | tf_op jit(solution)/shard_map/ppermute | solution.py:29
  29.1 1.9 %shard_map.100 = (bf16[512,1024]{1,0:T(8,128)(2,1)S(1)}, bf16[512,512]{1,0:T(8,128)(2,1)S(1)}, bf16[128,1024]{1,0:T(8,128)(2,1)S(1)}, bf16[128,1024]{1,0:T(8,128)(2,1)S(1)}) custom-call(bf16[1024,512]{1,0:T(8,128)(2,1)S(1)} %shard_map.94.xt, bf16[512,1024]{1,0:T(8,128)(2,1)S(1)} %get-tuple-element.58.act, f32[512,1024]{1,0:T(8,128)S(1)} %shard_map.99.slope, ...), custom_call_target="tpu_custom_call" | custom-call | flops 100000000 | bytes 100000000 | tf_op jit(solution)/shard_map/pallas_call | solution.py:42
  31.0 1.6 %collective-permute-start.15 = (bf16[128,1024]{1,0:T(8,128)(2,1)S(1)}, bf16[128,1024]{1,0:T(8,128)(2,1)S(1)}, u32[]{:S(2)}, u32[]{:S(2)}) collective-permute-start(bf16[128,1024]{1,0:T(8,128)(2,1)S(1)} %get-tuple-element.86), channel_id=1, source_target_pairs={{0,8},{4,12},{8,0},{12,4},{16,24},{20,28},{24,16},{28,20},{1,9},{5... | collective-permute-start | bytes 786440 | tf_op jit(solution)/shard_map/ppermute | solution.py:29
  32.6 1.5 %collective-permute-start.16 = (bf16[128,1024]{1,0:T(8,128)(2,1)S(1)}, bf16[128,1024]{1,0:T(8,128)(2,1)S(1)}, u32[]{:S(2)}, u32[]{:S(2)}) collective-permute-start(bf16[128,1024]{1,0:T(8,128)(2,1)S(1)} %get-tuple-element.87), channel_id=1, source_target_pairs={{0,16},{4,20},{8,24},{12,28},{16,0},{20,4},{24,8},{28,12},{1,17},{... | collective-permute-start | bytes 786440 | tf_op jit(solution)/shard_map/ppermute | solution.py:29
  34.1 0.7 %shard_map.103 = (bf16[256,1024]{1,0:T(8,128)(2,1)S(1)}, bf16[256,1024]{1,0:T(8,128)(2,1)S(1)}) custom-call(bf16[8,256,256]{2,1,0:T(8,128)(2,1)S(1)} %get-tuple-element.70.prob, bf16[512,512]{1,0:T(8,128)(2,1)S(1)} %get-tuple-element.71.dmixed, f32[512,512]{1,0:T(8,128)S(1)} %get-tuple-element.60.mixed, f32[8,512]{1,0:T(8,128)S(1)} %get-tuple-element.62.mine, ...), custom_call_target="tpu_custom_call" | custom-call | flops 3000000000 | bytes 3000000000 | tf_op jit(solution)/shard_map/pallas_call | solution.py:42
  34.9 0.1 collective-permute-start.10
  34.9 1.0 %shard_map.102 = (bf16[128,1024]{1,0:T(8,128)(2,1)S(1)}, bf16[128,1024]{1,0:T(8,128)(2,1)S(1)}, bf16[128,1024]{1,0:T(8,128)(2,1)S(1)}, bf16[128,1024]{1,0:T(8,12...) custom-call(bf16[1024,512]{1,0:T(8,128)(2,1)S(1)} %shard_map.94.xt, ...), custom_call_target="tpu_custom_call" | custom-call | flops 10000000000 | bytes 10000000000 | tf_op jit(solution)/shard_map/pallas_call | solution.py:42
  35.9 0.6 %collective-permute-start.13 = (bf16[128,1024]{1,0:T(8,128)(2,1)S(1)}, bf16[128,1024]{1,0:T(8,128)(2,1)S(1)}, u32[]{:S(2)}, u32[]{:S(2)}) collective-permute-start(bf16[128,1024]{1,0:T(8,128)(2,1)S(1)} %get-tuple-element.80), channel_id=1, source_target_pairs={{0,8},{4,12},{8,0},{12,4},{16,24},{20,28},{24,16},{28,20},{1,9},{5... | collective-permute-start | bytes 786440 | tf_op jit(solution)/shard_map/ppermute | solution.py:29
  36.5 0.3 collective-permute-start.14
  36.8 0.3 collective-permute-start.11
  37.1 1.4 %shard_map.101 = (f32[256,1024]{1,0:T(8,128)S(1)}, bf16[256,1024]{1,0:T(8,128)(2,1)S(1)}) custom-call(bf16[128,1024]{1,0:T(8,128)(2,1)S(1)} %pad_maximum_fusion.refs_0_.mine, bf16[640,1024]{1,0:T(8,128)(2,1)S(1)} %collective-permute-done.bp, bf16[128,1024]{1,0:T(8,128)(2,1)S(1)} %collective-permute-done.1.refs_1_.refs_0_, ...), custom_call_target="tpu_custom_call" | custom-call | flops 10000000000 | bytes 10000000000 | tf_op jit(solution)/shard_map/pallas_call | solution.py:42
  38.5 0.3 collective-permute-start.12
  38.8 1.4 %collective-permute-done.15.added = bf16[128,1024]{1,0:T(8,128)(2,1)S(1)} collective-permute-done((bf16[128,1024]{1,0:T(8,128)(2,1)S(1)}, bf16[128,1024]{1,0:T(8,128)(2,1)S(1)}, u32[]{:S(2)}, u32[]{:S(2)}) %collective-permute-start.15) | collective-permute-done | bytes 262176 | tf_op jit(solution)/shard_map/ppermute | solution.py:29
  40.2 1.5 %collective-permute-done.16.added = bf16[128,1024]{1,0:T(8,128)(2,1)S(1)} collective-permute-done((bf16[128,1024]{1,0:T(8,128)(2,1)S(1)}, bf16[128,1024]{1,0:T(8,128)(2,1)S(1)}, u32[]{:S(2)}, u32[]{:S(2)}) %collective-permute-start.16) | collective-permute-done | bytes 262176 | tf_op jit(solution)/shard_map/ppermute | solution.py:29
  41.8 0.1 shard_map.107
  41.8 0.1 collective-permute-start.18
  41.9 0.1 shard_map.106
  42.0 1.6 %collective-permute-start.17 = (bf16[128,1024]{1,0:T(8,128)(2,1)S(1)}, bf16[128,1024]{1,0:T(8,128)(2,1)S(1)}, u32[]{:S(2)}, u32[]{:S(2)}) collective-permute-start(bf16[128,1024]{1,0:T(8,128)(2,1)S(1)} %shard_map.106), channel_id=1, source_target_pairs={{0,16},{4,20},{8,24},{12,28},{16,0},{20,4},{24,8},{28,12},{1,17},{... | collective-permute-start | bytes 786440 | tf_op jit(solution)/shard_map/ppermute | solution.py:29
  43.6 2.1 %collective-permute-done.13.x = bf16[128,1024]{1,0:T(8,128)(2,1)S(1)} collective-permute-done((bf16[128,1024]{1,0:T(8,128)(2,1)S(1)}, bf16[128,1024]{1,0:T(8,128)(2,1)S(1)}, u32[]{:S(2)}, u32[]{:S(2)}) %collective-permute-start.13) | collective-permute-done | bytes 262176 | tf_op jit(solution)/shard_map/ppermute | solution.py:29
  45.6 0.8 %collective-permute-done.14.y = bf16[128,1024]{1,0:T(8,128)(2,1)S(1)} collective-permute-done((bf16[128,1024]{1,0:T(8,128)(2,1)S(1)}, bf16[128,1024]{1,0:T(8,128)(2,1)S(1)}, u32[]{:S(2)}, u32[]{:S(2)}) %collective-permute-start.14) | collective-permute-done | bytes 262176 | tf_op jit(solution)/shard_map/ppermute | solution.py:29
  46.4 0.1 shard_map.105
  46.5 1.3 %shard_map.104 = (bf16[256,1024]{1,0:T(8,128)(2,1)}, bf16[256,1024]{1,0:T(8,128)(2,1)}, bf16[256,1024]{1,0:T(8,128)(2,1)}) custom-call(f32[256,1024]{1,0:T(8,128)S(1)} %get-tuple-element.67.gi_o, bf16[256,1024]{1,0:T(8,128)(2,1)S(1)} %collective-permute-done.12.gi_r, bf16[256,1024]{1,0:T(8,128)(2,1)S(1)} %get-tuple-element.75.own, ...), custom_call_target="tpu_custom_call" | custom-call | flops 300000000 | bytes 300000000 | tf_op jit(solution)/shard_map/pallas_call | solution.py:42
  47.8 2.7 %collective-permute-done.18.y = bf16[128,1024]{1,0:T(8,128)(2,1)S(1)} collective-permute-done((bf16[128,1024]{1,0:T(8,128)(2,1)S(1)}, bf16[128,1024]{1,0:T(8,128)(2,1)S(1)}, u32[]{:S(2)}, u32[]{:S(2)}) %collective-permute-start.18) | collective-permute-done | bytes 262176 | tf_op jit(solution)/shard_map/ppermute | solution.py:29
  50.6 1.5 %collective-permute-done.17.x = bf16[128,1024]{1,0:T(8,128)(2,1)S(1)} collective-permute-done((bf16[128,1024]{1,0:T(8,128)(2,1)S(1)}, bf16[128,1024]{1,0:T(8,128)(2,1)S(1)}, u32[]{:S(2)}, u32[]{:S(2)}) %collective-permute-start.17) | collective-permute-done | bytes 262176 | tf_op jit(solution)/shard_map/ppermute | solution.py:29
  52.1 1.0 %shard_map.108 = f32[128,2048]{1,0:T(8,128)} custom-call(f32[128,1024]{1,0:T(8,128)S(1)} %get-tuple-element.92.own, bf16[128,1024]{1,0:T(8,128)(2,1)S(1)} %collective-permute-done.17.x, f32[128,1024]{1,0:T(8,128)S(1)} %get-tuple-element.94.far, bf16[128,1024]{1,0:T(8,128)(2,1)S(1)} %collective-permute-done.18.y), custom_call_target="tpu_custom_call" | custom-call | tf_op jit(solution)/shard_map/pallas_call | solution.py:447
  (19 shorter events, 0.2 us)
Async XLA Ops:
  0.6 1.3 %copy-start = (bf16[1,1,256,1024]{3,2,1,0:T(8,128)(2,1)S(1)}, bf16[1,1,256,1024]{3,2,1,0:T(8,128)(2,1)}, u32[]{:S(2)}) copy-start(bf16[1,1,256,1024]{3,2,1,0:T(8,128)(2,1)} %param.6) | copy-start | bytes 1572868
  0.6 1.3 %copy-start.1 = (bf16[1,1,256,1024]{3,2,1,0:T(8,128)(2,1)S(1)}, bf16[1,1,256,1024]{3,2,1,0:T(8,128)(2,1)}, u32[]{:S(2)}) copy-start(bf16[1,1,256,1024]{3,2,1,0:T(8,128)(2,1)} %param.7) | copy-start | bytes 1572868
  0.7 1.5 %copy-start.2 = (bf16[1,1,256,1024]{3,2,1,0:T(8,128)(2,1)S(1)}, bf16[1,1,256,1024]{3,2,1,0:T(8,128)(2,1)}, u32[]{:S(2)}) copy-start(bf16[1,1,256,1024]{3,2,1,0:T(8,128)(2,1)} %param.8) | copy-start | bytes 1572868
  1.9 7.4 %copy-start.3 = (bf16[1,1,256,1024]{3,2,1,0:T(8,128)(2,1)S(1)}, bf16[1,1,256,1024]{3,2,1,0:T(8,128)(2,1)}, u32[]{:S(2)}) copy-start(bf16[1,1,256,1024]{3,2,1,0:T(8,128)(2,1)} %param.9) | copy-start | bytes 1572868
  2.3 4.7 %collective-permute-start = (bf16[640,1024]{1,0:T(8,128)(2,1)S(1)}, bf16[640,1024]{1,0:T(8,128)(2,1)S(1)}, u32[]{:S(2)}, u32[]{:S(2)}) collective-permute-start(bf16[640,1024]{1,0:T(8,128)(2,1)S(1)} %get-tuple-element.51.bo), channel_id=1, source_target_pairs={{0,4},{4,0},{8,12},{12,8},{16,20},{20,16},{24,28},{28,24},{1,5},{5... | collective-permute-start | bytes 3932168 | tf_op jit(solution)/shard_map/ppermute | solution.py:29
  2.8 10.2 %collective-permute-start.4 = (bf16[128,1024]{1,0:T(8,128)(2,1)S(1)}, bf16[128,1024]{1,0:T(8,128)(2,1)S(1)}, u32[]{:S(2)}, u32[]{:S(2)}) collective-permute-start(bf16[128,1024]{1,0:T(8,128)(2,1)S(1)} %pad_maximum_fusion.1.other), channel_id=1, source_target_pairs={{0,20},{4,16},{8,28},{12,24},{16,4},{20,0},{24,12},{28,8},{1,21},{... | collective-permute-start | bytes 786440 | tf_op jit(solution)/shard_map/ppermute | solution.py:29
  5.4 9.2 %collective-permute-start.1 = (bf16[128,1024]{1,0:T(8,128)(2,1)S(1)}, bf16[128,1024]{1,0:T(8,128)(2,1)S(1)}, u32[]{:S(2)}, u32[]{:S(2)}) collective-permute-start(bf16[128,1024]{1,0:T(8,128)(2,1)S(1)} %pad_maximum_fusion.refs_0_.mine), channel_id=1, source_target_pairs={{0,8},{4,12},{8,0},{12,4},{16,24},{20,28},{24,16},{28,20},{1,9},{5... | collective-permute-start | bytes 786440 | tf_op jit(solution)/shard_map/ppermute | solution.py:29
  6.9 11.2 %collective-permute-start.3 = (bf16[128,1024]{1,0:T(8,128)(2,1)S(1)}, bf16[128,1024]{1,0:T(8,128)(2,1)S(1)}, u32[]{:S(2)}, u32[]{:S(2)}) collective-permute-start(bf16[128,1024]{1,0:T(8,128)(2,1)S(1)} %pad_maximum_fusion.refs_0_.mine), channel_id=1, source_target_pairs={{0,16},{4,20},{8,24},{12,28},{16,0},{20,4},{24,8},{28,12},{1,17},{... | collective-permute-start | bytes 786440 | tf_op jit(solution)/shard_map/ppermute | solution.py:29
  8.3 14.0 %collective-permute-start.2 = (bf16[128,1024]{1,0:T(8,128)(2,1)S(1)}, bf16[128,1024]{1,0:T(8,128)(2,1)S(1)}, u32[]{:S(2)}, u32[]{:S(2)}) collective-permute-start(bf16[128,1024]{1,0:T(8,128)(2,1)S(1)} %pad_maximum_fusion.1.other), channel_id=1, source_target_pairs={{0,12},{4,8},{8,4},{12,0},{16,28},{20,24},{24,20},{28,16},{1,13},{... | collective-permute-start | bytes 786440 | tf_op jit(solution)/shard_map/ppermute | solution.py:29
  9.3 13.9 %collective-permute-start.7 = (bf16[256,512]{1,0:T(8,128)(2,1)S(1)}, bf16[256,512]{1,0:T(8,128)(2,1)S(1)}, u32[]{:S(2)}, u32[]{:S(2)}) collective-permute-start(bf16[256,512]{1,0:T(8,128)(2,1)S(1)} %get-tuple-element.97), channel_id=1, source_target_pairs={{0,3},{1,0},{2,1},{3,2},{4,7},{5,4},{6,5},{7,6},{8,11},{9,8},{10,9... | collective-permute-start | bytes 786440 | tf_op jit(solution)/shard_map/ppermute | solution.py:34
  13.0 12.0 %collective-permute-start.6 = (bf16[128,1024]{1,0:T(8,128)(2,1)S(1)}, bf16[128,1024]{1,0:T(8,128)(2,1)S(1)}, u32[]{:S(2)}, u32[]{:S(2)}) collective-permute-start(bf16[128,1024]{1,0:T(8,128)(2,1)S(1)} %collective-permute-done.4.refs_4_.refs_3_), channel_id=1, source_target_pairs={{0,8},{4,12},{8,0},{12,4},{16,24},{20,28},{24,16},{28,20},{1,9},{5... | collective-permute-start | bytes 786440 | tf_op jit(solution)/shard_map/ppermute | solution.py:29
  14.6 10.3 %collective-permute-start.5 = (bf16[128,1024]{1,0:T(8,128)(2,1)S(1)}, bf16[128,1024]{1,0:T(8,128)(2,1)S(1)}, u32[]{:S(2)}, u32[]{:S(2)}) collective-permute-start(bf16[128,1024]{1,0:T(8,128)(2,1)S(1)} %collective-permute-done.1.refs_1_.refs_0_), channel_id=1, source_target_pairs={{0,16},{4,20},{8,24},{12,28},{16,0},{20,4},{24,8},{28,12},{1,17},{... | collective-permute-start | bytes 786440 | tf_op jit(solution)/shard_map/ppermute | solution.py:29
  18.2 8.8 %collective-permute-start.8 = (bf16[256,512]{1,0:T(8,128)(2,1)S(1)}, bf16[256,512]{1,0:T(8,128)(2,1)S(1)}, u32[]{:S(2)}, u32[]{:S(2)}) collective-permute-start(bf16[256,512]{1,0:T(8,128)(2,1)S(1)} %get-tuple-element.96), channel_id=1, source_target_pairs={{0,7},{1,4},{2,5},{3,6},{4,3},{5,0},{6,1},{7,2},{8,15},{9,12},{10,... | collective-permute-start | bytes 786440 | tf_op jit(solution)/shard_map/ppermute | solution.py:34
  27.5 1.6 %collective-permute-start.9 = (f32[8,512]{1,0:T(8,128)S(1)}, f32[8,512]{1,0:T(8,128)S(1)}, u32[]{:S(2)}, u32[]{:S(2)}) collective-permute-start(f32[8,512]{1,0:T(8,128)S(1)} %get-tuple-element.62.mine), channel_id=1, source_target_pairs={{0,4},{4,0},{8,12},{12,8},{16,20},{20,16},{24,28},{28,24},{1,5},{5... | collective-permute-start | bytes 49160 | tf_op jit(solution)/shard_map/ppermute | solution.py:29
  31.0 9.2 %collective-permute-start.15 = (bf16[128,1024]{1,0:T(8,128)(2,1)S(1)}, bf16[128,1024]{1,0:T(8,128)(2,1)S(1)}, u32[]{:S(2)}, u32[]{:S(2)}) collective-permute-start(bf16[128,1024]{1,0:T(8,128)(2,1)S(1)} %get-tuple-element.86), channel_id=1, source_target_pairs={{0,8},{4,12},{8,0},{12,4},{16,24},{20,28},{24,16},{28,20},{1,9},{5... | collective-permute-start | bytes 786440 | tf_op jit(solution)/shard_map/ppermute | solution.py:29
  32.6 9.2 %collective-permute-start.16 = (bf16[128,1024]{1,0:T(8,128)(2,1)S(1)}, bf16[128,1024]{1,0:T(8,128)(2,1)S(1)}, u32[]{:S(2)}, u32[]{:S(2)}) collective-permute-start(bf16[128,1024]{1,0:T(8,128)(2,1)S(1)} %get-tuple-element.87), channel_id=1, source_target_pairs={{0,16},{4,20},{8,24},{12,28},{16,0},{20,4},{24,8},{28,12},{1,17},{... | collective-permute-start | bytes 786440 | tf_op jit(solution)/shard_map/ppermute | solution.py:29
  34.9 2.0 %collective-permute-start.10 = (bf16[256,1024]{1,0:T(8,128)(2,1)S(1)}, bf16[256,1024]{1,0:T(8,128)(2,1)S(1)}, u32[]{:S(2)}, u32[]{:S(2)}) collective-permute-start(bf16[256,1024]{1,0:T(8,128)(2,1)S(1)} %get-tuple-element.72), channel_id=1, source_target_pairs={{0,4},{4,0},{8,12},{12,8},{16,20},{20,16},{24,28},{28,24},{1,5},{5... | collective-permute-start | bytes 1572872 | tf_op jit(solution)/shard_map/ppermute | solution.py:29
  35.9 9.7 %collective-permute-start.13 = (bf16[128,1024]{1,0:T(8,128)(2,1)S(1)}, bf16[128,1024]{1,0:T(8,128)(2,1)S(1)}, u32[]{:S(2)}, u32[]{:S(2)}) collective-permute-start(bf16[128,1024]{1,0:T(8,128)(2,1)S(1)} %get-tuple-element.80), channel_id=1, source_target_pairs={{0,8},{4,12},{8,0},{12,4},{16,24},{20,28},{24,16},{28,20},{1,9},{5... | collective-permute-start | bytes 786440 | tf_op jit(solution)/shard_map/ppermute | solution.py:29
  36.5 9.9 %collective-permute-start.14 = (bf16[128,1024]{1,0:T(8,128)(2,1)S(1)}, bf16[128,1024]{1,0:T(8,128)(2,1)S(1)}, u32[]{:S(2)}, u32[]{:S(2)}) collective-permute-start(bf16[128,1024]{1,0:T(8,128)(2,1)S(1)} %get-tuple-element.81), channel_id=1, source_target_pairs={{0,20},{4,16},{8,28},{12,24},{16,4},{20,0},{24,12},{28,8},{1,21},{... | collective-permute-start | bytes 786440 | tf_op jit(solution)/shard_map/ppermute | solution.py:29
  36.8 1.7 %collective-permute-start.11 = (bf16[128,1024]{1,0:T(8,128)(2,1)S(1)}, bf16[128,1024]{1,0:T(8,128)(2,1)S(1)}, u32[]{:S(2)}, u32[]{:S(2)}) collective-permute-start(bf16[128,1024]{1,0:T(8,128)(2,1)S(1)} %get-tuple-element.73), channel_id=1, source_target_pairs={{0,4},{4,0},{8,12},{12,8},{16,20},{20,16},{24,28},{28,24},{1,5},{5... | collective-permute-start | bytes 786440 | tf_op jit(solution)/shard_map/ppermute | solution.py:29
  38.5 8.0 %collective-permute-start.12 = (bf16[256,1024]{1,0:T(8,128)(2,1)S(1)}, bf16[256,1024]{1,0:T(8,128)(2,1)S(1)}, u32[]{:S(2)}, u32[]{:S(2)}) collective-permute-start(bf16[256,1024]{1,0:T(8,128)(2,1)S(1)} %get-tuple-element.74), channel_id=1, source_target_pairs={{0,4},{4,0},{8,12},{12,8},{16,20},{20,16},{24,28},{28,24},{1,5},{5... | collective-permute-start | bytes 1572872 | tf_op jit(solution)/shard_map/ppermute | solution.py:29
  41.8 8.7 %collective-permute-start.18 = (bf16[128,1024]{1,0:T(8,128)(2,1)S(1)}, bf16[128,1024]{1,0:T(8,128)(2,1)S(1)}, u32[]{:S(2)}, u32[]{:S(2)}) collective-permute-start(bf16[128,1024]{1,0:T(8,128)(2,1)S(1)} %shard_map.107), channel_id=1, source_target_pairs={{0,12},{4,8},{8,4},{12,0},{16,28},{20,24},{24,20},{28,16},{1,13},{... | collective-permute-start | bytes 786440 | tf_op jit(solution)/shard_map/ppermute | solution.py:29
  42.0 10.1 %collective-permute-start.17 = (bf16[128,1024]{1,0:T(8,128)(2,1)S(1)}, bf16[128,1024]{1,0:T(8,128)(2,1)S(1)}, u32[]{:S(2)}, u32[]{:S(2)}) collective-permute-start(bf16[128,1024]{1,0:T(8,128)(2,1)S(1)} %shard_map.106), channel_id=1, source_target_pairs={{0,16},{4,20},{8,24},{12,28},{16,0},{20,4},{24,8},{28,12},{1,17},{... | collective-permute-start | bytes 786440 | tf_op jit(solution)/shard_map/ppermute | solution.py:29

commit v6 on v5

--- a/solution.py
+++ b/solution.py
@@ -158,12 +158,12 @@
     raws = []
     for s, h in units:
         own = pl.ds(s * seq_len, seq_len)
-        raws.append(dot(act[own, pl.ds(h * DH, DH)], act[own, pl.ds(HALF + h * DH, DH)], 1, 1))
+        q, k = act[own, pl.ds(h * DH, DH)], act[own, pl.ds(HALF + h * DH, DH)]
+        raws.append((dot(q[:top], k[:top], 1, 1), dot(q[top:], k, 1, 1)))
     probs = []
     for (s, h), raw in zip(units, raws):
-        halves = raw[:top, :top], raw[top:, :]
-        sigs_h = [sigmoid(x, SCALE) for x in halves]
-        outs = [x * sig for x, sig in zip(halves, sigs_h)]
+        sigs_h = [sigmoid(x, SCALE) for x in raw]
+        outs = [x * sig for x, sig in zip(raw, sigs_h)]
         p = lower_half(*outs, causal)
         probs.append(p)
         prob[s * HL + h] = p
@@ -171,7 +171,8 @@
     for (s, h), p in zip(units, probs):
         at = pl.ds(h * DH, DH)
         val = bp[far, at] if s else vgo[:, at]
-        mixed[pl.ds(s * seq_len, seq_len), pl.ds(h * DH, DH)] = dot(p, val, 1, 0)
+        mixed[pl.ds(s * seq_len, top), at] = dot(p[:top, :top], val[:top], 1, 0)
+        mixed[pl.ds(s * seq_len + top, top), at] = dot(p[top:], val, 1, 0)
 
 
 def stats_kernel(length, mixed, vgo, bp, co, cp, prod, stats):
@@ -229,13 +230,18 @@
             dmix = (rate * (prod[own, local] - c1 - normed * c2)).astype(BF)
             dmixed[own, local] = dmix
             units.append((own, h, s * HL + h, val, dmix))
-    dscores = [dot(dmix, val, 1, 1).astype(BF) * prob_slope[u] for _, _, u, val, dmix in units]
+    dscores = []
+    for _, _, u, val, dmix in units:
+        top = seq_len // 2
+        upper = dot(dmix[:top], val[:top], 1, 1).astype(BF) * prob_slope[u][:top, :top]
+        lower = dot(dmix[top:], val, 1, 1).astype(BF) * prob_slope[u][top:]
+        dscores.append(jnp.concatenate([jnp.concatenate([upper, jnp.zeros_like(upper)], 1), lower], 0))
     for (own, h, _, _, _), dscore in zip(units, dscores):
         q_at, k_at = pl.ds(h * DH, DH), pl.ds(HALF + h * DH, DH)
-        dq = dot(dscore, act[own, k_at], 1, 0)
-        dk = dot(dscore, act[own, q_at], 0, 0)
-        gpre[own, q_at] = (dq * slope[own, q_at]).astype(BF)
-        gpre[own, k_at] = (dk * slope[own, k_at]).astype(BF)
+        gpre[own, q_at] = (dot(dscore, act[own, k_at], 1, 0) * slope[own, q_at]).astype(BF)
+    for (own, h, _, _, _), dscore in zip(units, dscores):
+        q_at, k_at = pl.ds(h * DH, DH), pl.ds(HALF + h * DH, DH)
+        gpre[own, k_at] = (dot(dscore, act[own, q_at], 0, 0) * slope[own, k_at]).astype(BF)
     rows = terms[0].shape[0]
     for m, term in zip(far, terms):
         term[...] = dot(xt[m * rows : (m + 1) * rows, :], gpre[...], 1, 0).astype(BF)

time: 53.3 us -> 53.2 us (level)
  no operation moved by 1% of the time
where the time goes in v6:
time: 53.2 us; the launch traced here: 53 us
  starting transfers between devices  21.5 us (40%)
  waiting for transfers between devices  16.6 us (31%)
  Pallas kernels  12 us (23%)
  between operations  1.53 us (3%)
  local copies, waits for them, and re-layouts  1.43 us (3%)
    ppermute x17, waiting for transfers between devices, pair(): return lax.ppermute(x, 'dp', [(i, i ^ mask) for i in range(count)])  16.6 us
    ppermute x17, starting transfers between devices, pair(): return lax.ppermute(x, 'dp', [(i, i ^ mask) for i in range(count)])  15.1 us
    pallas_call x15, Pallas kernels, call(): pl.pallas_call(body, out_shape=out_shape, in_specs=[SMEM if x.dtype == jn...  10.9 us
    ppermute x2, starting transfers between devices, from_next(): lax.ppermute(x, ('dp', 'segment'), [(i * seg + s, (i ^ mask) * seg + (s -...  6.33 us
    slice x1, local copies, waits for them, and re-layouts, on_device(): shard[:, :F]  1.18 us
  transfers between devices with their start and end apart: 19, of which 10 were waited for; matrix products, arithmetic and copies ran while one was open for 0% of the time, Pallas kernels for 16%

profile of v6, /device:TPU:0, one launch (start us, length us, event | category | flops | bytes accessed | tf_op | source)
XLA Modules:
  0.0 53.0 jit_solution(14341703032627089926)
XLA Ops:
  0.7 1.2 %fusion = (bf16[128,1024]{1,0:T(8,128)(2,1)S(1)}, bf16[128,1024]{1,0:T(8,128)(2,1)S(1)}) fusion(bf16[128,2048]{1,0:T(8,128)(2,1)} %bitcast.14), kind=kLoop, calls=%fused_computation.8 | loop fusion | bytes 1048576 | tf_op jit(solution)/shard_map/slice | solution.py:350
  1.9 0.0 copy-start.3
  2.0 0.2 copy-done.2
  2.2 0.1 shard_map.93
  2.3 0.5 collective-permute-start
  2.8 2.6 %collective-permute-start.4 = (bf16[128,1024]{1,0:T(8,128)(2,1)S(1)}, bf16[128,1024]{1,0:T(8,128)(2,1)S(1)}, u32[]{:S(2)}, u32[]{:S(2)}) collective-permute-start(bf16[128,1024]{1,0:T(8,128)(2,1)S(1)} %pad_maximum_fusion.1.other), channel_id=1, source_target_pairs={{0,20},{4,16},{8,28},{12,24},{16,4},{20,0},{24,12},{28,8},{1,21},{... | collective-permute-start | bytes 786440 | tf_op jit(solution)/shard_map/ppermute | solution.py:29
  5.4 1.5 %collective-permute-start.1 = (bf16[128,1024]{1,0:T(8,128)(2,1)S(1)}, bf16[128,1024]{1,0:T(8,128)(2,1)S(1)}, u32[]{:S(2)}, u32[]{:S(2)}) collective-permute-start(bf16[128,1024]{1,0:T(8,128)(2,1)S(1)} %pad_maximum_fusion.refs_0_.mine), channel_id=1, source_target_pairs={{0,8},{4,12},{8,0},{12,4},{16,24},{20,28},{24,16},{28,20},{1,9},{5... | collective-permute-start | bytes 786440 | tf_op jit(solution)/shard_map/ppermute | solution.py:29
  6.9 1.4 %collective-permute-start.3 = (bf16[128,1024]{1,0:T(8,128)(2,1)S(1)}, bf16[128,1024]{1,0:T(8,128)(2,1)S(1)}, u32[]{:S(2)}, u32[]{:S(2)}) collective-permute-start(bf16[128,1024]{1,0:T(8,128)(2,1)S(1)} %pad_maximum_fusion.refs_0_.mine), channel_id=1, source_target_pairs={{0,16},{4,20},{8,24},{12,28},{16,0},{20,4},{24,8},{28,12},{1,17},{... | collective-permute-start | bytes 786440 | tf_op jit(solution)/shard_map/ppermute | solution.py:29
  8.3 1.0 %collective-permute-start.2 = (bf16[128,1024]{1,0:T(8,128)(2,1)S(1)}, bf16[128,1024]{1,0:T(8,128)(2,1)S(1)}, u32[]{:S(2)}, u32[]{:S(2)}) collective-permute-start(bf16[128,1024]{1,0:T(8,128)(2,1)S(1)} %pad_maximum_fusion.1.other), channel_id=1, source_target_pairs={{0,12},{4,8},{8,4},{12,0},{16,28},{20,24},{24,20},{28,16},{1,13},{... | collective-permute-start | bytes 786440 | tf_op jit(solution)/shard_map/ppermute | solution.py:29
  9.3 3.7 %collective-permute-start.7 = (bf16[256,512]{1,0:T(8,128)(2,1)S(1)}, bf16[256,512]{1,0:T(8,128)(2,1)S(1)}, u32[]{:S(2)}, u32[]{:S(2)}) collective-permute-start(bf16[256,512]{1,0:T(8,128)(2,1)S(1)} %get-tuple-element.97), channel_id=1, source_target_pairs={{0,3},{1,0},{2,1},{3,2},{4,7},{5,4},{6,5},{7,6},{8,11},{9,8},{10,9... | collective-permute-start | bytes 786440 | tf_op jit(solution)/shard_map/ppermute | solution.py:34
  13.0 0.6 %collective-permute-start.6 = (bf16[128,1024]{1,0:T(8,128)(2,1)S(1)}, bf16[128,1024]{1,0:T(8,128)(2,1)S(1)}, u32[]{:S(2)}, u32[]{:S(2)}) collective-permute-start(bf16[128,1024]{1,0:T(8,128)(2,1)S(1)} %collective-permute-done.4.refs_4_.refs_3_), channel_id=1, source_target_pairs={{0,8},{4,12},{8,0},{12,4},{16,24},{20,28},{24,16},{28,20},{1,9},{5... | collective-permute-start | bytes 786440 | tf_op jit(solution)/shard_map/ppermute | solution.py:29
  13.6 1.0 %collective-permute-done.1.refs_1_.refs_0_ = bf16[128,1024]{1,0:T(8,128)(2,1)S(1)} collective-permute-done((bf16[128,1024]{1,0:T(8,128)(2,1)S(1)}, bf16[128,1024]{1,0:T(8,128)(2,1)S(1)}, u32[]{:S(2)}, u32[]{:S(2)}) %collective-permute-start.1) | collective-permute-done | bytes 262176 | tf_op jit(solution)/shard_map/ppermute | solution.py:29
  14.6 0.3 collective-permute-start.5
  14.9 3.2 %collective-permute-done.3.refs_3_.refs_2_ = bf16[128,1024]{1,0:T(8,128)(2,1)S(1)} collective-permute-done((bf16[128,1024]{1,0:T(8,128)(2,1)S(1)}, bf16[128,1024]{1,0:T(8,128)(2,1)S(1)}, u32[]{:S(2)}, u32[]{:S(2)}) %collective-permute-start.3) | collective-permute-done | bytes 262176 | tf_op jit(solution)/shard_map/ppermute | solution.py:29
  18.2 2.7 %collective-permute-start.8 = (bf16[256,512]{1,0:T(8,128)(2,1)S(1)}, bf16[256,512]{1,0:T(8,128)(2,1)S(1)}, u32[]{:S(2)}, u32[]{:S(2)}) collective-permute-start(bf16[256,512]{1,0:T(8,128)(2,1)S(1)} %get-tuple-element.96), channel_id=1, source_target_pairs={{0,7},{1,4},{2,5},{3,6},{4,3},{5,0},{6,1},{7,2},{8,15},{9,12},{10,... | collective-permute-start | bytes 786440 | tf_op jit(solution)/shard_map/ppermute | solution.py:34
  21.5 0.5 shard_map.95.refs_0_
  22.0 0.4 shard_map.94.xt
  22.4 0.9 %shard_map.96.prev = f32[512,1024]{1,0:T(8,128)S(1)} custom-call(bf16[640,1024]{1,0:T(8,128)(2,1)S(1)} %get-tuple-element.51.bo, bf16[640,1024]{1,0:T(8,128)(2,1)S(1)} %collective-permute-done.bp, f32[512,1024]{1,0:T(8,128)S(1)} %shard_map.95.refs_0_, bf16[128,1024]{1,0:T(8,128)(2,1)S(1)} %collective-permute-done.1.refs_1_.refs_0_, ...), custom_call_target="tpu_custom_call" | custom-call | flops 1000000 | bytes 1000000 | tf_op jit(solution)/shard_map/pallas_call | solution.py:42
  23.3 1.7 %collective-permute-done.6.refs_1_.refs_5_ = bf16[128,1024]{1,0:T(8,128)(2,1)S(1)} collective-permute-done((bf16[128,1024]{1,0:T(8,128)(2,1)S(1)}, bf16[128,1024]{1,0:T(8,128)(2,1)S(1)}, u32[]{:S(2)}, u32[]{:S(2)}) %collective-permute-start.6) | collective-permute-done | bytes 262176 | tf_op jit(solution)/shard_map/ppermute | solution.py:29
  24.9 1.8 %shard_map.97 = (bf16[512,1024]{1,0:T(8,128)(2,1)S(1)}, f32[512,1024]{1,0:T(8,128)S(1)}, bf16[8,256,256]{2,1,0:T(8,128)(2,1)S(1)}, bf16[8,256,256]{2,1,0:T(8,128)(2,1)S(1)}, f32[512,512]{1,0:T(8,128)S(1)}) custom-call(bf16[640,1024]{1,0:T(8,128)(2,1)S(1)} %get-tuple-element.51.bo, bf16[640,1024]{1,0:T(8,128)(2,1)S(1)} %collective-permute-done.bp, ...), custom_call_target="tpu_custom_call" | custom-call | flops 1000000 | bytes 1000000 | tf_op jit(solution)/shard_map/pallas_call | solution.py:42
  26.8 0.6 %shard_map.98 = (f32[512,512]{1,0:T(8,128)S(1)}, f32[8,512]{1,0:T(8,128)S(1)}) custom-call(s32[1,1]{1,0:T(1,128)S(6)} %copy.10.length, f32[512,512]{1,0:T(8,128)S(1)} %get-tuple-element.60.mixed, bf16[256,1024]{1,0:T(8,128)(2,1)S(1)} %get-tuple-element.57.vgo, bf16[640,1024]{1,0:T(8,128)(2,1)S(1)} %collective-permute-done.bp, ...), custom_call_target="tpu_custom_call" | custom-call | flops 1000000000 | bytes 1000000000 | tf_op jit(solution)/shard_map/pallas_call | solution.py:42
  27.4 0.9 %collective-permute-start.9 = (f32[8,512]{1,0:T(8,128)S(1)}, f32[8,512]{1,0:T(8,128)S(1)}, u32[]{:S(2)}, u32[]{:S(2)}) collective-permute-start(f32[8,512]{1,0:T(8,128)S(1)} %get-tuple-element.62.mine), channel_id=1, source_target_pairs={{0,4},{4,0},{8,12},{12,8},{16,20},{20,16},{24,28},{28,24},{1,5},{5... | collective-permute-start | bytes 49160 | tf_op jit(solution)/shard_map/ppermute | solution.py:29
  28.3 0.3 shard_map.99.slope
  28.5 0.6 %collective-permute-done.9.theirs = f32[8,512]{1,0:T(8,128)S(1)} collective-permute-done((f32[8,512]{1,0:T(8,128)S(1)}, f32[8,512]{1,0:T(8,128)S(1)}, u32[]{:S(2)}, u32[]{:S(2)}) %collective-permute-start.9) | collective-permute-done | bytes 16416 | tf_op jit(solution)/shard_map/ppermute | solution.py:29
  29.1 1.8 %shard_map.100 = (bf16[512,1024]{1,0:T(8,128)(2,1)S(1)}, bf16[512,512]{1,0:T(8,128)(2,1)S(1)}, bf16[128,1024]{1,0:T(8,128)(2,1)S(1)}, bf16[128,1024]{1,0:T(8,128)(2,1)S(1)}) custom-call(bf16[1024,512]{1,0:T(8,128)(2,1)S(1)} %shard_map.94.xt, bf16[512,1024]{1,0:T(8,128)(2,1)S(1)} %get-tuple-element.58.act, f32[512,1024]{1,0:T(8,128)S(1)} %shard_map.99.slope, ...), custom_call_target="tpu_custom_call" | custom-call | flops 100000000 | bytes 100000000 | tf_op jit(solution)/shard_map/pallas_call | solution.py:42
  30.9 1.6 %collective-permute-start.15 = (bf16[128,1024]{1,0:T(8,128)(2,1)S(1)}, bf16[128,1024]{1,0:T(8,128)(2,1)S(1)}, u32[]{:S(2)}, u32[]{:S(2)}) collective-permute-start(bf16[128,1024]{1,0:T(8,128)(2,1)S(1)} %get-tuple-element.86), channel_id=1, source_target_pairs={{0,8},{4,12},{8,0},{12,4},{16,24},{20,28},{24,16},{28,20},{1,9},{5... | collective-permute-start | bytes 786440 | tf_op jit(solution)/shard_map/ppermute | solution.py:29
  32.5 1.5 %collective-permute-start.16 = (bf16[128,1024]{1,0:T(8,128)(2,1)S(1)}, bf16[128,1024]{1,0:T(8,128)(2,1)S(1)}, u32[]{:S(2)}, u32[]{:S(2)}) collective-permute-start(bf16[128,1024]{1,0:T(8,128)(2,1)S(1)} %get-tuple-element.87), channel_id=1, source_target_pairs={{0,16},{4,20},{8,24},{12,28},{16,0},{20,4},{24,8},{28,12},{1,17},{... | collective-permute-start | bytes 786440 | tf_op jit(solution)/shard_map/ppermute | solution.py:29
  34.0 0.7 %shard_map.103 = (bf16[256,1024]{1,0:T(8,128)(2,1)S(1)}, bf16[256,1024]{1,0:T(8,128)(2,1)S(1)}) custom-call(bf16[8,256,256]{2,1,0:T(8,128)(2,1)S(1)} %get-tuple-element.70.prob, bf16[512,512]{1,0:T(8,128)(2,1)S(1)} %get-tuple-element.71.dmixed, f32[512,512]{1,0:T(8,128)S(1)} %get-tuple-element.60.mixed, f32[8,512]{1,0:T(8,128)S(1)} %get-tuple-element.62.mine, ...), custom_call_target="tpu_custom_call" | custom-call | flops 3000000000 | bytes 3000000000 | tf_op jit(solution)/shard_map/pallas_call | solution.py:42
  34.7 0.1 collective-permute-start.10
  34.8 1.0 %shard_map.102 = (bf16[128,1024]{1,0:T(8,128)(2,1)S(1)}, bf16[128,1024]{1,0:T(8,128)(2,1)S(1)}, bf16[128,1024]{1,0:T(8,128)(2,1)S(1)}, bf16[128,1024]{1,0:T(8,12...) custom-call(bf16[1024,512]{1,0:T(8,128)(2,1)S(1)} %shard_map.94.xt, ...), custom_call_target="tpu_custom_call" | custom-call | flops 10000000000 | bytes 10000000000 | tf_op jit(solution)/shard_map/pallas_call | solution.py:42
  35.8 0.6 %collective-permute-start.13 = (bf16[128,1024]{1,0:T(8,128)(2,1)S(1)}, bf16[128,1024]{1,0:T(8,128)(2,1)S(1)}, u32[]{:S(2)}, u32[]{:S(2)}) collective-permute-start(bf16[128,1024]{1,0:T(8,128)(2,1)S(1)} %get-tuple-element.80), channel_id=1, source_target_pairs={{0,8},{4,12},{8,0},{12,4},{16,24},{20,28},{24,16},{28,20},{1,9},{5... | collective-permute-start | bytes 786440 | tf_op jit(solution)/shard_map/ppermute | solution.py:29
  36.4 0.3 collective-permute-start.14
  36.7 0.3 collective-permute-start.11
  37.0 1.4 %shard_map.101 = (f32[256,1024]{1,0:T(8,128)S(1)}, bf16[256,1024]{1,0:T(8,128)(2,1)S(1)}) custom-call(bf16[128,1024]{1,0:T(8,128)(2,1)S(1)} %pad_maximum_fusion.refs_0_.mine, bf16[640,1024]{1,0:T(8,128)(2,1)S(1)} %collective-permute-done.bp, bf16[128,1024]{1,0:T(8,128)(2,1)S(1)} %collective-permute-done.1.refs_1_.refs_0_, ...), custom_call_target="tpu_custom_call" | custom-call | flops 10000000000 | bytes 10000000000 | tf_op jit(solution)/shard_map/pallas_call | solution.py:42
  38.4 0.3 collective-permute-start.12
  38.7 1.4 %collective-permute-done.15.added = bf16[128,1024]{1,0:T(8,128)(2,1)S(1)} collective-permute-done((bf16[128,1024]{1,0:T(8,128)(2,1)S(1)}, bf16[128,1024]{1,0:T(8,128)(2,1)S(1)}, u32[]{:S(2)}, u32[]{:S(2)}) %collective-permute-start.15) | collective-permute-done | bytes 262176 | tf_op jit(solution)/shard_map/ppermute | solution.py:29
  40.1 1.5 %collective-permute-done.16.added = bf16[128,1024]{1,0:T(8,128)(2,1)S(1)} collective-permute-done((bf16[128,1024]{1,0:T(8,128)(2,1)S(1)}, bf16[128,1024]{1,0:T(8,128)(2,1)S(1)}, u32[]{:S(2)}, u32[]{:S(2)}) %collective-permute-start.16) | collective-permute-done | bytes 262176 | tf_op jit(solution)/shard_map/ppermute | solution.py:29
  41.6 0.1 shard_map.107
  41.7 0.1 collective-permute-start.18
  41.8 0.1 shard_map.106
  41.8 1.6 %collective-permute-start.17 = (bf16[128,1024]{1,0:T(8,128)(2,1)S(1)}, bf16[128,1024]{1,0:T(8,128)(2,1)S(1)}, u32[]{:S(2)}, u32[]{:S(2)}) collective-permute-start(bf16[128,1024]{1,0:T(8,128)(2,1)S(1)} %shard_map.106), channel_id=1, source_target_pairs={{0,16},{4,20},{8,24},{12,28},{16,0},{20,4},{24,8},{28,12},{1,17},{... | collective-permute-start | bytes 786440 | tf_op jit(solution)/shard_map/ppermute | solution.py:29
  43.4 2.0 %collective-permute-done.13.x = bf16[128,1024]{1,0:T(8,128)(2,1)S(1)} collective-permute-done((bf16[128,1024]{1,0:T(8,128)(2,1)S(1)}, bf16[128,1024]{1,0:T(8,128)(2,1)S(1)}, u32[]{:S(2)}, u32[]{:S(2)}) %collective-permute-start.13) | collective-permute-done | bytes 262176 | tf_op jit(solution)/shard_map/ppermute | solution.py:29
  45.5 0.8 %collective-permute-done.14.y = bf16[128,1024]{1,0:T(8,128)(2,1)S(1)} collective-permute-done((bf16[128,1024]{1,0:T(8,128)(2,1)S(1)}, bf16[128,1024]{1,0:T(8,128)(2,1)S(1)}, u32[]{:S(2)}, u32[]{:S(2)}) %collective-permute-start.14) | collective-permute-done | bytes 262176 | tf_op jit(solution)/shard_map/ppermute | solution.py:29
  46.3 0.1 shard_map.105
  46.4 1.3 %shard_map.104 = (bf16[256,1024]{1,0:T(8,128)(2,1)}, bf16[256,1024]{1,0:T(8,128)(2,1)}, bf16[256,1024]{1,0:T(8,128)(2,1)}) custom-call(f32[256,1024]{1,0:T(8,128)S(1)} %get-tuple-element.67.gi_o, bf16[256,1024]{1,0:T(8,128)(2,1)S(1)} %collective-permute-done.12.gi_r, bf16[256,1024]{1,0:T(8,128)(2,1)S(1)} %get-tuple-element.75.own, ...), custom_call_target="tpu_custom_call" | custom-call | flops 300000000 | bytes 300000000 | tf_op jit(solution)/shard_map/pallas_call | solution.py:42
  47.7 2.7 %collective-permute-done.18.y = bf16[128,1024]{1,0:T(8,128)(2,1)S(1)} collective-permute-done((bf16[128,1024]{1,0:T(8,128)(2,1)S(1)}, bf16[128,1024]{1,0:T(8,128)(2,1)S(1)}, u32[]{:S(2)}, u32[]{:S(2)}) %collective-permute-start.18) | collective-permute-done | bytes 262176 | tf_op jit(solution)/shard_map/ppermute | solution.py:29
  50.4 1.6 %collective-permute-done.17.x = bf16[128,1024]{1,0:T(8,128)(2,1)S(1)} collective-permute-done((bf16[128,1024]{1,0:T(8,128)(2,1)S(1)}, bf16[128,1024]{1,0:T(8,128)(2,1)S(1)}, u32[]{:S(2)}, u32[]{:S(2)}) %collective-permute-start.17) | collective-permute-done | bytes 262176 | tf_op jit(solution)/shard_map/ppermute | solution.py:29
  52.0 1.0 %shard_map.108 = f32[128,2048]{1,0:T(8,128)} custom-call(f32[128,1024]{1,0:T(8,128)S(1)} %get-tuple-element.92.own, bf16[128,1024]{1,0:T(8,128)(2,1)S(1)} %collective-permute-done.17.x, f32[128,1024]{1,0:T(8,128)S(1)} %get-tuple-element.94.far, bf16[128,1024]{1,0:T(8,128)(2,1)S(1)} %collective-permute-done.18.y), custom_call_target="tpu_custom_call" | custom-call | tf_op jit(solution)/shard_map/pallas_call | solution.py:453
  (19 shorter events, 0.2 us)
Async XLA Ops:
  0.6 1.3 %copy-start = (bf16[1,1,256,1024]{3,2,1,0:T(8,128)(2,1)S(1)}, bf16[1,1,256,1024]{3,2,1,0:T(8,128)(2,1)}, u32[]{:S(2)}) copy-start(bf16[1,1,256,1024]{3,2,1,0:T(8,128)(2,1)} %param.6) | copy-start | bytes 1572868
  0.6 1.3 %copy-start.1 = (bf16[1,1,256,1024]{3,2,1,0:T(8,128)(2,1)S(1)}, bf16[1,1,256,1024]{3,2,1,0:T(8,128)(2,1)}, u32[]{:S(2)}) copy-start(bf16[1,1,256,1024]{3,2,1,0:T(8,128)(2,1)} %param.7) | copy-start | bytes 1572868
  0.7 1.5 %copy-start.2 = (bf16[1,1,256,1024]{3,2,1,0:T(8,128)(2,1)S(1)}, bf16[1,1,256,1024]{3,2,1,0:T(8,128)(2,1)}, u32[]{:S(2)}) copy-start(bf16[1,1,256,1024]{3,2,1,0:T(8,128)(2,1)} %param.8) | copy-start | bytes 1572868
  1.9 7.4 %copy-start.3 = (bf16[1,1,256,1024]{3,2,1,0:T(8,128)(2,1)S(1)}, bf16[1,1,256,1024]{3,2,1,0:T(8,128)(2,1)}, u32[]{:S(2)}) copy-start(bf16[1,1,256,1024]{3,2,1,0:T(8,128)(2,1)} %param.9) | copy-start | bytes 1572868
  2.3 4.7 %collective-permute-start = (bf16[640,1024]{1,0:T(8,128)(2,1)S(1)}, bf16[640,1024]{1,0:T(8,128)(2,1)S(1)}, u32[]{:S(2)}, u32[]{:S(2)}) collective-permute-start(bf16[640,1024]{1,0:T(8,128)(2,1)S(1)} %get-tuple-element.51.bo), channel_id=1, source_target_pairs={{0,4},{4,0},{8,12},{12,8},{16,20},{20,16},{24,28},{28,24},{1,5},{5... | collective-permute-start | bytes 3932168 | tf_op jit(solution)/shard_map/ppermute | solution.py:29
  2.8 10.2 %collective-permute-start.4 = (bf16[128,1024]{1,0:T(8,128)(2,1)S(1)}, bf16[128,1024]{1,0:T(8,128)(2,1)S(1)}, u32[]{:S(2)}, u32[]{:S(2)}) collective-permute-start(bf16[128,1024]{1,0:T(8,128)(2,1)S(1)} %pad_maximum_fusion.1.other), channel_id=1, source_target_pairs={{0,20},{4,16},{8,28},{12,24},{16,4},{20,0},{24,12},{28,8},{1,21},{... | collective-permute-start | bytes 786440 | tf_op jit(solution)/shard_map/ppermute | solution.py:29
  5.4 9.2 %collective-permute-start.1 = (bf16[128,1024]{1,0:T(8,128)(2,1)S(1)}, bf16[128,1024]{1,0:T(8,128)(2,1)S(1)}, u32[]{:S(2)}, u32[]{:S(2)}) collective-permute-start(bf16[128,1024]{1,0:T(8,128)(2,1)S(1)} %pad_maximum_fusion.refs_0_.mine), channel_id=1, source_target_pairs={{0,8},{4,12},{8,0},{12,4},{16,24},{20,28},{24,16},{28,20},{1,9},{5... | collective-permute-start | bytes 786440 | tf_op jit(solution)/shard_map/ppermute | solution.py:29
  6.9 11.2 %collective-permute-start.3 = (bf16[128,1024]{1,0:T(8,128)(2,1)S(1)}, bf16[128,1024]{1,0:T(8,128)(2,1)S(1)}, u32[]{:S(2)}, u32[]{:S(2)}) collective-permute-start(bf16[128,1024]{1,0:T(8,128)(2,1)S(1)} %pad_maximum_fusion.refs_0_.mine), channel_id=1, source_target_pairs={{0,16},{4,20},{8,24},{12,28},{16,0},{20,4},{24,8},{28,12},{1,17},{... | collective-permute-start | bytes 786440 | tf_op jit(solution)/shard_map/ppermute | solution.py:29
  8.3 14.0 %collective-permute-start.2 = (bf16[128,1024]{1,0:T(8,128)(2,1)S(1)}, bf16[128,1024]{1,0:T(8,128)(2,1)S(1)}, u32[]{:S(2)}, u32[]{:S(2)}) collective-permute-start(bf16[128,1024]{1,0:T(8,128)(2,1)S(1)} %pad_maximum_fusion.1.other), channel_id=1, source_target_pairs={{0,12},{4,8},{8,4},{12,0},{16,28},{20,24},{24,20},{28,16},{1,13},{... | collective-permute-start | bytes 786440 | tf_op jit(solution)/shard_map/ppermute | solution.py:29
  9.3 13.9 %collective-permute-start.7 = (bf16[256,512]{1,0:T(8,128)(2,1)S(1)}, bf16[256,512]{1,0:T(8,128)(2,1)S(1)}, u32[]{:S(2)}, u32[]{:S(2)}) collective-permute-start(bf16[256,512]{1,0:T(8,128)(2,1)S(1)} %get-tuple-element.97), channel_id=1, source_target_pairs={{0,3},{1,0},{2,1},{3,2},{4,7},{5,4},{6,5},{7,6},{8,11},{9,8},{10,9... | collective-permute-start | bytes 786440 | tf_op jit(solution)/shard_map/ppermute | solution.py:34
  13.0 12.0 %collective-permute-start.6 = (bf16[128,1024]{1,0:T(8,128)(2,1)S(1)}, bf16[128,1024]{1,0:T(8,128)(2,1)S(1)}, u32[]{:S(2)}, u32[]{:S(2)}) collective-permute-start(bf16[128,1024]{1,0:T(8,128)(2,1)S(1)} %collective-permute-done.4.refs_4_.refs_3_), channel_id=1, source_target_pairs={{0,8},{4,12},{8,0},{12,4},{16,24},{20,28},{24,16},{28,20},{1,9},{5... | collective-permute-start | bytes 786440 | tf_op jit(solution)/shard_map/ppermute | solution.py:29
  14.6 10.3 %collective-permute-start.5 = (bf16[128,1024]{1,0:T(8,128)(2,1)S(1)}, bf16[128,1024]{1,0:T(8,128)(2,1)S(1)}, u32[]{:S(2)}, u32[]{:S(2)}) collective-permute-start(bf16[128,1024]{1,0:T(8,128)(2,1)S(1)} %collective-permute-done.1.refs_1_.refs_0_), channel_id=1, source_target_pairs={{0,16},{4,20},{8,24},{12,28},{16,0},{20,4},{24,8},{28,12},{1,17},{... | collective-permute-start | bytes 786440 | tf_op jit(solution)/shard_map/ppermute | solution.py:29
  18.2 8.6 %collective-permute-start.8 = (bf16[256,512]{1,0:T(8,128)(2,1)S(1)}, bf16[256,512]{1,0:T(8,128)(2,1)S(1)}, u32[]{:S(2)}, u32[]{:S(2)}) collective-permute-start(bf16[256,512]{1,0:T(8,128)(2,1)S(1)} %get-tuple-element.96), channel_id=1, source_target_pairs={{0,7},{1,4},{2,5},{3,6},{4,3},{5,0},{6,1},{7,2},{8,15},{9,12},{10,... | collective-permute-start | bytes 786440 | tf_op jit(solution)/shard_map/ppermute | solution.py:34
  27.4 1.7 %collective-permute-start.9 = (f32[8,512]{1,0:T(8,128)S(1)}, f32[8,512]{1,0:T(8,128)S(1)}, u32[]{:S(2)}, u32[]{:S(2)}) collective-permute-start(f32[8,512]{1,0:T(8,128)S(1)} %get-tuple-element.62.mine), channel_id=1, source_target_pairs={{0,4},{4,0},{8,12},{12,8},{16,20},{20,16},{24,28},{28,24},{1,5},{5... | collective-permute-start | bytes 49160 | tf_op jit(solution)/shard_map/ppermute | solution.py:29
  30.9 9.2 %collective-permute-start.15 = (bf16[128,1024]{1,0:T(8,128)(2,1)S(1)}, bf16[128,1024]{1,0:T(8,128)(2,1)S(1)}, u32[]{:S(2)}, u32[]{:S(2)}) collective-permute-start(bf16[128,1024]{1,0:T(8,128)(2,1)S(1)} %get-tuple-element.86), channel_id=1, source_target_pairs={{0,8},{4,12},{8,0},{12,4},{16,24},{20,28},{24,16},{28,20},{1,9},{5... | collective-permute-start | bytes 786440 | tf_op jit(solution)/shard_map/ppermute | solution.py:29
  32.5 9.2 %collective-permute-start.16 = (bf16[128,1024]{1,0:T(8,128)(2,1)S(1)}, bf16[128,1024]{1,0:T(8,128)(2,1)S(1)}, u32[]{:S(2)}, u32[]{:S(2)}) collective-permute-start(bf16[128,1024]{1,0:T(8,128)(2,1)S(1)} %get-tuple-element.87), channel_id=1, source_target_pairs={{0,16},{4,20},{8,24},{12,28},{16,0},{20,4},{24,8},{28,12},{1,17},{... | collective-permute-start | bytes 786440 | tf_op jit(solution)/shard_map/ppermute | solution.py:29
  34.7 2.0 %collective-permute-start.10 = (bf16[256,1024]{1,0:T(8,128)(2,1)S(1)}, bf16[256,1024]{1,0:T(8,128)(2,1)S(1)}, u32[]{:S(2)}, u32[]{:S(2)}) collective-permute-start(bf16[256,1024]{1,0:T(8,128)(2,1)S(1)} %get-tuple-element.72), channel_id=1, source_target_pairs={{0,4},{4,0},{8,12},{12,8},{16,20},{20,16},{24,28},{28,24},{1,5},{5... | collective-permute-start | bytes 1572872 | tf_op jit(solution)/shard_map/ppermute | solution.py:29
  35.8 9.7 %collective-permute-start.13 = (bf16[128,1024]{1,0:T(8,128)(2,1)S(1)}, bf16[128,1024]{1,0:T(8,128)(2,1)S(1)}, u32[]{:S(2)}, u32[]{:S(2)}) collective-permute-start(bf16[128,1024]{1,0:T(8,128)(2,1)S(1)} %get-tuple-element.80), channel_id=1, source_target_pairs={{0,8},{4,12},{8,0},{12,4},{16,24},{20,28},{24,16},{28,20},{1,9},{5... | collective-permute-start | bytes 786440 | tf_op jit(solution)/shard_map/ppermute | solution.py:29
  36.4 9.9 %collective-permute-start.14 = (bf16[128,1024]{1,0:T(8,128)(2,1)S(1)}, bf16[128,1024]{1,0:T(8,128)(2,1)S(1)}, u32[]{:S(2)}, u32[]{:S(2)}) collective-permute-start(bf16[128,1024]{1,0:T(8,128)(2,1)S(1)} %get-tuple-element.81), channel_id=1, source_target_pairs={{0,20},{4,16},{8,28},{12,24},{16,4},{20,0},{24,12},{28,8},{1,21},{... | collective-permute-start | bytes 786440 | tf_op jit(solution)/shard_map/ppermute | solution.py:29
  36.7 1.7 %collective-permute-start.11 = (bf16[128,1024]{1,0:T(8,128)(2,1)S(1)}, bf16[128,1024]{1,0:T(8,128)(2,1)S(1)}, u32[]{:S(2)}, u32[]{:S(2)}) collective-permute-start(bf16[128,1024]{1,0:T(8,128)(2,1)S(1)} %get-tuple-element.73), channel_id=1, source_target_pairs={{0,4},{4,0},{8,12},{12,8},{16,20},{20,16},{24,28},{28,24},{1,5},{5... | collective-permute-start | bytes 786440 | tf_op jit(solution)/shard_map/ppermute | solution.py:29
  38.4 8.0 %collective-permute-start.12 = (bf16[256,1024]{1,0:T(8,128)(2,1)S(1)}, bf16[256,1024]{1,0:T(8,128)(2,1)S(1)}, u32[]{:S(2)}, u32[]{:S(2)}) collective-permute-start(bf16[256,1024]{1,0:T(8,128)(2,1)S(1)} %get-tuple-element.74), channel_id=1, source_target_pairs={{0,4},{4,0},{8,12},{12,8},{16,20},{20,16},{24,28},{28,24},{1,5},{5... | collective-permute-start | bytes 1572872 | tf_op jit(solution)/shard_map/ppermute | solution.py:29
  41.7 8.7 %collective-permute-start.18 = (bf16[128,1024]{1,0:T(8,128)(2,1)S(1)}, bf16[128,1024]{1,0:T(8,128)(2,1)S(1)}, u32[]{:S(2)}, u32[]{:S(2)}) collective-permute-start(bf16[128,1024]{1,0:T(8,128)(2,1)S(1)} %shard_map.107), channel_id=1, source_target_pairs={{0,12},{4,8},{8,4},{12,0},{16,28},{20,24},{24,20},{28,16},{1,13},{... | collective-permute-start | bytes 786440 | tf_op jit(solution)/shard_map/ppermute | solution.py:29
  41.8 10.1 %collective-permute-start.17 = (bf16[128,1024]{1,0:T(8,128)(2,1)S(1)}, bf16[128,1024]{1,0:T(8,128)(2,1)S(1)}, u32[]{:S(2)}, u32[]{:S(2)}) collective-permute-start(bf16[128,1024]{1,0:T(8,128)(2,1)S(1)} %shard_map.106), channel_id=1, source_target_pairs={{0,16},{4,20},{8,24},{12,28},{16,0},{20,4},{24,8},{28,12},{1,17},{... | collective-permute-start | bytes 786440 | tf_op jit(solution)/shard_map/ppermute | solution.py:29

commit v7 on v6

--- a/solution.py
+++ b/solution.py
@@ -354,21 +354,21 @@
     pieces = {0: mine}
     pieces[2] = pair(mine, 2)
     pieces[5] = pair(other, 5)
-    partner = pair(after(bundle, mine), 1)
+    partner = pair(bundle, 1)
     cp = from_next(half(after(grads, partner), 1 - core), 1)
-    co = from_next(half(after(grads, partner), core))
+    co = from_next(half(grads, core))
     pieces[3] = pair(after(other, partner), 3)
     pieces[4] = pair(after(mine, partner), 4)
     xt = call(
         functools.partial(turn_kernel, count),
-        1,
+        10,
         like((depth, two), BF),
         bundle,
         partner,
         scratch=[pltpu.VMEM((depth, two), BF)],
     )
-    pieces[6] = pair(pieces[2], 4)
-    pieces[7] = pair(pieces[5], 2)
+    pieces[6] = pair(after(pieces[2], xt), 4)
+    pieces[7] = pair(after(pieces[5], xt), 2)
     pieces[1] = partner[two:]
     bit = 8
     while bit < count:
@@ -378,11 +378,11 @@
     first = functools.partial(pre_kernel, blocks[:1], False)
     pre = call(first, 0.001, like((two, F), F32), bundle, partner, *held(blocks[:1]), scratch=[block])
     more = functools.partial(pre_kernel, blocks[1:-1], True)
-    pre = call(more, 0.001, like((two, F), F32), bundle, partner, after(pre, xt), *held(blocks[1:-1]), scratch=[block])
-    co, pre = lax.optimization_barrier((co, pre))
+    pre = call(more, 10, like((two, F), F32), bundle, partner, after(pre, xt), *held(blocks[1:-1]), scratch=[block])
+    co, cp, pre = lax.optimization_barrier((co, cp, pre))
     act, sigs, prob, prob_slope, mixed = call(
         functools.partial(forward_kernel, blocks[-1]),
-        0.001,
+        1,
         [
             like((two, F), BF),
             like((two, F), F32),
@@ -399,7 +399,7 @@
     )
     prod, stats = call(
         stats_kernel,
-        1, [like((two, HALF), F32), like((8, two), F32)], lengths, mixed, vgo, partner, co, cp
+        0.1, [like((two, HALF), F32), like((8, two), F32)], lengths, mixed, vgo, partner, co, cp
     )
     theirs = pair(stats, 1)
     slope = call(slope_kernel, 0.3, like((two, F), F32), act, after(sigs, stats))

time: 53.2 us -> 53.2 us (level)
    ppermute x17, starting transfers between devices: 15.1 us -> 13.8 us  [pair(): return lax.ppermute(x, 'dp', [(i, i ^ mask) for i in range(count)])]
    ppermute x2, waiting for transfers between devices: 0.01 us -> 1.01 us  [from_next(): lax.ppermute(x, ('dp', 'segment'), [(i * seg + s, (i ^ mask) * seg + (s -...]
    ppermute x2, starting transfers between devices: 6.33 us -> 7.15 us  [from_next(): lax.ppermute(x, ('dp', 'segment'), [(i * seg + s, (i ^ mask) * seg + (s -...]
    ppermute x17, waiting for transfers between devices: 16.6 us -> 16 us  [pair(): return lax.ppermute(x, 'dp', [(i, i ^ mask) for i in range(count)])]
  transfers between devices with their start and end apart: 19 -> 19, of which waited for: 10 -> 12; matrix products, arithmetic and copies ran while one was open for 0% -> 0% of each run, Pallas kernels for 16% -> 13%
where the time goes in v7:
time: 53.2 us; the launch traced here: 53 us
  starting transfers between devices  21 us (39%)
  waiting for transfers between devices  17 us (32%)
  Pallas kernels  12 us (23%)
  local copies, waits for them, and re-layouts  1.54 us (3%)
  between operations  1.54 us (3%)
    ppermute x17, waiting for transfers between devices, pair(): return lax.ppermute(x, 'dp', [(i, i ^ mask) for i in range(count)])  16 us
    ppermute x17, starting transfers between devices, pair(): return lax.ppermute(x, 'dp', [(i, i ^ mask) for i in range(count)])  13.8 us
    pallas_call x15, Pallas kernels, call(): pl.pallas_call(body, out_shape=out_shape, in_specs=[SMEM if x.dtype == jn...  10.9 us
    ppermute x2, starting transfers between devices, from_next(): lax.ppermute(x, ('dp', 'segment'), [(i * seg + s, (i ^ mask) * seg + (s -...  7.15 us
    slice x1, local copies, waits for them, and re-layouts, on_device(): shard[:, :F]  1.21 us
  transfers between devices with their start and end apart: 19, of which 12 were waited for; matrix products, arithmetic and copies ran while one was open for 0% of the time, Pallas kernels for 13%

profile of v7, /device:TPU:0, one launch (start us, length us, event | category | flops | bytes accessed | tf_op | source)
XLA Modules:
  0.0 53.0 jit_solution(3443860938685950744)
XLA Ops:
  0.7 1.2 %fusion = (bf16[128,1024]{1,0:T(8,128)(2,1)S(1)}, bf16[128,1024]{1,0:T(8,128)(2,1)S(1)}) fusion(bf16[128,2048]{1,0:T(8,128)(2,1)} %bitcast.16), kind=kLoop, calls=%fused_computation.8 | loop fusion | bytes 1048576 | tf_op jit(solution)/shard_map/slice | solution.py:350
  2.0 0.1 copy-done.2
  2.1 0.2 copy-done.3
  2.2 0.1 shard_map.93
  2.3 0.5 collective-permute-start
  2.9 2.6 %collective-permute-start.4 = (bf16[128,1024]{1,0:T(8,128)(2,1)S(1)}, bf16[128,1024]{1,0:T(8,128)(2,1)S(1)}, u32[]{:S(2)}, u32[]{:S(2)}) collective-permute-start(bf16[128,1024]{1,0:T(8,128)(2,1)S(1)} %pad_maximum_fusion.1.other), channel_id=1, source_target_pairs={{0,20},{4,16},{8,28},{12,24},{16,4},{20,0},{24,12},{28,8},{1,21},{... | collective-permute-start | bytes 786440 | tf_op jit(solution)/shard_map/ppermute | solution.py:29
  5.5 1.6 %collective-permute-start.1 = (bf16[128,1024]{1,0:T(8,128)(2,1)S(1)}, bf16[128,1024]{1,0:T(8,128)(2,1)S(1)}, u32[]{:S(2)}, u32[]{:S(2)}) collective-permute-start(bf16[128,1024]{1,0:T(8,128)(2,1)S(1)} %pad_maximum_fusion.refs_0_.mine), channel_id=1, source_target_pairs={{0,8},{4,12},{8,0},{12,4},{16,24},{20,28},{24,16},{28,20},{1,9},{5... | collective-permute-start | bytes 786440 | tf_op jit(solution)/shard_map/ppermute | solution.py:29
  7.1 3.7 %collective-permute-start.7 = (bf16[256,512]{1,0:T(8,128)(2,1)S(1)}, bf16[256,512]{1,0:T(8,128)(2,1)S(1)}, u32[]{:S(2)}, u32[]{:S(2)}) collective-permute-start(bf16[256,512]{1,0:T(8,128)(2,1)S(1)} %dynamic-slice_bitcast_fusion), channel_id=1, source_target_pairs={{0,3},{1,0},{2,1},{3,2},{4,7},{5,4},{6,5},{7,6},{8,11},{9,8},{10,9... | collective-permute-start | bytes 786440 | tf_op jit(solution)/shard_map/ppermute | solution.py:34
  11.4 0.6 %collective-permute-start.3 = (bf16[128,1024]{1,0:T(8,128)(2,1)S(1)}, bf16[128,1024]{1,0:T(8,128)(2,1)S(1)}, u32[]{:S(2)}, u32[]{:S(2)}) collective-permute-start(bf16[128,1024]{1,0:T(8,128)(2,1)S(1)} %pad_maximum_fusion.refs_0_.mine), channel_id=1, source_target_pairs={{0,16},{4,20},{8,24},{12,28},{16,0},{20,4},{24,8},{28,12},{1,17},{... | collective-permute-start | bytes 786440 | tf_op jit(solution)/shard_map/ppermute | solution.py:29
  12.0 0.4 shard_map.94.xt
  12.4 0.5 shard_map.95.refs_0_
  12.9 3.5 %collective-permute-start.8 = (bf16[256,512]{1,0:T(8,128)(2,1)S(1)}, bf16[256,512]{1,0:T(8,128)(2,1)S(1)}, u32[]{:S(2)}, u32[]{:S(2)}) collective-permute-start(bf16[256,512]{1,0:T(8,128)(2,1)S(1)} %constant_dynamic-slice_fusion), channel_id=1, source_target_pairs={{0,7},{1,4},{2,5},{3,6},{4,3},{5,0},{6,1},{7,2},{8,15},{9,12},{10,... | collective-permute-start | bytes 786440 | tf_op jit(solution)/shard_map/ppermute | solution.py:34
  16.4 1.5 %collective-permute-start.6 = (bf16[128,1024]{1,0:T(8,128)(2,1)S(1)}, bf16[128,1024]{1,0:T(8,128)(2,1)S(1)}, u32[]{:S(2)}, u32[]{:S(2)}) collective-permute-start(bf16[128,1024]{1,0:T(8,128)(2,1)S(1)} %collective-permute-done.4.refs_4_.refs_3_), channel_id=1, source_target_pairs={{0,8},{4,12},{8,0},{12,4},{16,24},{20,28},{24,16},{28,20},{1,9},{5... | collective-permute-start | bytes 786440 | tf_op jit(solution)/shard_map/ppermute | solution.py:29
  17.9 1.3 %collective-permute-done.3.refs_3_.refs_2_ = bf16[128,1024]{1,0:T(8,128)(2,1)S(1)} collective-permute-done((bf16[128,1024]{1,0:T(8,128)(2,1)S(1)}, bf16[128,1024]{1,0:T(8,128)(2,1)S(1)}, u32[]{:S(2)}, u32[]{:S(2)}) %collective-permute-start.3) | collective-permute-done | bytes 262176 | tf_op jit(solution)/shard_map/ppermute | solution.py:29
  19.2 0.5 collective-permute-start.5
  19.7 0.3 collective-permute-done.2.refs_2_.refs_1_
  20.0 0.9 %shard_map.96.prev = f32[512,1024]{1,0:T(8,128)S(1)} custom-call(bf16[640,1024]{1,0:T(8,128)(2,1)S(1)} %get-tuple-element.52.bo, bf16[640,1024]{1,0:T(8,128)(2,1)S(1)} %collective-permute-done.bp, f32[512,1024]{1,0:T(8,128)S(1)} %shard_map.95.refs_0_, bf16[128,1024]{1,0:T(8,128)(2,1)S(1)} %collective-permute-done.1.refs_1_.refs_0_, ...), custom_call_target="tpu_custom_call" | custom-call | flops 10000000000 | bytes 10000000000 | tf_op jit(solution)/shard_map/pallas_call | solution.py:42
  20.9 1.0 %collective-permute-done.8.cp = bf16[256,512]{1,0:T(8,128)(2,1)S(1)} collective-permute-done((bf16[256,512]{1,0:T(8,128)(2,1)S(1)}, bf16[256,512]{1,0:T(8,128)(2,1)S(1)}, u32[]{:S(2)}, u32[]{:S(2)}) %collective-permute-start.8) | collective-permute-done | bytes 262176 | tf_op jit(solution)/shard_map/ppermute | solution.py:34
  21.9 3.7 %collective-permute-done.6.refs_1_.refs_5_ = bf16[128,1024]{1,0:T(8,128)(2,1)S(1)} collective-permute-done((bf16[128,1024]{1,0:T(8,128)(2,1)S(1)}, bf16[128,1024]{1,0:T(8,128)(2,1)S(1)}, u32[]{:S(2)}, u32[]{:S(2)}) %collective-permute-start.6) | collective-permute-done | bytes 262176 | tf_op jit(solution)/shard_map/ppermute | solution.py:29
  25.6 0.4 collective-permute-done.5.refs_0_.refs_4_
  26.0 1.8 %shard_map.97 = (bf16[512,1024]{1,0:T(8,128)(2,1)S(1)}, f32[512,1024]{1,0:T(8,128)S(1)}, bf16[8,256,256]{2,1,0:T(8,128)(2,1)S(1)}, bf16[8,256,256]{2,1,0:T(8,128)(2,1)S(1)}, f32[512,512]{1,0:T(8,128)S(1)}) custom-call(bf16[640,1024]{1,0:T(8,128)(2,1)S(1)} %get-tuple-element.52.bo, bf16[640,1024]{1,0:T(8,128)(2,1)S(1)} %collective-permute-done.bp, ...), custom_call_target="tpu_custom_call" | custom-call | flops 1000000000 | bytes 1000000000 | tf_op jit(solution)/shard_map/pallas_call | solution.py:42
  27.8 0.6 %shard_map.98 = (f32[512,512]{1,0:T(8,128)S(1)}, f32[8,512]{1,0:T(8,128)S(1)}) custom-call(s32[1,1]{1,0:T(1,128)S(6)} %copy.10.length, f32[512,512]{1,0:T(8,128)S(1)} %get-tuple-element.63.mixed, bf16[256,1024]{1,0:T(8,128)(2,1)S(1)} %get-tuple-element.60.vgo, bf16[640,1024]{1,0:T(8,128)(2,1)S(1)} %collective-permute-done.bp, ...), custom_call_target="tpu_custom_call" | custom-call | flops 100000000 | bytes 100000000 | tf_op jit(solution)/shard_map/pallas_call | solution.py:42
  28.5 0.3 shard_map.99.slope
  28.7 0.9 %collective-permute-done.9.theirs = f32[8,512]{1,0:T(8,128)S(1)} collective-permute-done((f32[8,512]{1,0:T(8,128)S(1)}, f32[8,512]{1,0:T(8,128)S(1)}, u32[]{:S(2)}, u32[]{:S(2)}) %collective-permute-start.9) | collective-permute-done | bytes 16416 | tf_op jit(solution)/shard_map/ppermute | solution.py:29
  29.6 1.8 %shard_map.100 = (bf16[512,1024]{1,0:T(8,128)(2,1)S(1)}, bf16[512,512]{1,0:T(8,128)(2,1)S(1)}, bf16[128,1024]{1,0:T(8,128)(2,1)S(1)}, bf16[128,1024]{1,0:T(8,128)(2,1)S(1)}) custom-call(bf16[1024,512]{1,0:T(8,128)(2,1)S(1)} %shard_map.94.xt, bf16[512,1024]{1,0:T(8,128)(2,1)S(1)} %get-tuple-element.61.act, f32[512,1024]{1,0:T(8,128)S(1)} %shard_map.99.slope, ...), custom_call_target="tpu_custom_call" | custom-call | flops 100000000 | bytes 100000000 | tf_op jit(solution)/shard_map/pallas_call | solution.py:42
  31.4 1.2 %collective-permute-start.15 = (bf16[128,1024]{1,0:T(8,128)(2,1)S(1)}, bf16[128,1024]{1,0:T(8,128)(2,1)S(1)}, u32[]{:S(2)}, u32[]{:S(2)}) collective-permute-start(bf16[128,1024]{1,0:T(8,128)(2,1)S(1)} %get-tuple-element.90), channel_id=1, source_target_pairs={{0,8},{4,12},{8,0},{12,4},{16,24},{20,28},{24,16},{28,20},{1,9},{5... | collective-permute-start | bytes 786440 | tf_op jit(solution)/shard_map/ppermute | solution.py:29
  32.7 1.7 %collective-permute-start.16 = (bf16[128,1024]{1,0:T(8,128)(2,1)S(1)}, bf16[128,1024]{1,0:T(8,128)(2,1)S(1)}, u32[]{:S(2)}, u32[]{:S(2)}) collective-permute-start(bf16[128,1024]{1,0:T(8,128)(2,1)S(1)} %get-tuple-element.91), channel_id=1, source_target_pairs={{0,16},{4,20},{8,24},{12,28},{16,0},{20,4},{24,8},{28,12},{1,17},{... | collective-permute-start | bytes 786440 | tf_op jit(solution)/shard_map/ppermute | solution.py:29
  34.4 0.7 %shard_map.103 = (bf16[256,1024]{1,0:T(8,128)(2,1)S(1)}, bf16[256,1024]{1,0:T(8,128)(2,1)S(1)}) custom-call(bf16[8,256,256]{2,1,0:T(8,128)(2,1)S(1)} %get-tuple-element.74.prob, bf16[512,512]{1,0:T(8,128)(2,1)S(1)} %get-tuple-element.75.dmixed, f32[512,512]{1,0:T(8,128)S(1)} %get-tuple-element.63.mixed, f32[8,512]{1,0:T(8,128)S(1)} %get-tuple-element.66.mine, ...), custom_call_target="tpu_custom_call" | custom-call | flops 3000000000 | bytes 3000000000 | tf_op jit(solution)/shard_map/pallas_call | solution.py:42
  35.1 0.1 collective-permute-start.10
  35.2 1.0 %shard_map.102 = (bf16[128,1024]{1,0:T(8,128)(2,1)S(1)}, bf16[128,1024]{1,0:T(8,128)(2,1)S(1)}, bf16[128,1024]{1,0:T(8,128)(2,1)S(1)}, bf16[128,1024]{1,0:T(8,12...) custom-call(bf16[1024,512]{1,0:T(8,128)(2,1)S(1)} %shard_map.94.xt, ...), custom_call_target="tpu_custom_call" | custom-call | flops 10000000000 | bytes 10000000000 | tf_op jit(solution)/shard_map/pallas_call | solution.py:42
  36.2 0.3 collective-permute-start.13
  36.5 0.7 %collective-permute-start.14 = (bf16[128,1024]{1,0:T(8,128)(2,1)S(1)}, bf16[128,1024]{1,0:T(8,128)(2,1)S(1)}, u32[]{:S(2)}, u32[]{:S(2)}) collective-permute-start(bf16[128,1024]{1,0:T(8,128)(2,1)S(1)} %get-tuple-element.85), channel_id=1, source_target_pairs={{0,20},{4,16},{8,28},{12,24},{16,4},{20,0},{24,12},{28,8},{1,21},{... | collective-permute-start | bytes 786440 | tf_op jit(solution)/shard_map/ppermute | solution.py:29
  37.2 0.3 collective-permute-start.11
  37.5 1.4 %shard_map.101 = (f32[256,1024]{1,0:T(8,128)S(1)}, bf16[256,1024]{1,0:T(8,128)(2,1)S(1)}) custom-call(bf16[128,1024]{1,0:T(8,128)(2,1)S(1)} %pad_maximum_fusion.refs_0_.mine, bf16[640,1024]{1,0:T(8,128)(2,1)S(1)} %collective-permute-done.bp, bf16[128,1024]{1,0:T(8,128)(2,1)S(1)} %collective-permute-done.1.refs_1_.refs_0_, ...), custom_call_target="tpu_custom_call" | custom-call | flops 10000000000 | bytes 10000000000 | tf_op jit(solution)/shard_map/pallas_call | solution.py:42
  39.0 0.3 collective-permute-start.12
  39.2 1.1 %collective-permute-done.15.added = bf16[128,1024]{1,0:T(8,128)(2,1)S(1)} collective-permute-done((bf16[128,1024]{1,0:T(8,128)(2,1)S(1)}, bf16[128,1024]{1,0:T(8,128)(2,1)S(1)}, u32[]{:S(2)}, u32[]{:S(2)}) %collective-permute-start.15) | collective-permute-done | bytes 262176 | tf_op jit(solution)/shard_map/ppermute | solution.py:29
  40.3 1.5 %collective-permute-done.16.added = bf16[128,1024]{1,0:T(8,128)(2,1)S(1)} collective-permute-done((bf16[128,1024]{1,0:T(8,128)(2,1)S(1)}, bf16[128,1024]{1,0:T(8,128)(2,1)S(1)}, u32[]{:S(2)}, u32[]{:S(2)}) %collective-permute-start.16) | collective-permute-done | bytes 262176 | tf_op jit(solution)/shard_map/ppermute | solution.py:29
  41.9 0.1 shard_map.107
  41.9 0.1 collective-permute-start.18
  42.0 0.1 shard_map.106
  42.1 1.8 %collective-permute-start.17 = (bf16[128,1024]{1,0:T(8,128)(2,1)S(1)}, bf16[128,1024]{1,0:T(8,128)(2,1)S(1)}, u32[]{:S(2)}, u32[]{:S(2)}) collective-permute-start(bf16[128,1024]{1,0:T(8,128)(2,1)S(1)} %shard_map.106), channel_id=1, source_target_pairs={{0,16},{4,20},{8,24},{12,28},{16,0},{20,4},{24,8},{28,12},{1,17},{... | collective-permute-start | bytes 786440 | tf_op jit(solution)/shard_map/ppermute | solution.py:29
  43.9 2.1 %collective-permute-done.13.x = bf16[128,1024]{1,0:T(8,128)(2,1)S(1)} collective-permute-done((bf16[128,1024]{1,0:T(8,128)(2,1)S(1)}, bf16[128,1024]{1,0:T(8,128)(2,1)S(1)}, u32[]{:S(2)}, u32[]{:S(2)}) %collective-permute-start.13) | collective-permute-done | bytes 262176 | tf_op jit(solution)/shard_map/ppermute | solution.py:29
  45.9 0.8 %collective-permute-done.14.y = bf16[128,1024]{1,0:T(8,128)(2,1)S(1)} collective-permute-done((bf16[128,1024]{1,0:T(8,128)(2,1)S(1)}, bf16[128,1024]{1,0:T(8,128)(2,1)S(1)}, u32[]{:S(2)}, u32[]{:S(2)}) %collective-permute-start.14) | collective-permute-done | bytes 262176 | tf_op jit(solution)/shard_map/ppermute | solution.py:29
  46.7 0.1 shard_map.105
  46.9 1.3 %shard_map.104 = (bf16[256,1024]{1,0:T(8,128)(2,1)}, bf16[256,1024]{1,0:T(8,128)(2,1)}, bf16[256,1024]{1,0:T(8,128)(2,1)}) custom-call(f32[256,1024]{1,0:T(8,128)S(1)} %get-tuple-element.71.gi_o, bf16[256,1024]{1,0:T(8,128)(2,1)S(1)} %collective-permute-done.12.gi_r, bf16[256,1024]{1,0:T(8,128)(2,1)S(1)} %get-tuple-element.79.own, ...), custom_call_target="tpu_custom_call" | custom-call | flops 300000000 | bytes 300000000 | tf_op jit(solution)/shard_map/pallas_call | solution.py:42
  48.1 2.5 %collective-permute-done.18.y = bf16[128,1024]{1,0:T(8,128)(2,1)S(1)} collective-permute-done((bf16[128,1024]{1,0:T(8,128)(2,1)S(1)}, bf16[128,1024]{1,0:T(8,128)(2,1)S(1)}, u32[]{:S(2)}, u32[]{:S(2)}) %collective-permute-start.18) | collective-permute-done | bytes 262176 | tf_op jit(solution)/shard_map/ppermute | solution.py:29
  50.7 1.3 %collective-permute-done.17.x = bf16[128,1024]{1,0:T(8,128)(2,1)S(1)} collective-permute-done((bf16[128,1024]{1,0:T(8,128)(2,1)S(1)}, bf16[128,1024]{1,0:T(8,128)(2,1)S(1)}, u32[]{:S(2)}, u32[]{:S(2)}) %collective-permute-start.17) | collective-permute-done | bytes 262176 | tf_op jit(solution)/shard_map/ppermute | solution.py:29
  52.0 1.0 %shard_map.108 = f32[128,2048]{1,0:T(8,128)} custom-call(f32[128,1024]{1,0:T(8,128)S(1)} %get-tuple-element.96.own, bf16[128,1024]{1,0:T(8,128)(2,1)S(1)} %collective-permute-done.17.x, f32[128,1024]{1,0:T(8,128)S(1)} %get-tuple-element.98.far, bf16[128,1024]{1,0:T(8,128)(2,1)S(1)} %collective-permute-done.18.y), custom_call_target="tpu_custom_call" | custom-call | tf_op jit(solution)/shard_map/pallas_call | solution.py:453
  (20 shorter events, 0.2 us)
Async XLA Ops:
  0.6 6.5 %copy-start = (bf16[1,1,256,1024]{3,2,1,0:T(8,128)(2,1)S(1)}, bf16[1,1,256,1024]{3,2,1,0:T(8,128)(2,1)}, u32[]{:S(2)}) copy-start(bf16[1,1,256,1024]{3,2,1,0:T(8,128)(2,1)} %param.9) | copy-start | bytes 1572868
  0.6 1.3 %copy-start.1 = (bf16[1,1,256,1024]{3,2,1,0:T(8,128)(2,1)S(1)}, bf16[1,1,256,1024]{3,2,1,0:T(8,128)(2,1)}, u32[]{:S(2)}) copy-start(bf16[1,1,256,1024]{3,2,1,0:T(8,128)(2,1)} %param.6) | copy-start | bytes 1572868
  0.7 1.4 %copy-start.2 = (bf16[1,1,256,1024]{3,2,1,0:T(8,128)(2,1)S(1)}, bf16[1,1,256,1024]{3,2,1,0:T(8,128)(2,1)}, u32[]{:S(2)}) copy-start(bf16[1,1,256,1024]{3,2,1,0:T(8,128)(2,1)} %param.7) | copy-start | bytes 1572868
  0.7 1.6 %copy-start.3 = (bf16[1,1,256,1024]{3,2,1,0:T(8,128)(2,1)S(1)}, bf16[1,1,256,1024]{3,2,1,0:T(8,128)(2,1)}, u32[]{:S(2)}) copy-start(bf16[1,1,256,1024]{3,2,1,0:T(8,128)(2,1)} %param.8) | copy-start | bytes 1572868
  2.3 9.1 %collective-permute-start = (bf16[640,1024]{1,0:T(8,128)(2,1)S(1)}, bf16[640,1024]{1,0:T(8,128)(2,1)S(1)}, u32[]{:S(2)}, u32[]{:S(2)}) collective-permute-start(bf16[640,1024]{1,0:T(8,128)(2,1)S(1)} %get-tuple-element.52.bo), channel_id=1, source_target_pairs={{0,4},{4,0},{8,12},{12,8},{16,20},{20,16},{24,28},{28,24},{1,5},{5... | collective-permute-start | bytes 3932168 | tf_op jit(solution)/shard_map/ppermute | solution.py:29
  2.9 10.1 %collective-permute-start.4 = (bf16[128,1024]{1,0:T(8,128)(2,1)S(1)}, bf16[128,1024]{1,0:T(8,128)(2,1)S(1)}, u32[]{:S(2)}, u32[]{:S(2)}) collective-permute-start(bf16[128,1024]{1,0:T(8,128)(2,1)S(1)} %pad_maximum_fusion.1.other), channel_id=1, source_target_pairs={{0,20},{4,16},{8,28},{12,24},{16,4},{20,0},{24,12},{28,8},{1,21},{... | collective-permute-start | bytes 786440 | tf_op jit(solution)/shard_map/ppermute | solution.py:29
  5.5 10.9 %collective-permute-start.1 = (bf16[128,1024]{1,0:T(8,128)(2,1)S(1)}, bf16[128,1024]{1,0:T(8,128)(2,1)S(1)}, u32[]{:S(2)}, u32[]{:S(2)}) collective-permute-start(bf16[128,1024]{1,0:T(8,128)(2,1)S(1)} %pad_maximum_fusion.refs_0_.mine), channel_id=1, source_target_pairs={{0,8},{4,12},{8,0},{12,4},{16,24},{20,28},{24,16},{28,20},{1,9},{5... | collective-permute-start | bytes 786440 | tf_op jit(solution)/shard_map/ppermute | solution.py:29
  7.1 13.8 %collective-permute-start.7 = (bf16[256,512]{1,0:T(8,128)(2,1)S(1)}, bf16[256,512]{1,0:T(8,128)(2,1)S(1)}, u32[]{:S(2)}, u32[]{:S(2)}) collective-permute-start(bf16[256,512]{1,0:T(8,128)(2,1)S(1)} %dynamic-slice_bitcast_fusion), channel_id=1, source_target_pairs={{0,3},{1,0},{2,1},{3,2},{4,7},{5,4},{6,5},{7,6},{8,11},{9,8},{10,9... | collective-permute-start | bytes 786440 | tf_op jit(solution)/shard_map/ppermute | solution.py:34
  11.4 7.8 %collective-permute-start.3 = (bf16[128,1024]{1,0:T(8,128)(2,1)S(1)}, bf16[128,1024]{1,0:T(8,128)(2,1)S(1)}, u32[]{:S(2)}, u32[]{:S(2)}) collective-permute-start(bf16[128,1024]{1,0:T(8,128)(2,1)S(1)} %pad_maximum_fusion.refs_0_.mine), channel_id=1, source_target_pairs={{0,16},{4,20},{8,24},{12,28},{16,0},{20,4},{24,8},{28,12},{1,17},{... | collective-permute-start | bytes 786440 | tf_op jit(solution)/shard_map/ppermute | solution.py:29
  12.0 8.0 %collective-permute-start.2 = (bf16[128,1024]{1,0:T(8,128)(2,1)S(1)}, bf16[128,1024]{1,0:T(8,128)(2,1)S(1)}, u32[]{:S(2)}, u32[]{:S(2)}) collective-permute-start(bf16[128,1024]{1,0:T(8,128)(2,1)S(1)} %pad_maximum_fusion.1.other), channel_id=1, source_target_pairs={{0,12},{4,8},{8,4},{12,0},{16,28},{20,24},{24,20},{28,16},{1,13},{... | collective-permute-start | bytes 786440 | tf_op jit(solution)/shard_map/ppermute | solution.py:29
  12.9 9.0 %collective-permute-start.8 = (bf16[256,512]{1,0:T(8,128)(2,1)S(1)}, bf16[256,512]{1,0:T(8,128)(2,1)S(1)}, u32[]{:S(2)}, u32[]{:S(2)}) collective-permute-start(bf16[256,512]{1,0:T(8,128)(2,1)S(1)} %constant_dynamic-slice_fusion), channel_id=1, source_target_pairs={{0,7},{1,4},{2,5},{3,6},{4,3},{5,0},{6,1},{7,2},{8,15},{9,12},{10,... | collective-permute-start | bytes 786440 | tf_op jit(solution)/shard_map/ppermute | solution.py:34
  16.4 9.2 %collective-permute-start.6 = (bf16[128,1024]{1,0:T(8,128)(2,1)S(1)}, bf16[128,1024]{1,0:T(8,128)(2,1)S(1)}, u32[]{:S(2)}, u32[]{:S(2)}) collective-permute-start(bf16[128,1024]{1,0:T(8,128)(2,1)S(1)} %collective-permute-done.4.refs_4_.refs_3_), channel_id=1, source_target_pairs={{0,8},{4,12},{8,0},{12,4},{16,24},{20,28},{24,16},{28,20},{1,9},{5... | collective-permute-start | bytes 786440 | tf_op jit(solution)/shard_map/ppermute | solution.py:29
  19.2 6.8 %collective-permute-start.5 = (bf16[128,1024]{1,0:T(8,128)(2,1)S(1)}, bf16[128,1024]{1,0:T(8,128)(2,1)S(1)}, u32[]{:S(2)}, u32[]{:S(2)}) collective-permute-start(bf16[128,1024]{1,0:T(8,128)(2,1)S(1)} %collective-permute-done.1.refs_1_.refs_0_), channel_id=1, source_target_pairs={{0,16},{4,20},{8,24},{12,28},{16,0},{20,4},{24,8},{28,12},{1,17},{... | collective-permute-start | bytes 786440 | tf_op jit(solution)/shard_map/ppermute | solution.py:29
  28.4 1.2 %collective-permute-start.9 = (f32[8,512]{1,0:T(8,128)S(1)}, f32[8,512]{1,0:T(8,128)S(1)}, u32[]{:S(2)}, u32[]{:S(2)}) collective-permute-start(f32[8,512]{1,0:T(8,128)S(1)} %get-tuple-element.66.mine), channel_id=1, source_target_pairs={{0,4},{4,0},{8,12},{12,8},{16,20},{20,16},{24,28},{28,24},{1,5},{5... | collective-permute-start | bytes 49160 | tf_op jit(solution)/shard_map/ppermute | solution.py:29
  31.4 8.9 %collective-permute-start.15 = (bf16[128,1024]{1,0:T(8,128)(2,1)S(1)}, bf16[128,1024]{1,0:T(8,128)(2,1)S(1)}, u32[]{:S(2)}, u32[]{:S(2)}) collective-permute-start(bf16[128,1024]{1,0:T(8,128)(2,1)S(1)} %get-tuple-element.90), channel_id=1, source_target_pairs={{0,8},{4,12},{8,0},{12,4},{16,24},{20,28},{24,16},{28,20},{1,9},{5... | collective-permute-start | bytes 786440 | tf_op jit(solution)/shard_map/ppermute | solution.py:29
  32.7 9.2 %collective-permute-start.16 = (bf16[128,1024]{1,0:T(8,128)(2,1)S(1)}, bf16[128,1024]{1,0:T(8,128)(2,1)S(1)}, u32[]{:S(2)}, u32[]{:S(2)}) collective-permute-start(bf16[128,1024]{1,0:T(8,128)(2,1)S(1)} %get-tuple-element.91), channel_id=1, source_target_pairs={{0,16},{4,20},{8,24},{12,28},{16,0},{20,4},{24,8},{28,12},{1,17},{... | collective-permute-start | bytes 786440 | tf_op jit(solution)/shard_map/ppermute | solution.py:29
  35.1 2.1 %collective-permute-start.10 = (bf16[256,1024]{1,0:T(8,128)(2,1)S(1)}, bf16[256,1024]{1,0:T(8,128)(2,1)S(1)}, u32[]{:S(2)}, u32[]{:S(2)}) collective-permute-start(bf16[256,1024]{1,0:T(8,128)(2,1)S(1)} %get-tuple-element.76), channel_id=1, source_target_pairs={{0,4},{4,0},{8,12},{12,8},{16,20},{20,16},{24,28},{28,24},{1,5},{5... | collective-permute-start | bytes 1572872 | tf_op jit(solution)/shard_map/ppermute | solution.py:29
  36.2 9.7 %collective-permute-start.13 = (bf16[128,1024]{1,0:T(8,128)(2,1)S(1)}, bf16[128,1024]{1,0:T(8,128)(2,1)S(1)}, u32[]{:S(2)}, u32[]{:S(2)}) collective-permute-start(bf16[128,1024]{1,0:T(8,128)(2,1)S(1)} %get-tuple-element.84), channel_id=1, source_target_pairs={{0,8},{4,12},{8,0},{12,4},{16,24},{20,28},{24,16},{28,20},{1,9},{5... | collective-permute-start | bytes 786440 | tf_op jit(solution)/shard_map/ppermute | solution.py:29
  36.5 10.2 %collective-permute-start.14 = (bf16[128,1024]{1,0:T(8,128)(2,1)S(1)}, bf16[128,1024]{1,0:T(8,128)(2,1)S(1)}, u32[]{:S(2)}, u32[]{:S(2)}) collective-permute-start(bf16[128,1024]{1,0:T(8,128)(2,1)S(1)} %get-tuple-element.85), channel_id=1, source_target_pairs={{0,20},{4,16},{8,28},{12,24},{16,4},{20,0},{24,12},{28,8},{1,21},{... | collective-permute-start | bytes 786440 | tf_op jit(solution)/shard_map/ppermute | solution.py:29
  37.2 1.7 %collective-permute-start.11 = (bf16[128,1024]{1,0:T(8,128)(2,1)S(1)}, bf16[128,1024]{1,0:T(8,128)(2,1)S(1)}, u32[]{:S(2)}, u32[]{:S(2)}) collective-permute-start(bf16[128,1024]{1,0:T(8,128)(2,1)S(1)} %get-tuple-element.77), channel_id=1, source_target_pairs={{0,4},{4,0},{8,12},{12,8},{16,20},{20,16},{24,28},{28,24},{1,5},{5... | collective-permute-start | bytes 786440 | tf_op jit(solution)/shard_map/ppermute | solution.py:29
  39.0 7.9 %collective-permute-start.12 = (bf16[256,1024]{1,0:T(8,128)(2,1)S(1)}, bf16[256,1024]{1,0:T(8,128)(2,1)S(1)}, u32[]{:S(2)}, u32[]{:S(2)}) collective-permute-start(bf16[256,1024]{1,0:T(8,128)(2,1)S(1)} %get-tuple-element.78), channel_id=1, source_target_pairs={{0,4},{4,0},{8,12},{12,8},{16,20},{20,16},{24,28},{28,24},{1,5},{5... | collective-permute-start | bytes 1572872 | tf_op jit(solution)/shard_map/ppermute | solution.py:29
  41.9 8.7 %collective-permute-start.18 = (bf16[128,1024]{1,0:T(8,128)(2,1)S(1)}, bf16[128,1024]{1,0:T(8,128)(2,1)S(1)}, u32[]{:S(2)}, u32[]{:S(2)}) collective-permute-start(bf16[128,1024]{1,0:T(8,128)(2,1)S(1)} %shard_map.107), channel_id=1, source_target_pairs={{0,12},{4,8},{8,4},{12,0},{16,28},{20,24},{24,20},{28,16},{1,13},{... | collective-permute-start | bytes 786440 | tf_op jit(solution)/shard_map/ppermute | solution.py:29
  42.1 9.9 %collective-permute-start.17 = (bf16[128,1024]{1,0:T(8,128)(2,1)S(1)}, bf16[128,1024]{1,0:T(8,128)(2,1)S(1)}, u32[]{:S(2)}, u32[]{:S(2)}) collective-permute-start(bf16[128,1024]{1,0:T(8,128)(2,1)S(1)} %shard_map.106), channel_id=1, source_target_pairs={{0,16},{4,20},{8,24},{12,28},{16,0},{20,4},{24,8},{28,12},{1,17},{... | collective-permute-start | bytes 786440 | tf_op jit(solution)/shard_map/ppermute | solution.py:29
